TPU v7x, 128 devices: a whole 4x4x4 slice. The times are simulated.
128 devices in a mesh: blk: 32 (over x, z, y_hi), xor: 4 (over y_lo, core).
Axes of the slice: x: 4, y: 4 (y_hi: 2, y_lo: 2; y = y_hi * 2 + y_lo), z: 4, core: 2. Of those that a mesh axis runs over, the one named last changes fastest.
Arguments:
- users: float32 [131072, 256], P(('blk', 'xor')), may hold values from -1.5 to 1.5
- user_accum: float32 [131072, 256], P(('blk', 'xor')), may hold values from 0.05 to 1
- items: float32 [65536, 256], P(('blk', 'xor')), may hold values from -1.5 to 1.5
- item_accum: float32 [65536, 256], P(('blk', 'xor')), may hold values from 0.05 to 1
- seen_user: int32 [6, 2048], P(None, ('blk', 'xor')), may hold values from 0 to 7
- seen_item: int32 [6, 2048], P(None, ('blk', 'xor')), may hold values from 0 to 3
- row_live: int32 [6, 2048, 128], P(None, ('blk', 'xor')), may hold values 0 or 1
- col_live: int32 [6, 2048, 128], P(None, ('blk', 'xor')), may hold values 0 or 1
- neg_user: int32 [6, 1024], P(None, ('blk', 'xor')), may hold values from 0 to 7
- neg_item: int32 [6, 1024], P(None, ('blk', 'xor')), may hold values from 0 to 3
Outputs:
- users_out: float32 [131072, 256], P(('blk', 'xor'))
- user_accum_out: float32 [131072, 256], P(('blk', 'xor'))
- items_out: float32 [65536, 256], P(('blk', 'xor'))
- item_accum_out: float32 [65536, 256], P(('blk', 'xor'))
All inputs are finite; a program needn't handle non-finite values. No bound on the sum of `row_live` or of `col_live` on one device may be relied on, other than what follows from the above.
Results may differ from a plain program's by a relative error of at most 0.0051.
Values sent between devices are 32-bit elements; how exact they have to be, the bound alone decides.
No kernel may reach another device: no remote copies, remote signals or barrier semaphores. Data moves between devices by JAX's collectives and lax.ppermute only.
A program may use at most 64 MiB of HBM per device.

v0:
```python
import functools

import jax
import jax.numpy as jnp
from jax import lax
from jax.experimental import pallas as pl
from jax.experimental.pallas import tpu as pltpu
from jax.sharding import PartitionSpec as P

SUBS = 6
TILE = 128
HALF = 256
LEARN_RATE = 0.05
DECAY = 0.02
NEG_WEIGHT = 0.25
AXES = ("blk", "xor")
BF = jnp.bfloat16
F32 = jnp.float32


def rows_of(scalars, sub_round, count):
    row = lax.broadcasted_iota(jnp.int32, (count, TILE), 0)
    out = jnp.zeros((count, TILE), jnp.int32)
    for t in range(count):
        out = jnp.where(row == t, scalars[sub_round, t], out)
    return out


def spread(tile, live, first, count):
    return jnp.concatenate([jnp.where(tile == first + n, live, 0.0) for n in range(count)], axis=1)


def pair_factors(sub_round, half, su, si, nu, ni, row_live, col_live, user_tiles):
    obs, neg = su.shape[1], nu.shape[1]
    rows = row_live[sub_round].astype(F32)
    cols = col_live[sub_round].astype(F32)
    ones = jnp.ones((neg, TILE), F32)
    left = jnp.concatenate(
        [
            spread(rows_of(su, sub_round, obs), rows, 0, user_tiles),
            spread(rows_of(nu, sub_round, neg), ones, 0, user_tiles),
        ],
        axis=0,
    ).astype(BF)
    first = half * (HALF // TILE)
    seen = spread(rows_of(si, sub_round, obs), cols, first, HALF // TILE)
    sampled = spread(rows_of(ni, sub_round, neg), ones, first, HALF // TILE)
    right = jnp.concatenate(
        [
            jnp.concatenate([seen, seen], axis=1),
            jnp.concatenate([NEG_WEIGHT * sampled, jnp.zeros_like(sampled)], axis=1),
        ],
        axis=0,
    ).astype(BF)
    return left, right


def adagrad(factor, accum, grad):
    accum = accum + grad * grad
    return factor - LEARN_RATE * grad * lax.rsqrt(accum), accum


def dot(a, b, contract):
    return lax.dot_general(a, b, ((contract[:1], contract[1:]), ((), ())), preferred_element_type=F32)


STEP = 256


def half_kernel(sub_round, half, from_whole, last, *refs):
    refs = list(refs)
    su, si, nu, ni, row_live, col_live, users = refs[:7]
    del refs[:7]
    if from_whole:
        factor_ref, accum_ref = refs[:2]
        del refs[:2]
        factor = factor_ref[half * HALF : (half + 1) * HALF, :]
        accum = accum_ref[half * HALF : (half + 1) * HALF, :]
    else:
        state = refs.pop(0)
        factor = state[:HALF, :]
        accum = state[HALF:, :]
    if half == 1:
        user_accum, grad_in = refs[:2]
        del refs[:2]
        if last:
            other = refs.pop(0)
            users_out, user_accum_out, items_out, item_accum_out = refs
        else:
            users_out, user_accum_out, state_out = refs
    else:
        grad_out, state_out = refs
    left, right = pair_factors(sub_round, half, su, si, nu, ni, row_live, col_live, users.shape[0] // TILE)
    item_bf = factor.astype(BF)
    grad_items = DECAY * factor
    for start in range(0, users.shape[0], STEP):
        at = slice(start, start + STEP)
        user = users[at, :]
        user_bf = user.astype(BF)
        scores = dot(user_bf, item_bf, (1, 1))
        both = dot(left[:, at], right, (0, 0))
        err = (both[:, :HALF] * scores - both[:, HALF:]).astype(BF)
        grad_user = dot(err, item_bf, (1, 0))
        grad_items += dot(err, user_bf, (0, 0))
        if half == 0:
            grad_out[at, :] = grad_user
        else:
            grad = grad_in[at, :] + grad_user + DECAY * user
            users_out[at, :], user_accum_out[at, :] = adagrad(user, user_accum[at, :], grad)
    factor, accum = adagrad(factor, accum, grad_items)
    if half == 1 and last:
        items_out[:HALF, :] = other[:HALF, :]
        item_accum_out[:HALF, :] = other[HALF:, :]
        items_out[HALF:, :] = factor
        item_accum_out[HALF:, :] = accum
    else:
        state_out[:HALF, :] = factor
        state_out[HALF:, :] = accum


def run_half(sub_round, half, idx, users, state, extra=()):
    from_whole = isinstance(state, tuple)
    last = half == 1 and len(extra) == 3
    states = list(state) if from_whole else [state]
    user_shape = jax.ShapeDtypeStruct(users.shape, F32)
    state_shape = jax.ShapeDtypeStruct((2 * HALF, users.shape[1]), F32)
    if half == 0:
        out = [user_shape, state_shape]
    elif last:
        out = [user_shape, user_shape, state_shape, state_shape]
    else:
        out = [user_shape, user_shape, state_shape]
    smem = pl.BlockSpec(memory_space=pltpu.SMEM)
    vmem = pl.BlockSpec(memory_space=pltpu.VMEM)
    operands = [*idx, users, *states, *extra]
    size = users.shape[0] * HALF * users.shape[1]
    return pl.pallas_call(
        functools.partial(half_kernel, sub_round, half, from_whole, last),
        out_shape=out,
        in_specs=[smem] * 4 + [vmem] * (len(operands) - 4),
        out_specs=[vmem] * len(out),
        compiler_params=pltpu.CompilerParams(vmem_limit_bytes=24 * 1024 * 1024),
        cost_estimate=pl.CostEstimate(flops=10 * size, bytes_accessed=6 * 1024 * 1024, transcendentals=0),
        name="half_b" if half else "half_a",
    )(*operands)


def move(state, sub_round, half):
    blks, xors = lax.axis_size("blk"), lax.axis_size("xor")
    flip = 2 ** (sub_round % 2) if half == 1 else 0
    pairs = [
        (b * xors + x, ((b + 1) % blks) * xors + (x ^ flip)) for b in range(blks) for x in range(xors)
    ]
    return lax.ppermute(state, AXES, pairs)


def per_device(
    users,
    user_accum,
    items,
    item_accum,
    seen_user,
    seen_item,
    row_live,
    col_live,
    neg_user,
    neg_item,
):
    idx = (seen_user, seen_item, neg_user, neg_item, row_live, col_live)
    a = b = (items, item_accum)
    for s in range(SUBS):
        grad, a = run_half(s, 0, idx, users, a)
        if s + 1 < SUBS:
            a = move(a, s, 0)
            users, user_accum, b = run_half(s, 1, idx, users, b, (user_accum, grad))
            b = move(b, s, 1)
        else:
            return tuple(run_half(s, 1, idx, users, b, (user_accum, grad, a)))


def solution(mesh):
    rows = P(AXES, None)
    placed = (rows,) * 4 + (P(None, AXES),) * 2 + (P(None, AXES, None),) * 2 + (P(None, AXES),) * 2
    return jax.shard_map(
        per_device, mesh=mesh, in_specs=placed, out_specs=(rows,) * 4, check_vma=False
    )
```

profile of v0, /device:TPU:1, one launch (start us, length us, event | category | flops | bytes accessed | tf_op | source)
XLA Modules:
  0.0 150.4 jit_solution(5198425503645284142)
XLA Ops:
  10.5 3.8 %collective-permute-start.1 = (f32[512,256]{1,0:T(8,128)S(1)}, f32[512,256]{1,0:T(8,128)S(1)}, u32[]{:S(2)}, u32[]{:S(2)}) collective-permute-start(f32[512,256]{1,0:T(8,128)S(1)} %get-tuple-element.35), channel_id=1, source_target_pairs={{0,4},{1,5},{2,6},{3,7},{4,8},{5,9},{6,10},{7,11},{8,12},{9,13},{1... | collective-permute-start | bytes 1572872 | tf_op jit(solution)/shard_map/ppermute | solution.py:154
  14.4 2.3 %half_b.6 = (f32[1024,256]{1,0:T(8,128)S(1)}, f32[1024,256]{1,0:T(8,128)S(1)}, f32[512,256]{1,0:T(8,128)S(1)}) custom-call(s32[6,16]{1,0:T(8,128)S(1)} %copy-done.6, s32[6,16]{1,0:T(8,128)S(1)} %copy-done.7, s32[6,8]{1,0:T(8,128)S(1)} %copy-done.8, s32[6,8]{1,0:T(8,128)S(1)} %copy-done.9, s32[6,16,128]{2,1,0:T(8,128)S(1)} %copy-done, ...), custom_call_target="tpu_custom_call" | custom-call | flops 671088640 | bytes 6291456 | tf_op jit(solution)/shard_map/half_b/pallas_call | solution.py:137
  16.6 2.3 %collective-permute-start = (f32[512,256]{1,0:T(8,128)S(1)}, f32[512,256]{1,0:T(8,128)S(1)}, u32[]{:S(2)}, u32[]{:S(2)}) collective-permute-start(f32[512,256]{1,0:T(8,128)S(1)} %get-tuple-element.33), channel_id=1, source_target_pairs={{0,5},{1,4},{2,7},{3,6},{4,9},{5,8},{6,11},{7,10},{8,13},{9,12},{1... | collective-permute-start | bytes 1572872 | tf_op jit(solution)/shard_map/ppermute | solution.py:154
  18.9 12.7 %collective-permute-done.1.refs_7_ = f32[512,256]{1,0:T(8,128)S(1)} collective-permute-done((f32[512,256]{1,0:T(8,128)S(1)}, f32[512,256]{1,0:T(8,128)S(1)}, u32[]{:S(2)}, u32[]{:S(2)}) %collective-permute-start.1) | collective-permute-done | bytes 524320 | tf_op jit(solution)/shard_map/ppermute | solution.py:154
  31.7 2.2 %half_a.7 = (f32[1024,256]{1,0:T(8,128)S(1)}, f32[512,256]{1,0:T(8,128)S(1)}) custom-call(s32[6,16]{1,0:T(8,128)S(1)} %copy-done.6, s32[6,16]{1,0:T(8,128)S(1)} %copy-done.7, s32[6,8]{1,0:T(8,128)S(1)} %copy-done.8, s32[6,8]{1,0:T(8,128)S(1)} %copy-done.9, s32[6,16,128]{2,1,0:T(8,128)S(1)} %copy-done, s32[6,16,128]{2,1,0:T(8,128)S(1)} %copy-done.1, ...), custom_call_target="tpu_custom_call" | custom-call | flops 671088640 | bytes 6291456 | tf_op jit(solution)/shard_map/half_a/pallas_call | solution.py:137
  34.0 10.3 %collective-permute-done.refs_7_ = f32[512,256]{1,0:T(8,128)S(1)} collective-permute-done((f32[512,256]{1,0:T(8,128)S(1)}, f32[512,256]{1,0:T(8,128)S(1)}, u32[]{:S(2)}, u32[]{:S(2)}) %collective-permute-start) | collective-permute-done | bytes 524320 | tf_op jit(solution)/shard_map/ppermute | solution.py:154
  44.3 2.3 %half_b.7 = (f32[1024,256]{1,0:T(8,128)S(1)}, f32[1024,256]{1,0:T(8,128)S(1)}, f32[512,256]{1,0:T(8,128)S(1)}) custom-call(s32[6,16]{1,0:T(8,128)S(1)} %copy-done.6, s32[6,16]{1,0:T(8,128)S(1)} %copy-done.7, s32[6,8]{1,0:T(8,128)S(1)} %copy-done.8, s32[6,8]{1,0:T(8,128)S(1)} %copy-done.9, s32[6,16,128]{2,1,0:T(8,128)S(1)} %copy-done, ...), custom_call_target="tpu_custom_call" | custom-call | flops 671088640 | bytes 6291456 | tf_op jit(solution)/shard_map/half_b/pallas_call | solution.py:137
  46.6 7.1 %collective-permute-done.3.refs_7_ = f32[512,256]{1,0:T(8,128)S(1)} collective-permute-done((f32[512,256]{1,0:T(8,128)S(1)}, f32[512,256]{1,0:T(8,128)S(1)}, u32[]{:S(2)}, u32[]{:S(2)}) %collective-permute-start.3) | collective-permute-done | bytes 524320 | tf_op jit(solution)/shard_map/ppermute | solution.py:154
  53.7 2.2 %half_a.8 = (f32[1024,256]{1,0:T(8,128)S(1)}, f32[512,256]{1,0:T(8,128)S(1)}) custom-call(s32[6,16]{1,0:T(8,128)S(1)} %copy-done.6, s32[6,16]{1,0:T(8,128)S(1)} %copy-done.7, s32[6,8]{1,0:T(8,128)S(1)} %copy-done.8, s32[6,8]{1,0:T(8,128)S(1)} %copy-done.9, s32[6,16,128]{2,1,0:T(8,128)S(1)} %copy-done, s32[6,16,128]{2,1,0:T(8,128)S(1)} %copy-done.1, ...), custom_call_target="tpu_custom_call" | custom-call | flops 671088640 | bytes 6291456 | tf_op jit(solution)/shard_map/half_a/pallas_call | solution.py:137
  56.0 15.2 %collective-permute-done.2.refs_7_ = f32[512,256]{1,0:T(8,128)S(1)} collective-permute-done((f32[512,256]{1,0:T(8,128)S(1)}, f32[512,256]{1,0:T(8,128)S(1)}, u32[]{:S(2)}, u32[]{:S(2)}) %collective-permute-start.2) | collective-permute-done | bytes 524320 | tf_op jit(solution)/shard_map/ppermute | solution.py:154
  71.2 2.3 %half_b.8 = (f32[1024,256]{1,0:T(8,128)S(1)}, f32[1024,256]{1,0:T(8,128)S(1)}, f32[512,256]{1,0:T(8,128)S(1)}) custom-call(s32[6,16]{1,0:T(8,128)S(1)} %copy-done.6, s32[6,16]{1,0:T(8,128)S(1)} %copy-done.7, s32[6,8]{1,0:T(8,128)S(1)} %copy-done.8, s32[6,8]{1,0:T(8,128)S(1)} %copy-done.9, s32[6,16,128]{2,1,0:T(8,128)S(1)} %copy-done, ...), custom_call_target="tpu_custom_call" | custom-call | flops 671088640 | bytes 6291456 | tf_op jit(solution)/shard_map/half_b/pallas_call | solution.py:137
  73.5 3.8 %collective-permute-start.4 = (f32[512,256]{1,0:T(8,128)S(1)}, f32[512,256]{1,0:T(8,128)S(1)}, u32[]{:S(2)}, u32[]{:S(2)}) collective-permute-start(f32[512,256]{1,0:T(8,128)S(1)} %get-tuple-element.43), channel_id=1, source_target_pairs={{0,5},{1,4},{2,7},{3,6},{4,9},{5,8},{6,11},{7,10},{8,13},{9,12},{1... | collective-permute-start | bytes 1572872 | tf_op jit(solution)/shard_map/ppermute | solution.py:154
  77.3 2.2 %half_a.9 = (f32[1024,256]{1,0:T(8,128)S(1)}, f32[512,256]{1,0:T(8,128)S(1)}) custom-call(s32[6,16]{1,0:T(8,128)S(1)} %copy-done.6, s32[6,16]{1,0:T(8,128)S(1)} %copy-done.7, s32[6,8]{1,0:T(8,128)S(1)} %copy-done.8, s32[6,8]{1,0:T(8,128)S(1)} %copy-done.9, s32[6,16,128]{2,1,0:T(8,128)S(1)} %copy-done, s32[6,16,128]{2,1,0:T(8,128)S(1)} %copy-done.1, ...), custom_call_target="tpu_custom_call" | custom-call | flops 671088640 | bytes 6291456 | tf_op jit(solution)/shard_map/half_a/pallas_call | solution.py:137
  79.5 2.6 %collective-permute-start.7 = (f32[512,256]{1,0:T(8,128)S(1)}, f32[512,256]{1,0:T(8,128)S(1)}, u32[]{:S(2)}, u32[]{:S(2)}) collective-permute-start(f32[512,256]{1,0:T(8,128)S(1)} %get-tuple-element.50), channel_id=1, source_target_pairs={{0,4},{1,5},{2,6},{3,7},{4,8},{5,9},{6,10},{7,11},{8,12},{9,13},{1... | collective-permute-start | bytes 1572872 | tf_op jit(solution)/shard_map/ppermute | solution.py:154
  82.2 13.2 %collective-permute-done.4.refs_7_ = f32[512,256]{1,0:T(8,128)S(1)} collective-permute-done((f32[512,256]{1,0:T(8,128)S(1)}, f32[512,256]{1,0:T(8,128)S(1)}, u32[]{:S(2)}, u32[]{:S(2)}) %collective-permute-start.4) | collective-permute-done | bytes 524320 | tf_op jit(solution)/shard_map/ppermute | solution.py:154
  95.4 2.3 %half_b.9 = (f32[1024,256]{1,0:T(8,128)S(1)}, f32[1024,256]{1,0:T(8,128)S(1)}, f32[512,256]{1,0:T(8,128)S(1)}) custom-call(s32[6,16]{1,0:T(8,128)S(1)} %copy-done.6, s32[6,16]{1,0:T(8,128)S(1)} %copy-done.7, s32[6,8]{1,0:T(8,128)S(1)} %copy-done.8, s32[6,8]{1,0:T(8,128)S(1)} %copy-done.9, s32[6,16,128]{2,1,0:T(8,128)S(1)} %copy-done, ...), custom_call_target="tpu_custom_call" | custom-call | flops 671088640 | bytes 6291456 | tf_op jit(solution)/shard_map/half_b/pallas_call | solution.py:137
  97.7 8.1 %collective-permute-done.7.refs_7_ = f32[512,256]{1,0:T(8,128)S(1)} collective-permute-done((f32[512,256]{1,0:T(8,128)S(1)}, f32[512,256]{1,0:T(8,128)S(1)}, u32[]{:S(2)}, u32[]{:S(2)}) %collective-permute-start.7) | collective-permute-done | bytes 524320 | tf_op jit(solution)/shard_map/ppermute | solution.py:154
  105.9 2.2 %half_a.10 = (f32[1024,256]{1,0:T(8,128)S(1)}, f32[512,256]{1,0:T(8,128)S(1)}) custom-call(s32[6,16]{1,0:T(8,128)S(1)} %copy-done.6, s32[6,16]{1,0:T(8,128)S(1)} %copy-done.7, s32[6,8]{1,0:T(8,128)S(1)} %copy-done.8, s32[6,8]{1,0:T(8,128)S(1)} %copy-done.9, s32[6,16,128]{2,1,0:T(8,128)S(1)} %copy-done, s32[6,16,128]{2,1,0:T(8,128)S(1)} %copy-done.1, ...), custom_call_target="tpu_custom_call" | custom-call | flops 671088640 | bytes 6291456 | tf_op jit(solution)/shard_map/half_a/pallas_call | solution.py:137
  108.2 14.7 %collective-permute-done.6.refs_7_ = f32[512,256]{1,0:T(8,128)S(1)} collective-permute-done((f32[512,256]{1,0:T(8,128)S(1)}, f32[512,256]{1,0:T(8,128)S(1)}, u32[]{:S(2)}, u32[]{:S(2)}) %collective-permute-start.6) | collective-permute-done | bytes 524320 | tf_op jit(solution)/shard_map/ppermute | solution.py:154
  122.9 2.3 %half_b.10 = (f32[1024,256]{1,0:T(8,128)S(1)}, f32[1024,256]{1,0:T(8,128)S(1)}, f32[512,256]{1,0:T(8,128)S(1)}) custom-call(s32[6,16]{1,0:T(8,128)S(1)} %copy-done.6, s32[6,16]{1,0:T(8,128)S(1)} %copy-done.7, s32[6,8]{1,0:T(8,128)S(1)} %copy-done.8, s32[6,8]{1,0:T(8,128)S(1)} %copy-done.9, s32[6,16,128]{2,1,0:T(8,128)S(1)} %copy-done, ...), custom_call_target="tpu_custom_call" | custom-call | flops 671088640 | bytes 6291456 | tf_op jit(solution)/shard_map/half_b/pallas_call | solution.py:137
  125.1 4.2 %collective-permute-start.8 = (f32[512,256]{1,0:T(8,128)S(1)}, f32[512,256]{1,0:T(8,128)S(1)}, u32[]{:S(2)}, u32[]{:S(2)}) collective-permute-start(f32[512,256]{1,0:T(8,128)S(1)} %get-tuple-element.53), channel_id=1, source_target_pairs={{0,5},{1,4},{2,7},{3,6},{4,9},{5,8},{6,11},{7,10},{8,13},{9,12},{1... | collective-permute-start | bytes 1572872 | tf_op jit(solution)/shard_map/ppermute | solution.py:154
  129.3 2.2 %half_a.11 = (f32[1024,256]{1,0:T(8,128)S(1)}, f32[512,256]{1,0:T(8,128)S(1)}) custom-call(s32[6,16]{1,0:T(8,128)S(1)} %copy-done.6, s32[6,16]{1,0:T(8,128)S(1)} %copy-done.7, s32[6,8]{1,0:T(8,128)S(1)} %copy-done.8, s32[6,8]{1,0:T(8,128)S(1)} %copy-done.9, s32[6,16,128]{2,1,0:T(8,128)S(1)} %copy-done, s32[6,16,128]{2,1,0:T(8,128)S(1)} %copy-done.1, ...), custom_call_target="tpu_custom_call" | custom-call | flops 671088640 | bytes 6291456 | tf_op jit(solution)/shard_map/half_a/pallas_call | solution.py:137
  131.5 15.1 %collective-permute-done.8.refs_7_ = f32[512,256]{1,0:T(8,128)S(1)} collective-permute-done((f32[512,256]{1,0:T(8,128)S(1)}, f32[512,256]{1,0:T(8,128)S(1)}, u32[]{:S(2)}, u32[]{:S(2)}) %collective-permute-start.8) | collective-permute-done | bytes 524320 | tf_op jit(solution)/shard_map/ppermute | solution.py:154
  146.6 3.8 %half_b.11 = (f32[1024,256]{1,0:T(8,128)}, f32[1024,256]{1,0:T(8,128)}, f32[512,256]{1,0:T(8,128)}, f32[512,256]{1,0:T(8,128)}) custom-call(s32[6,16]{1,0:T(8,128)S(1)} %copy-done.6, s32[6,16]{1,0:T(8,128)S(1)} %copy-done.7, s32[6,8]{1,0:T(8,128)S(1)} %copy-done.8, s32[6,8]{1,0:T(8,128)S(1)} %copy-done.9, s32[6,16,128]{2,1,0:T(8,128)S(1)} %copy-done, ...), custom_call_target="tpu_custom_call" | custom-call | flops 671088640 | bytes 6291456 | tf_op jit(solution)/shard_map/half_b/pallas_call | solution.py:137
  (28 shorter events, 10.3 us)
Async XLA Ops:
  0.6 0.8 copy-start
  1.4 0.8 copy-start.1
  2.2 1.2 copy-start.2
  3.5 1.0 copy-start.4
  4.5 1.0 copy-start.5
  5.5 0.7 copy-start.6
  6.2 0.7 copy-start.7
  6.9 0.7 copy-start.8
  7.6 0.7 copy-start.9
  8.3 6.1 %copy-start.3 = (f32[1024,256]{1,0:T(8,128)S(1)}, f32[1024,256]{1,0:T(8,128)}, u32[]{:S(2)}) copy-start(f32[1024,256]{1,0:T(8,128)} %refs_9_.1) | copy-start | bytes 3145732
  10.5 21.1 %collective-permute-start.1 = (f32[512,256]{1,0:T(8,128)S(1)}, f32[512,256]{1,0:T(8,128)S(1)}, u32[]{:S(2)}, u32[]{:S(2)}) collective-permute-start(f32[512,256]{1,0:T(8,128)S(1)} %get-tuple-element.35), channel_id=1, source_target_pairs={{0,4},{1,5},{2,6},{3,7},{4,8},{5,9},{6,10},{7,11},{8,12},{9,13},{1... | collective-permute-start | bytes 1572872 | tf_op jit(solution)/shard_map/ppermute | solution.py:154
  16.6 27.6 %collective-permute-start = (f32[512,256]{1,0:T(8,128)S(1)}, f32[512,256]{1,0:T(8,128)S(1)}, u32[]{:S(2)}, u32[]{:S(2)}) collective-permute-start(f32[512,256]{1,0:T(8,128)S(1)} %get-tuple-element.33), channel_id=1, source_target_pairs={{0,5},{1,4},{2,7},{3,6},{4,9},{5,8},{6,11},{7,10},{8,13},{9,12},{1... | collective-permute-start | bytes 1572872 | tf_op jit(solution)/shard_map/ppermute | solution.py:154
  33.9 19.8 %collective-permute-start.3 = (f32[512,256]{1,0:T(8,128)S(1)}, f32[512,256]{1,0:T(8,128)S(1)}, u32[]{:S(2)}, u32[]{:S(2)}) collective-permute-start(f32[512,256]{1,0:T(8,128)S(1)} %get-tuple-element.40), channel_id=1, source_target_pairs={{0,4},{1,5},{2,6},{3,7},{4,8},{5,9},{6,10},{7,11},{8,12},{9,13},{1... | collective-permute-start | bytes 1572872 | tf_op jit(solution)/shard_map/ppermute | solution.py:154
  46.6 24.7 %collective-permute-start.2 = (f32[512,256]{1,0:T(8,128)S(1)}, f32[512,256]{1,0:T(8,128)S(1)}, u32[]{:S(2)}, u32[]{:S(2)}) collective-permute-start(f32[512,256]{1,0:T(8,128)S(1)} %get-tuple-element.38), channel_id=1, source_target_pairs={{0,6},{1,7},{2,4},{3,5},{4,10},{5,11},{6,8},{7,9},{8,14},{9,15},{1... | collective-permute-start | bytes 1572872 | tf_op jit(solution)/shard_map/ppermute | solution.py:154
  56.0 21.3 %collective-permute-start.5 = (f32[512,256]{1,0:T(8,128)S(1)}, f32[512,256]{1,0:T(8,128)S(1)}, u32[]{:S(2)}, u32[]{:S(2)}) collective-permute-start(f32[512,256]{1,0:T(8,128)S(1)} %get-tuple-element.45), channel_id=1, source_target_pairs={{0,4},{1,5},{2,6},{3,7},{4,8},{5,9},{6,10},{7,11},{8,12},{9,13},{1... | collective-permute-start | bytes 1572872 | tf_op jit(solution)/shard_map/ppermute | solution.py:154
  73.5 21.9 %collective-permute-start.4 = (f32[512,256]{1,0:T(8,128)S(1)}, f32[512,256]{1,0:T(8,128)S(1)}, u32[]{:S(2)}, u32[]{:S(2)}) collective-permute-start(f32[512,256]{1,0:T(8,128)S(1)} %get-tuple-element.43), channel_id=1, source_target_pairs={{0,5},{1,4},{2,7},{3,6},{4,9},{5,8},{6,11},{7,10},{8,13},{9,12},{1... | collective-permute-start | bytes 1572872 | tf_op jit(solution)/shard_map/ppermute | solution.py:154
  79.5 26.3 %collective-permute-start.7 = (f32[512,256]{1,0:T(8,128)S(1)}, f32[512,256]{1,0:T(8,128)S(1)}, u32[]{:S(2)}, u32[]{:S(2)}) collective-permute-start(f32[512,256]{1,0:T(8,128)S(1)} %get-tuple-element.50), channel_id=1, source_target_pairs={{0,4},{1,5},{2,6},{3,7},{4,8},{5,9},{6,10},{7,11},{8,12},{9,13},{1... | collective-permute-start | bytes 1572872 | tf_op jit(solution)/shard_map/ppermute | solution.py:154
  97.6 25.2 %collective-permute-start.6 = (f32[512,256]{1,0:T(8,128)S(1)}, f32[512,256]{1,0:T(8,128)S(1)}, u32[]{:S(2)}, u32[]{:S(2)}) collective-permute-start(f32[512,256]{1,0:T(8,128)S(1)} %get-tuple-element.48), channel_id=1, source_target_pairs={{0,6},{1,7},{2,4},{3,5},{4,10},{5,11},{6,8},{7,9},{8,14},{9,15},{1... | collective-permute-start | bytes 1572872 | tf_op jit(solution)/shard_map/ppermute | solution.py:154
  108.1 21.2 %collective-permute-start.9 = (f32[512,256]{1,0:T(8,128)S(1)}, f32[512,256]{1,0:T(8,128)S(1)}, u32[]{:S(2)}, u32[]{:S(2)}) collective-permute-start(f32[512,256]{1,0:T(8,128)S(1)} %get-tuple-element.55), channel_id=1, source_target_pairs={{0,4},{1,5},{2,6},{3,7},{4,8},{5,9},{6,10},{7,11},{8,12},{9,13},{1... | collective-permute-start | bytes 1572872 | tf_op jit(solution)/shard_map/ppermute | solution.py:154
  125.1 21.5 %collective-permute-start.8 = (f32[512,256]{1,0:T(8,128)S(1)}, f32[512,256]{1,0:T(8,128)S(1)}, u32[]{:S(2)}, u32[]{:S(2)}) collective-permute-start(f32[512,256]{1,0:T(8,128)S(1)} %get-tuple-element.53), channel_id=1, source_target_pairs={{0,5},{1,4},{2,7},{3,6},{4,9},{5,8},{6,11},{7,10},{8,13},{9,12},{1... | collective-permute-start | bytes 1572872 | tf_op jit(solution)/shard_map/ppermute | solution.py:154
where the time goes:
time: 151 us; the launch traced here: 150 us
  waiting for transfers between devices  96.3 us (64%)
  Pallas kernels  28.6 us (19%)
  starting transfers between devices  17.1 us (11%)
  local copies, waits for them, and re-layouts  7.64 us (5%)
    ppermute x10, waiting for transfers between devices, move(): return lax.ppermute(state, AXES, pairs)  96.3 us
    pallas_call x12, Pallas kernels, run_half(): pl.pallas_call(functools.partial(half_kernel, sub_round, half, from_whole...  28.6 us
    ppermute x10, starting transfers between devices, move(): return lax.ppermute(state, AXES, pairs)  17.1 us
    unnamed x20, local copies, waits for them, and re-layouts  7.64 us
  transfers between devices with their start and end apart: 10, of which 8 were waited for; matrix products, arithmetic and copies ran while one was open for 0% of the time, Pallas kernels for 15%

commit v1 on v0

v1 whole, which is shorter than its diff:
```python
import functools

import jax
import jax.numpy as jnp
from jax import lax
from jax.experimental import pallas as pl
from jax.experimental.pallas import tpu as pltpu
from jax.sharding import PartitionSpec as P

SUBS = 6
TILE = 128
CHUNK = 128
STEP = 256
LEARN_RATE = 0.05
DECAY = 0.02
NEG_WEIGHT = 0.25
AXES = ("blk", "xor")
BF = jnp.bfloat16
F32 = jnp.float32


def rows_of(scalars, sub_round, count):
    row = lax.broadcasted_iota(jnp.int32, (count, TILE), 0)
    out = jnp.zeros((count, TILE), jnp.int32)
    for t in range(count):
        out = jnp.where(row == t, scalars[sub_round, t], out)
    return out


def spread(tile, live, first, count):
    groups = [jnp.where(tile == first + n, live, 0.0) for n in range(count)]
    return groups[0] if count == 1 else jnp.concatenate(groups, axis=1)


def pair_factors(sub_round, chunk, su, si, nu, ni, row_live, col_live, user_tiles):
    obs, neg = su.shape[1], nu.shape[1]
    rows = row_live[sub_round].astype(F32)
    cols = col_live[sub_round].astype(F32)
    ones = jnp.ones((neg, TILE), F32)
    left = jnp.concatenate(
        [
            spread(rows_of(su, sub_round, obs), rows, 0, user_tiles),
            spread(rows_of(nu, sub_round, neg), ones, 0, user_tiles),
        ],
        axis=0,
    ).astype(BF)
    count = CHUNK // TILE
    seen = spread(rows_of(si, sub_round, obs), cols, chunk * count, count)
    sampled = spread(rows_of(ni, sub_round, neg), ones, chunk * count, count)
    right = jnp.concatenate(
        [
            jnp.concatenate([seen, seen], axis=1),
            jnp.concatenate([NEG_WEIGHT * sampled, jnp.zeros_like(sampled)], axis=1),
        ],
        axis=0,
    ).astype(BF)
    return left, right


def adagrad(factor, accum, grad):
    accum = accum + grad * grad
    return factor - LEARN_RATE * grad * lax.rsqrt(accum), accum


def dot(a, b, contract):
    return lax.dot_general(a, b, ((contract[:1], contract[1:]), ((), ())), preferred_element_type=F32)


def chunk_kernel(sub_round, chunk, chunks, *refs):
    refs = list(refs)

    def take(count):
        out = refs[:count]
        del refs[:count]
        return out

    first, final = chunk == 0, chunk == chunks - 1
    end = sub_round == SUBS - 1
    su, si, nu, ni, row_live, col_live, users = take(7)
    if sub_round == 0:
        factor_ref, accum_ref = take(2)
        at = slice(chunk * CHUNK, (chunk + 1) * CHUNK)
        if factor_ref.shape[0] == CHUNK:
            at = slice(None)
        factor, accum = factor_ref[at, :], accum_ref[at, :]
    else:
        (state,) = take(1)
        factor, accum = state[:CHUNK, :], state[CHUNK:, :]
    if not first:
        (grad_in,) = take(1)
    if final:
        (user_accum,) = take(1)
        if end:
            others = take(chunks - 1)
        users_out, user_accum_out = take(2)
    else:
        (grad_out,) = take(1)
    left, right = pair_factors(sub_round, chunk, su, si, nu, ni, row_live, col_live, users.shape[0] // TILE)
    item_bf = factor.astype(BF)
    grad_items = DECAY * factor
    for start in range(0, users.shape[0], STEP):
        at = slice(start, start + STEP)
        user = users[at, :]
        user_bf = user.astype(BF)
        scores = dot(user_bf, item_bf, (1, 1))
        both = dot(left[:, at], right, (0, 0))
        err = (both[:, :CHUNK] * scores - both[:, CHUNK:]).astype(BF)
        grad_user = dot(err, item_bf, (1, 0))
        grad_items += dot(err, user_bf, (0, 0))
        if not first:
            grad_user += grad_in[at, :]
        if final:
            grad_user += DECAY * user
            users_out[at, :], user_accum_out[at, :] = adagrad(user, user_accum[at, :], grad_user)
        else:
            grad_out[at, :] = grad_user
    factor, accum = adagrad(factor, accum, grad_items)
    if final and end:
        items_out, item_accum_out = refs
        for n, other in enumerate(others):
            items_out[n * CHUNK : (n + 1) * CHUNK, :] = other[:CHUNK, :]
            item_accum_out[n * CHUNK : (n + 1) * CHUNK, :] = other[CHUNK:, :]
        items_out[chunk * CHUNK :, :] = factor
        item_accum_out[chunk * CHUNK :, :] = accum
    else:
        (state_out,) = refs
        state_out[:CHUNK, :] = factor
        state_out[CHUNK:, :] = accum


def run_chunk(sub_round, chunk, chunks, idx, users, state, extra):
    width = users.shape[1]
    user_shape = jax.ShapeDtypeStruct(users.shape, F32)
    state_shape = jax.ShapeDtypeStruct((2 * CHUNK, width), F32)
    final, end = chunk == chunks - 1, sub_round == SUBS - 1
    out = [user_shape] * (2 if final else 1)
    if final and end:
        out += [jax.ShapeDtypeStruct((chunks * CHUNK, width), F32)] * 2
    else:
        out += [state_shape]
    smem = pl.BlockSpec(memory_space=pltpu.SMEM)
    vmem = pl.BlockSpec(memory_space=pltpu.VMEM)
    operands = [*idx, users, *state, *extra]
    in_specs = [smem] * 4 + [vmem] * (len(operands) - 4)
    out_specs = [vmem] * len(out)
    grid = ()
    if sub_round == 0 and chunk == 0:
        grid = (1,)
        whole = lambda x: pl.BlockSpec(x.shape, lambda i: (0,) * len(x.shape))
        part = pl.BlockSpec((CHUNK, width), lambda i: (0, 0))
        live = pl.BlockSpec((1, *idx[4].shape[1:]), lambda i: (0, 0, 0))
        in_specs = [smem] * 4 + [live] * 2 + [whole(users), part, part]
        out_specs = [whole(x) for x in out]
    size = users.shape[0] * CHUNK * width
    return pl.pallas_call(
        functools.partial(chunk_kernel, sub_round, chunk, chunks),
        grid=grid,
        out_shape=out,
        in_specs=in_specs,
        out_specs=out_specs,
        compiler_params=pltpu.CompilerParams(vmem_limit_bytes=24 * 1024 * 1024),
        cost_estimate=pl.CostEstimate(flops=10 * size, bytes_accessed=6 * 1024 * 1024, transcendentals=0),
        name=f"sub{sub_round}_chunk{chunk}",
    )(*operands)


def move(state, sub_round, second_half):
    blks, xors = lax.axis_size("blk"), lax.axis_size("xor")
    flip = 2 ** (sub_round % 2) if second_half else 0
    pairs = [
        (b * xors + x, ((b + 1) % blks) * xors + (x ^ flip)) for b in range(blks) for x in range(xors)
    ]
    return lax.ppermute(state, AXES, pairs)


def per_device(
    users,
    user_accum,
    items,
    item_accum,
    seen_user,
    seen_item,
    row_live,
    col_live,
    neg_user,
    neg_item,
):
    idx = (seen_user, seen_item, neg_user, neg_item, row_live, col_live)
    chunks = items.shape[0] // CHUNK
    states = [(items, item_accum)] * chunks
    for s in range(SUBS):
        grad = ()
        moved = []
        for n in range(chunks):
            final, end = n == chunks - 1, s == SUBS - 1
            extra = (*grad, user_accum) if final else grad
            if final and end:
                return tuple(run_chunk(s, n, chunks, idx, users, states[n], (*extra, *(m[0] for m in moved))))
            *grad, state = run_chunk(s, n, chunks, idx, users, states[n], extra)
            if not end:
                state = move(state, s, n >= chunks // 2)
            moved.append((state,))
        users, user_accum = grad
        states = moved


def solution(mesh):
    rows = P(AXES, None)
    placed = (rows,) * 4 + (P(None, AXES),) * 2 + (P(None, AXES, None),) * 2 + (P(None, AXES),) * 2
    return jax.shard_map(
        per_device, mesh=mesh, in_specs=placed, out_specs=(rows,) * 4, check_vma=False
    )
```

time: 151 us -> 139 us (0.921)
  waiting for transfers between devices: 96.3 us -> 39.6 us
  starting transfers between devices: 17.1 us -> 39.6 us
  Pallas kernels: 28.6 us -> 51 us
    ppermute x10 -> x20, waiting for transfers between devices: 96.3 us -> 39.6 us  [move(): return lax.ppermute(state, AXES, pairs)]
    ppermute x10 -> x20, starting transfers between devices: 17.1 us -> 39.6 us  [move(): return lax.ppermute(state, AXES, pairs)]
    pallas_call x12 -> x24, Pallas kernels: 28.6 us -> 51 us  [run_chunk(): pl.pallas_call(functools.partial(chunk_kernel, sub_round, chunk, chunks),...]
  transfers between devices with their start and end apart: 10 -> 20, of which waited for: 8 -> 10; matrix products, arithmetic and copies ran while one was open for 0% -> 0% of each run, Pallas kernels for 15% -> 33%
where the time goes in v1:
time: 139 us
  Pallas kernels  51 us (37%)
  starting transfers between devices  39.6 us (28%)
  waiting for transfers between devices  39.6 us (28%)
  local copies, waits for them, and re-layouts  7.64 us (5%)
    pallas_call x24, Pallas kernels, run_chunk(): pl.pallas_call(functools.partial(chunk_kernel, sub_round, chunk, chunks),...  51 us
    ppermute x20, waiting for transfers between devices, move(): return lax.ppermute(state, AXES, pairs)  39.6 us
    ppermute x20, starting transfers between devices, move(): return lax.ppermute(state, AXES, pairs)  39.6 us
    unnamed x20, local copies, waits for them, and re-layouts  7.64 us
  transfers between devices with their start and end apart: 20, of which 10 were waited for; matrix products, arithmetic and copies ran while one was open for 0% of the time, Pallas kernels for 33%

profile of v1, /device:TPU:1, one launch (start us, length us, event | category | flops | bytes accessed | tf_op | source)
XLA Modules:
  0.0 138.8 jit_solution(12671657690623230852)
XLA Ops:
  10.2 3.8 %collective-permute-start.3 = (f32[256,256]{1,0:T(8,128)S(1)}, f32[256,256]{1,0:T(8,128)S(1)}, u32[]{:S(2)}, u32[]{:S(2)}) collective-permute-start(f32[256,256]{1,0:T(8,128)S(1)} %get-tuple-element.62), channel_id=1, source_target_pairs={{0,4},{1,5},{2,6},{3,7},{4,8},{5,9},{6,10},{7,11},{8,12},{9,13},{1... | collective-permute-start | bytes 786440 | tf_op jit(solution)/shard_map/ppermute | solution.py:173
  19.7 4.1 %collective-permute-start.1 = (f32[256,256]{1,0:T(8,128)S(1)}, f32[256,256]{1,0:T(8,128)S(1)}, u32[]{:S(2)}, u32[]{:S(2)}) collective-permute-start(f32[256,256]{1,0:T(8,128)S(1)} %get-tuple-element.60), channel_id=1, source_target_pairs={{0,5},{1,4},{2,7},{3,6},{4,9},{5,8},{6,11},{7,10},{8,13},{9,12},{1... | collective-permute-start | bytes 786440 | tf_op jit(solution)/shard_map/ppermute | solution.py:173
  23.8 2.1 %sub0_chunk3.1 = (f32[1024,256]{1,0:T(8,128)S(1)}, f32[1024,256]{1,0:T(8,128)S(1)}, f32[256,256]{1,0:T(8,128)S(1)}) custom-call(s32[6,16]{1,0:T(8,128)S(1)} %copy-done.5, s32[6,16]{1,0:T(8,128)S(1)} %copy-done.6, s32[6,8]{1,0:T(8,128)S(1)} %copy-done.7, s32[6,8]{1,0:T(8,128)S(1)} %copy-done.8, s32[6,16,128]{2,1,0:T(8,128)S(1)} %copy-done, ...), custom_call_target="tpu_custom_call" | custom-call | flops 335544320 | bytes 6291456 | tf_op jit(solution)/shard_map/sub0_chunk3/pallas_call | solution.py:155
  28.5 3.0 %collective-permute-start.7 = (f32[256,256]{1,0:T(8,128)S(1)}, f32[256,256]{1,0:T(8,128)S(1)}, u32[]{:S(2)}, u32[]{:S(2)}) collective-permute-start(f32[256,256]{1,0:T(8,128)S(1)} %get-tuple-element.71), channel_id=1, source_target_pairs={{0,4},{1,5},{2,6},{3,7},{4,8},{5,9},{6,10},{7,11},{8,12},{9,13},{1... | collective-permute-start | bytes 786440 | tf_op jit(solution)/shard_map/ppermute | solution.py:173
  34.8 3.8 %collective-permute-done.1.refs_7_ = f32[256,256]{1,0:T(8,128)S(1)} collective-permute-done((f32[256,256]{1,0:T(8,128)S(1)}, f32[256,256]{1,0:T(8,128)S(1)}, u32[]{:S(2)}, u32[]{:S(2)}) %collective-permute-start.1) | collective-permute-done | bytes 262176 | tf_op jit(solution)/shard_map/ppermute | solution.py:173
  40.8 3.1 %collective-permute-done.refs_7_ = f32[256,256]{1,0:T(8,128)S(1)} collective-permute-done((f32[256,256]{1,0:T(8,128)S(1)}, f32[256,256]{1,0:T(8,128)S(1)}, u32[]{:S(2)}, u32[]{:S(2)}) %collective-permute-start) | collective-permute-done | bytes 262176 | tf_op jit(solution)/shard_map/ppermute | solution.py:173
  43.9 2.1 %sub1_chunk3.1 = (f32[1024,256]{1,0:T(8,128)S(1)}, f32[1024,256]{1,0:T(8,128)S(1)}, f32[256,256]{1,0:T(8,128)S(1)}) custom-call(s32[6,16]{1,0:T(8,128)S(1)} %copy-done.5, s32[6,16]{1,0:T(8,128)S(1)} %copy-done.6, s32[6,8]{1,0:T(8,128)S(1)} %copy-done.7, s32[6,8]{1,0:T(8,128)S(1)} %copy-done.8, s32[6,16,128]{2,1,0:T(8,128)S(1)} %copy-done, ...), custom_call_target="tpu_custom_call" | custom-call | flops 335544320 | bytes 6291456 | tf_op jit(solution)/shard_map/sub1_chunk3/pallas_call | solution.py:155
  50.3 3.5 %collective-permute-done.6.refs_7_ = f32[256,256]{1,0:T(8,128)S(1)} collective-permute-done((f32[256,256]{1,0:T(8,128)S(1)}, f32[256,256]{1,0:T(8,128)S(1)}, u32[]{:S(2)}, u32[]{:S(2)}) %collective-permute-start.6) | collective-permute-done | bytes 262176 | tf_op jit(solution)/shard_map/ppermute | solution.py:173
  56.0 9.1 %collective-permute-done.5.refs_7_ = f32[256,256]{1,0:T(8,128)S(1)} collective-permute-done((f32[256,256]{1,0:T(8,128)S(1)}, f32[256,256]{1,0:T(8,128)S(1)}, u32[]{:S(2)}, u32[]{:S(2)}) %collective-permute-start.5) | collective-permute-done | bytes 262176 | tf_op jit(solution)/shard_map/ppermute | solution.py:173
  67.2 4.1 %collective-permute-start.9 = (f32[256,256]{1,0:T(8,128)S(1)}, f32[256,256]{1,0:T(8,128)S(1)}, u32[]{:S(2)}, u32[]{:S(2)}) collective-permute-start(f32[256,256]{1,0:T(8,128)S(1)} %get-tuple-element.78), channel_id=1, source_target_pairs={{0,5},{1,4},{2,7},{3,6},{4,9},{5,8},{6,11},{7,10},{8,13},{9,12},{1... | collective-permute-start | bytes 786440 | tf_op jit(solution)/shard_map/ppermute | solution.py:173
  71.3 2.1 %sub2_chunk3.1 = (f32[1024,256]{1,0:T(8,128)S(1)}, f32[1024,256]{1,0:T(8,128)S(1)}, f32[256,256]{1,0:T(8,128)S(1)}) custom-call(s32[6,16]{1,0:T(8,128)S(1)} %copy-done.5, s32[6,16]{1,0:T(8,128)S(1)} %copy-done.6, s32[6,8]{1,0:T(8,128)S(1)} %copy-done.7, s32[6,8]{1,0:T(8,128)S(1)} %copy-done.8, s32[6,16,128]{2,1,0:T(8,128)S(1)} %copy-done, ...), custom_call_target="tpu_custom_call" | custom-call | flops 335544320 | bytes 6291456 | tf_op jit(solution)/shard_map/sub2_chunk3/pallas_call | solution.py:155
  73.4 3.4 %collective-permute-start.8 = (f32[256,256]{1,0:T(8,128)S(1)}, f32[256,256]{1,0:T(8,128)S(1)}, u32[]{:S(2)}, u32[]{:S(2)}) collective-permute-start(f32[256,256]{1,0:T(8,128)S(1)} %get-tuple-element.77), channel_id=1, source_target_pairs={{0,5},{1,4},{2,7},{3,6},{4,9},{5,8},{6,11},{7,10},{8,13},{9,12},{1... | collective-permute-start | bytes 786440 | tf_op jit(solution)/shard_map/ppermute | solution.py:173
  78.7 2.4 %collective-permute-start.15 = (f32[256,256]{1,0:T(8,128)S(1)}, f32[256,256]{1,0:T(8,128)S(1)}, u32[]{:S(2)}, u32[]{:S(2)}) collective-permute-start(f32[256,256]{1,0:T(8,128)S(1)} %get-tuple-element.89), channel_id=1, source_target_pairs={{0,4},{1,5},{2,6},{3,7},{4,8},{5,9},{6,10},{7,11},{8,12},{9,13},{1... | collective-permute-start | bytes 786440 | tf_op jit(solution)/shard_map/ppermute | solution.py:173
  81.1 2.1 %sub3_chunk1.1 = (f32[1024,256]{1,0:T(8,128)S(1)}, f32[256,256]{1,0:T(8,128)S(1)}) custom-call(s32[6,16]{1,0:T(8,128)S(1)} %copy-done.5, s32[6,16]{1,0:T(8,128)S(1)} %copy-done.6, s32[6,8]{1,0:T(8,128)S(1)} %copy-done.7, s32[6,8]{1,0:T(8,128)S(1)} %copy-done.8, s32[6,16,128]{2,1,0:T(8,128)S(1)} %copy-done, s32[6,16,128]{2,1,0:T(8,128)S(1)} %copy-done.1, ...), custom_call_target="tpu_custom_call" | custom-call | flops 335544320 | bytes 6291456 | tf_op jit(solution)/shard_map/sub3_chunk1/pallas_call | solution.py:155
  87.5 3.1 %collective-permute-start.13 = (f32[256,256]{1,0:T(8,128)S(1)}, f32[256,256]{1,0:T(8,128)S(1)}, u32[]{:S(2)}, u32[]{:S(2)}) collective-permute-start(f32[256,256]{1,0:T(8,128)S(1)} %get-tuple-element.87), channel_id=1, source_target_pairs={{0,6},{1,7},{2,4},{3,5},{4,10},{5,11},{6,8},{7,9},{8,14},{9,15},{1... | collective-permute-start | bytes 786440 | tf_op jit(solution)/shard_map/ppermute | solution.py:173
  90.6 2.1 %sub3_chunk3.1 = (f32[1024,256]{1,0:T(8,128)S(1)}, f32[1024,256]{1,0:T(8,128)S(1)}, f32[256,256]{1,0:T(8,128)S(1)}) custom-call(s32[6,16]{1,0:T(8,128)S(1)} %copy-done.5, s32[6,16]{1,0:T(8,128)S(1)} %copy-done.6, s32[6,8]{1,0:T(8,128)S(1)} %copy-done.7, s32[6,8]{1,0:T(8,128)S(1)} %copy-done.8, s32[6,16,128]{2,1,0:T(8,128)S(1)} %copy-done, ...), custom_call_target="tpu_custom_call" | custom-call | flops 335544320 | bytes 6291456 | tf_op jit(solution)/shard_map/sub3_chunk3/pallas_call | solution.py:155
  96.5 3.1 %collective-permute-done.14.refs_7_ = f32[256,256]{1,0:T(8,128)S(1)} collective-permute-done((f32[256,256]{1,0:T(8,128)S(1)}, f32[256,256]{1,0:T(8,128)S(1)}, u32[]{:S(2)}, u32[]{:S(2)}) %collective-permute-start.14) | collective-permute-done | bytes 262176 | tf_op jit(solution)/shard_map/ppermute | solution.py:173
  102.0 9.1 %collective-permute-done.13.refs_7_ = f32[256,256]{1,0:T(8,128)S(1)} collective-permute-done((f32[256,256]{1,0:T(8,128)S(1)}, f32[256,256]{1,0:T(8,128)S(1)}, u32[]{:S(2)}, u32[]{:S(2)}) %collective-permute-start.13) | collective-permute-done | bytes 262176 | tf_op jit(solution)/shard_map/ppermute | solution.py:173
  113.2 4.7 %collective-permute-start.17 = (f32[256,256]{1,0:T(8,128)S(1)}, f32[256,256]{1,0:T(8,128)S(1)}, u32[]{:S(2)}, u32[]{:S(2)}) collective-permute-start(f32[256,256]{1,0:T(8,128)S(1)} %get-tuple-element.96), channel_id=1, source_target_pairs={{0,5},{1,4},{2,7},{3,6},{4,9},{5,8},{6,11},{7,10},{8,13},{9,12},{1... | collective-permute-start | bytes 786440 | tf_op jit(solution)/shard_map/ppermute | solution.py:173
  117.9 2.1 %sub4_chunk3.1 = (f32[1024,256]{1,0:T(8,128)S(1)}, f32[1024,256]{1,0:T(8,128)S(1)}, f32[256,256]{1,0:T(8,128)S(1)}) custom-call(s32[6,16]{1,0:T(8,128)S(1)} %copy-done.5, s32[6,16]{1,0:T(8,128)S(1)} %copy-done.6, s32[6,8]{1,0:T(8,128)S(1)} %copy-done.7, s32[6,8]{1,0:T(8,128)S(1)} %copy-done.8, s32[6,16,128]{2,1,0:T(8,128)S(1)} %copy-done, ...), custom_call_target="tpu_custom_call" | custom-call | flops 335544320 | bytes 6291456 | tf_op jit(solution)/shard_map/sub4_chunk3/pallas_call | solution.py:155
  120.0 3.2 %collective-permute-start.16 = (f32[256,256]{1,0:T(8,128)S(1)}, f32[256,256]{1,0:T(8,128)S(1)}, u32[]{:S(2)}, u32[]{:S(2)}) collective-permute-start(f32[256,256]{1,0:T(8,128)S(1)} %get-tuple-element.95), channel_id=1, source_target_pairs={{0,5},{1,4},{2,7},{3,6},{4,9},{5,8},{6,11},{7,10},{8,13},{9,12},{1... | collective-permute-start | bytes 786440 | tf_op jit(solution)/shard_map/ppermute | solution.py:173
  127.2 2.6 %collective-permute-done.17.refs_7_ = f32[256,256]{1,0:T(8,128)S(1)} collective-permute-done((f32[256,256]{1,0:T(8,128)S(1)}, f32[256,256]{1,0:T(8,128)S(1)}, u32[]{:S(2)}, u32[]{:S(2)}) %collective-permute-start.17) | collective-permute-done | bytes 262176 | tf_op jit(solution)/shard_map/ppermute | solution.py:173
  132.0 3.0 %collective-permute-done.16.refs_7_ = f32[256,256]{1,0:T(8,128)S(1)} collective-permute-done((f32[256,256]{1,0:T(8,128)S(1)}, f32[256,256]{1,0:T(8,128)S(1)}, u32[]{:S(2)}, u32[]{:S(2)}) %collective-permute-start.16) | collective-permute-done | bytes 262176 | tf_op jit(solution)/shard_map/ppermute | solution.py:173
  135.0 3.7 %sub5_chunk3.1 = (f32[1024,256]{1,0:T(8,128)}, f32[1024,256]{1,0:T(8,128)}, f32[512,256]{1,0:T(8,128)}, f32[512,256]{1,0:T(8,128)}) custom-call(s32[6,16]{1,0:T(8,128)S(1)} %copy-done.5, s32[6,16]{1,0:T(8,128)S(1)} %copy-done.6, s32[6,8]{1,0:T(8,128)S(1)} %copy-done.7, s32[6,8]{1,0:T(8,128)S(1)} %copy-done.8, s32[6,16,128]{2,1,0:T(8,128)S(1)} %copy-done, ...), custom_call_target="tpu_custom_call" | custom-call | flops 335544320 | bytes 6291456 | tf_op jit(solution)/shard_map/sub5_chunk3/pallas_call | solution.py:155
  (60 shorter events, 52.3 us)
Async XLA Ops:
  2.2 1.2 copy-start.2
  3.5 1.0 copy-start.3
  4.5 1.0 copy-start.4
  10.2 16.4 %collective-permute-start.3 = (f32[256,256]{1,0:T(8,128)S(1)}, f32[256,256]{1,0:T(8,128)S(1)}, u32[]{:S(2)}, u32[]{:S(2)}) collective-permute-start(f32[256,256]{1,0:T(8,128)S(1)} %get-tuple-element.62), channel_id=1, source_target_pairs={{0,4},{1,5},{2,6},{3,7},{4,8},{5,9},{6,10},{7,11},{8,12},{9,13},{1... | collective-permute-start | bytes 786440 | tf_op jit(solution)/shard_map/ppermute | solution.py:173
  16.1 15.4 %collective-permute-start.2 = (f32[256,256]{1,0:T(8,128)S(1)}, f32[256,256]{1,0:T(8,128)S(1)}, u32[]{:S(2)}, u32[]{:S(2)}) collective-permute-start(f32[256,256]{1,0:T(8,128)S(1)} %get-tuple-element.61), channel_id=1, source_target_pairs={{0,4},{1,5},{2,6},{3,7},{4,8},{5,9},{6,10},{7,11},{8,12},{9,13},{1... | collective-permute-start | bytes 786440 | tf_op jit(solution)/shard_map/ppermute | solution.py:173
  17.6 6.2 %copy-start.9 = (f32[1024,256]{1,0:T(8,128)S(1)}, f32[1024,256]{1,0:T(8,128)}, u32[]{:S(2)}) copy-start(f32[1024,256]{1,0:T(8,128)} %refs_10_.1) | copy-start | bytes 3145732
  19.7 18.9 %collective-permute-start.1 = (f32[256,256]{1,0:T(8,128)S(1)}, f32[256,256]{1,0:T(8,128)S(1)}, u32[]{:S(2)}, u32[]{:S(2)}) collective-permute-start(f32[256,256]{1,0:T(8,128)S(1)} %get-tuple-element.60), channel_id=1, source_target_pairs={{0,5},{1,4},{2,7},{3,6},{4,9},{5,8},{6,11},{7,10},{8,13},{9,12},{1... | collective-permute-start | bytes 786440 | tf_op jit(solution)/shard_map/ppermute | solution.py:173
  26.0 17.9 %collective-permute-start = (f32[256,256]{1,0:T(8,128)S(1)}, f32[256,256]{1,0:T(8,128)S(1)}, u32[]{:S(2)}, u32[]{:S(2)}) collective-permute-start(f32[256,256]{1,0:T(8,128)S(1)} %get-tuple-element.59), channel_id=1, source_target_pairs={{0,5},{1,4},{2,7},{3,6},{4,9},{5,8},{6,11},{7,10},{8,13},{9,12},{1... | collective-permute-start | bytes 786440 | tf_op jit(solution)/shard_map/ppermute | solution.py:173
  28.5 19.7 %collective-permute-start.7 = (f32[256,256]{1,0:T(8,128)S(1)}, f32[256,256]{1,0:T(8,128)S(1)}, u32[]{:S(2)}, u32[]{:S(2)}) collective-permute-start(f32[256,256]{1,0:T(8,128)S(1)} %get-tuple-element.71), channel_id=1, source_target_pairs={{0,4},{1,5},{2,6},{3,7},{4,8},{5,9},{6,10},{7,11},{8,12},{9,13},{1... | collective-permute-start | bytes 786440 | tf_op jit(solution)/shard_map/ppermute | solution.py:173
  33.6 20.2 %collective-permute-start.6 = (f32[256,256]{1,0:T(8,128)S(1)}, f32[256,256]{1,0:T(8,128)S(1)}, u32[]{:S(2)}, u32[]{:S(2)}) collective-permute-start(f32[256,256]{1,0:T(8,128)S(1)} %get-tuple-element.70), channel_id=1, source_target_pairs={{0,4},{1,5},{2,6},{3,7},{4,8},{5,9},{6,10},{7,11},{8,12},{9,13},{1... | collective-permute-start | bytes 786440 | tf_op jit(solution)/shard_map/ppermute | solution.py:173
  40.7 24.4 %collective-permute-start.5 = (f32[256,256]{1,0:T(8,128)S(1)}, f32[256,256]{1,0:T(8,128)S(1)}, u32[]{:S(2)}, u32[]{:S(2)}) collective-permute-start(f32[256,256]{1,0:T(8,128)S(1)} %get-tuple-element.69), channel_id=1, source_target_pairs={{0,6},{1,7},{2,4},{3,5},{4,10},{5,11},{6,8},{7,9},{8,14},{9,15},{1... | collective-permute-start | bytes 786440 | tf_op jit(solution)/shard_map/ppermute | solution.py:173
  46.0 25.2 %collective-permute-start.4 = (f32[256,256]{1,0:T(8,128)S(1)}, f32[256,256]{1,0:T(8,128)S(1)}, u32[]{:S(2)}, u32[]{:S(2)}) collective-permute-start(f32[256,256]{1,0:T(8,128)S(1)} %get-tuple-element.68), channel_id=1, source_target_pairs={{0,6},{1,7},{2,4},{3,5},{4,10},{5,11},{6,8},{7,9},{8,14},{9,15},{1... | collective-permute-start | bytes 786440 | tf_op jit(solution)/shard_map/ppermute | solution.py:173
  50.0 26.8 %collective-permute-start.11 = (f32[256,256]{1,0:T(8,128)S(1)}, f32[256,256]{1,0:T(8,128)S(1)}, u32[]{:S(2)}, u32[]{:S(2)}) collective-permute-start(f32[256,256]{1,0:T(8,128)S(1)} %get-tuple-element.80), channel_id=1, source_target_pairs={{0,4},{1,5},{2,6},{3,7},{4,8},{5,9},{6,10},{7,11},{8,12},{9,13},{1... | collective-permute-start | bytes 786440 | tf_op jit(solution)/shard_map/ppermute | solution.py:173
  55.9 25.2 %collective-permute-start.10 = (f32[256,256]{1,0:T(8,128)S(1)}, f32[256,256]{1,0:T(8,128)S(1)}, u32[]{:S(2)}, u32[]{:S(2)}) collective-permute-start(f32[256,256]{1,0:T(8,128)S(1)} %get-tuple-element.79), channel_id=1, source_target_pairs={{0,4},{1,5},{2,6},{3,7},{4,8},{5,9},{6,10},{7,11},{8,12},{9,13},{1... | collective-permute-start | bytes 786440 | tf_op jit(solution)/shard_map/ppermute | solution.py:173
  67.2 18.1 %collective-permute-start.9 = (f32[256,256]{1,0:T(8,128)S(1)}, f32[256,256]{1,0:T(8,128)S(1)}, u32[]{:S(2)}, u32[]{:S(2)}) collective-permute-start(f32[256,256]{1,0:T(8,128)S(1)} %get-tuple-element.78), channel_id=1, source_target_pairs={{0,5},{1,4},{2,7},{3,6},{4,9},{5,8},{6,11},{7,10},{8,13},{9,12},{1... | collective-permute-start | bytes 786440 | tf_op jit(solution)/shard_map/ppermute | solution.py:173
  73.4 17.1 %collective-permute-start.8 = (f32[256,256]{1,0:T(8,128)S(1)}, f32[256,256]{1,0:T(8,128)S(1)}, u32[]{:S(2)}, u32[]{:S(2)}) collective-permute-start(f32[256,256]{1,0:T(8,128)S(1)} %get-tuple-element.77), channel_id=1, source_target_pairs={{0,5},{1,4},{2,7},{3,6},{4,9},{5,8},{6,11},{7,10},{8,13},{9,12},{1... | collective-permute-start | bytes 786440 | tf_op jit(solution)/shard_map/ppermute | solution.py:173
  78.7 15.3 %collective-permute-start.15 = (f32[256,256]{1,0:T(8,128)S(1)}, f32[256,256]{1,0:T(8,128)S(1)}, u32[]{:S(2)}, u32[]{:S(2)}) collective-permute-start(f32[256,256]{1,0:T(8,128)S(1)} %get-tuple-element.89), channel_id=1, source_target_pairs={{0,4},{1,5},{2,6},{3,7},{4,8},{5,9},{6,10},{7,11},{8,12},{9,13},{1... | collective-permute-start | bytes 786440 | tf_op jit(solution)/shard_map/ppermute | solution.py:173
  83.3 16.4 %collective-permute-start.14 = (f32[256,256]{1,0:T(8,128)S(1)}, f32[256,256]{1,0:T(8,128)S(1)}, u32[]{:S(2)}, u32[]{:S(2)}) collective-permute-start(f32[256,256]{1,0:T(8,128)S(1)} %get-tuple-element.88), channel_id=1, source_target_pairs={{0,4},{1,5},{2,6},{3,7},{4,8},{5,9},{6,10},{7,11},{8,12},{9,13},{1... | collective-permute-start | bytes 786440 | tf_op jit(solution)/shard_map/ppermute | solution.py:173
  87.5 23.6 %collective-permute-start.13 = (f32[256,256]{1,0:T(8,128)S(1)}, f32[256,256]{1,0:T(8,128)S(1)}, u32[]{:S(2)}, u32[]{:S(2)}) collective-permute-start(f32[256,256]{1,0:T(8,128)S(1)} %get-tuple-element.87), channel_id=1, source_target_pairs={{0,6},{1,7},{2,4},{3,5},{4,10},{5,11},{6,8},{7,9},{8,14},{9,15},{1... | collective-permute-start | bytes 786440 | tf_op jit(solution)/shard_map/ppermute | solution.py:173
  92.7 25.2 %collective-permute-start.12 = (f32[256,256]{1,0:T(8,128)S(1)}, f32[256,256]{1,0:T(8,128)S(1)}, u32[]{:S(2)}, u32[]{:S(2)}) collective-permute-start(f32[256,256]{1,0:T(8,128)S(1)} %get-tuple-element.86), channel_id=1, source_target_pairs={{0,6},{1,7},{2,4},{3,5},{4,10},{5,11},{6,8},{7,9},{8,14},{9,15},{1... | collective-permute-start | bytes 786440 | tf_op jit(solution)/shard_map/ppermute | solution.py:173
  95.9 27.3 %collective-permute-start.19 = (f32[256,256]{1,0:T(8,128)S(1)}, f32[256,256]{1,0:T(8,128)S(1)}, u32[]{:S(2)}, u32[]{:S(2)}) collective-permute-start(f32[256,256]{1,0:T(8,128)S(1)} %get-tuple-element.98), channel_id=1, source_target_pairs={{0,4},{1,5},{2,6},{3,7},{4,8},{5,9},{6,10},{7,11},{8,12},{9,13},{1... | collective-permute-start | bytes 786440 | tf_op jit(solution)/shard_map/ppermute | solution.py:173
  101.7 23.3 %collective-permute-start.18 = (f32[256,256]{1,0:T(8,128)S(1)}, f32[256,256]{1,0:T(8,128)S(1)}, u32[]{:S(2)}, u32[]{:S(2)}) collective-permute-start(f32[256,256]{1,0:T(8,128)S(1)} %get-tuple-element.97), channel_id=1, source_target_pairs={{0,4},{1,5},{2,6},{3,7},{4,8},{5,9},{6,10},{7,11},{8,12},{9,13},{1... | collective-permute-start | bytes 786440 | tf_op jit(solution)/shard_map/ppermute | solution.py:173
  113.2 16.7 %collective-permute-start.17 = (f32[256,256]{1,0:T(8,128)S(1)}, f32[256,256]{1,0:T(8,128)S(1)}, u32[]{:S(2)}, u32[]{:S(2)}) collective-permute-start(f32[256,256]{1,0:T(8,128)S(1)} %get-tuple-element.96), channel_id=1, source_target_pairs={{0,5},{1,4},{2,7},{3,6},{4,9},{5,8},{6,11},{7,10},{8,13},{9,12},{1... | collective-permute-start | bytes 786440 | tf_op jit(solution)/shard_map/ppermute | solution.py:173
  120.0 15.0 %collective-permute-start.16 = (f32[256,256]{1,0:T(8,128)S(1)}, f32[256,256]{1,0:T(8,128)S(1)}, u32[]{:S(2)}, u32[]{:S(2)}) collective-permute-start(f32[256,256]{1,0:T(8,128)S(1)} %get-tuple-element.95), channel_id=1, source_target_pairs={{0,5},{1,4},{2,7},{3,6},{4,9},{5,8},{6,11},{7,10},{8,13},{9,12},{1... | collective-permute-start | bytes 786440 | tf_op jit(solution)/shard_map/ppermute | solution.py:173
  (6 other events, 4.3 us)

commit v2 on v1

v2 whole, which is shorter than its diff:
```python
import functools

import jax
import jax.numpy as jnp
from jax import lax
from jax.experimental import pallas as pl
from jax.experimental.pallas import tpu as pltpu
from jax.sharding import PartitionSpec as P

SUBS = 6
TILE = 128
CHUNK = 128
STEP = 256
LEARN_RATE = 0.05
DECAY = 0.02
NEG_WEIGHT = 0.25
AXES = ("blk", "xor")
ORDERS = ((0, 2, 1, 3),) * SUBS
BF = jnp.bfloat16
F32 = jnp.float32
VMEM_SPEC = pl.BlockSpec(memory_space=pltpu.VMEM)
HBM_SPEC = pl.BlockSpec(memory_space=pltpu.HBM)
PARAMS = pltpu.CompilerParams(vmem_limit_bytes=24 * 1024 * 1024)


def down(row):
    count = row.shape[1]
    values = jnp.broadcast_to(row.astype(F32), (count, count))
    here = lax.broadcasted_iota(jnp.int32, (count, count), 0) == lax.broadcasted_iota(
        jnp.int32, (count, count), 1
    )
    column = jnp.sum(jnp.where(here, values, 0.0), axis=1, keepdims=True)
    return jnp.broadcast_to(column, (count, TILE))


def spread(tile, live, first, count):
    groups = [jnp.where(tile == first + n, live, 0.0) for n in range(count)]
    return groups[0] if count == 1 else jnp.concatenate(groups, axis=1)


def pair_factors(s, su, si, nu, ni, row_live, col_live, user_tiles, chunks):
    rows = row_live[s].astype(F32)
    cols = col_live[s].astype(F32)
    ones = jnp.ones((nu.shape[1], TILE), F32)
    at = slice(s, s + 1)
    left = jnp.concatenate(
        [
            spread(down(su[at, :]), rows, 0, user_tiles),
            spread(down(nu[at, :]), ones, 0, user_tiles),
        ],
        axis=0,
    )
    count = CHUNK // TILE
    item, sampled_item = down(si[at, :]), down(ni[at, :])
    rights = []
    for chunk in range(chunks):
        seen = spread(item, cols, chunk * count, count)
        sampled = spread(sampled_item, ones, chunk * count, count)
        rights.append(
            jnp.concatenate(
                [
                    jnp.concatenate([seen, seen], axis=1),
                    jnp.concatenate([NEG_WEIGHT * sampled, jnp.zeros_like(sampled)], axis=1),
                ],
                axis=0,
            ).astype(BF)
        )
    return left.T.astype(BF), rights


def adagrad(factor, accum, grad):
    accum = accum + grad * grad
    return factor - LEARN_RATE * grad * lax.rsqrt(accum), accum


def dot(a, b, contract):
    return lax.dot_general(a, b, ((contract[:1], contract[1:]), ((), ())), preferred_element_type=F32)


def chunk_terms(users, left, right, factor, each):
    item_bf = factor.astype(BF)
    grad_items = DECAY * factor
    for start in range(0, users.shape[0], STEP):
        at = slice(start, start + STEP)
        user = users[at, :]
        user_bf = user.astype(BF)
        scores = dot(user_bf, item_bf, (1, 1))
        both = dot(left[at, :], right, (1, 0))
        err = (both[:, :CHUNK] * scores - both[:, CHUNK:]).astype(BF)
        each(at, user, dot(err, item_bf, (1, 0)))
        grad_items += dot(err, user_bf, (0, 0))
    return grad_items


def store_state(state, factor, accum):
    state[:CHUNK, :] = factor
    state[CHUNK:, :] = accum


def first_kernel(chunks, *refs):
    args, outs, scratch = refs[:10], refs[10 : 10 + 5 + chunks], refs[10 + 5 + chunks :]
    users_hbm, user_accum_hbm, items_hbm, item_accum_hbm = args[:4]
    users, user_accum, left_out, right_out, grad_out, *states = outs
    small, (raw, sems) = scratch[:6], scratch[6:]
    copies = [pltpu.make_async_copy(src, dst, sems.at[n]) for n, (src, dst) in enumerate(zip(args[4:], small))]
    copies.append(pltpu.make_async_copy(users_hbm, users, sems.at[6]))
    at = 7
    for chunk in range(chunks):
        target = raw if chunk == 0 else states[chunk]
        rows = pl.ds(chunk * CHUNK, CHUNK)
        for part, source in enumerate((items_hbm, item_accum_hbm)):
            copies.append(
                pltpu.make_async_copy(
                    source.at[rows], target.at[pl.ds(part * CHUNK, CHUNK)], sems.at[at]
                )
            )
            at += 1
    copies.append(pltpu.make_async_copy(user_accum_hbm, user_accum, sems.at[at]))
    for copy in copies:
        copy.start()
    for copy in copies[:6]:
        copy.wait()
    su, si, row_live, col_live, nu, ni = small
    left, rights = pair_factors(0, su, si, nu, ni, row_live, col_live, users.shape[0] // TILE, chunks)
    left_out[...] = left
    for chunk in range(chunks):
        right_out[chunk] = rights[chunk]
    for copy in copies[6:9]:
        copy.wait()
    factor, accum = raw[:CHUNK, :], raw[CHUNK:, :]

    def each(at, user, grad):
        grad_out[at, :] = grad

    grad_items = chunk_terms(users, left_out, rights[0], factor, each)
    store_state(states[0], *adagrad(factor, accum, grad_items))
    for copy in copies[9:]:
        copy.wait()


def run_first(args):
    users, user_accum, items, item_accum, *small = args
    width = users.shape[1]
    chunks = items.shape[0] // CHUNK
    terms = small[0].shape[1] + small[4].shape[1]
    sds = jax.ShapeDtypeStruct
    out = [
        sds(users.shape, F32),
        sds(users.shape, F32),
        sds((users.shape[0], terms), BF),
        sds((chunks, terms, 2 * CHUNK), BF),
        sds(users.shape, F32),
    ] + [sds((2 * CHUNK, width), F32)] * chunks
    return pl.pallas_call(
        functools.partial(first_kernel, chunks),
        out_shape=out,
        in_specs=[HBM_SPEC] * len(args),
        out_specs=[VMEM_SPEC] * len(out),
        scratch_shapes=[pltpu.VMEM(x.shape, x.dtype) for x in small]
        + [pltpu.VMEM((2 * CHUNK, width), F32), pltpu.SemaphoreType.DMA((8 + 2 * chunks,))],
        compiler_params=PARAMS,
        name="first_chunk",
    )(*(pltpu.with_memory_space_constraint(x, pltpu.HBM) for x in args))


def factors_kernel(user_tiles, chunks, *refs):
    args, (left_out, right_out), (*small, sems) = refs[:6], refs[7:9], refs[9:]
    copies = [pltpu.make_async_copy(src, dst, sems.at[n]) for n, (src, dst) in enumerate(zip(args, small))]
    for copy in copies:
        copy.start()
    for copy in copies:
        copy.wait()
    su, si, row_live, col_live, nu, ni = small
    for s in range(1, SUBS):
        left, rights = pair_factors(s, su, si, nu, ni, row_live, col_live, user_tiles, chunks)
        left_out[s - 1] = left
        for chunk in range(chunks):
            right_out[s - 1, chunk] = rights[chunk]


def run_factors(small, user_rows, chunks, after):
    terms = small[0].shape[1] + small[4].shape[1]
    pinned = [pltpu.with_memory_space_constraint(x, pltpu.HBM) for x in small]
    return pl.pallas_call(
        functools.partial(factors_kernel, user_rows // TILE, chunks),
        out_shape=[
            jax.ShapeDtypeStruct((SUBS - 1, user_rows, terms), BF),
            jax.ShapeDtypeStruct((SUBS - 1, chunks, terms, 2 * CHUNK), BF),
        ],
        in_specs=[HBM_SPEC] * 6 + [pl.BlockSpec(memory_space=pl.ANY)],
        out_specs=[VMEM_SPEC] * 2,
        scratch_shapes=[pltpu.VMEM(x.shape, x.dtype) for x in small] + [pltpu.SemaphoreType.DMA((6,))],
        compiler_params=PARAMS,
        name="pair_factors",
    )(*pinned, after)


def chunk_kernel(s, chunk, first, final, chunks, *refs):
    users, left, right, state, *refs = refs
    if s > 0:
        left, right = left.at[s - 1], right.at[s - 1]
    right = right[chunk]
    if not first:
        grad_in, *refs = refs
    if final:
        user_accum, *refs = refs
    end = final and s == SUBS - 1
    if end:
        others, refs = refs[: chunks - 1], refs[chunks - 1 :]
        outs, (users_out, user_accum_out, state_out, sems) = refs[:4], refs[4:]
        copies = []

        def send(src, dst):
            copies.append(pltpu.make_async_copy(src, dst, sems.at[len(copies)]))
            copies[-1].start()

        for n, other in zip([n for n in range(chunks) if n != chunk], others):
            for part in range(2):
                send(other.at[pl.ds(part * CHUNK, CHUNK)], outs[2 + part].at[pl.ds(n * CHUNK, CHUNK)])
    elif final:
        users_out, user_accum_out, state_out = refs
    else:
        grad_out, state_out = refs
    factor, accum = state[:CHUNK, :], state[CHUNK:, :]

    def each(at, user, grad):
        if not first:
            grad += grad_in[at, :]
        if final:
            grad += DECAY * user
            users_out[at, :], user_accum_out[at, :] = adagrad(user, user_accum[at, :], grad)
            if end:
                rows = pl.ds(at.start, STEP)
                send(users_out.at[rows], outs[0].at[rows])
                send(user_accum_out.at[rows], outs[1].at[rows])
        else:
            grad_out[at, :] = grad

    grad_items = chunk_terms(users, left, right, factor, each)
    store_state(state_out, *adagrad(factor, accum, grad_items))
    if end:
        for part in range(2):
            send(state_out.at[pl.ds(part * CHUNK, CHUNK)], outs[2 + part].at[pl.ds(chunk * CHUNK, CHUNK)])
        for copy in copies:
            copy.wait()


def run_chunk(s, chunk, first, final, chunks, users, factors, state, extra):
    width = users.shape[1]
    user_shape = jax.ShapeDtypeStruct(users.shape, F32)
    state_shape = jax.ShapeDtypeStruct((2 * CHUNK, width), F32)
    end = final and s == SUBS - 1
    out = [user_shape] * (2 if final else 1)
    out += [jax.ShapeDtypeStruct((chunks * CHUNK, width), F32)] * 2 if end else [state_shape]
    scratch = []
    if end:
        copies = 2 * chunks + 2 * (users.shape[0] // STEP)
        scratch = [pltpu.VMEM(x.shape, F32) for x in (users, users, state)]
        scratch.append(pltpu.SemaphoreType.DMA((copies,)))
    operands = [users, *factors, state, *extra]
    return pl.pallas_call(
        functools.partial(chunk_kernel, s, chunk, first, final, chunks),
        out_shape=out,
        in_specs=[VMEM_SPEC] * len(operands),
        out_specs=[HBM_SPEC if end else VMEM_SPEC] * len(out),
        scratch_shapes=scratch,
        compiler_params=PARAMS,
        cost_estimate=pl.CostEstimate(
            flops=10 * users.shape[0] * CHUNK * width, bytes_accessed=6 * 1024 * 1024, transcendentals=0
        ),
        name=f"sub{s}_chunk{chunk}",
    )(*operands)


def move(state, s, second_half):
    blks, xors = lax.axis_size("blk"), lax.axis_size("xor")
    flip = 2 ** (s % 2) if second_half else 0
    pairs = [
        (b * xors + x, ((b + 1) % blks) * xors + (x ^ flip)) for b in range(blks) for x in range(xors)
    ]
    return lax.ppermute(state, AXES, pairs)


def per_device(*args):
    chunks = args[2].shape[0] // CHUNK
    users, user_accum, left, right, grad, *states = run_first(args)
    factors = (left, right)
    grad = [grad]
    for s, order in enumerate(ORDERS):
        moved = [None] * chunks
        for n in order:
            first, final = n == order[0], n == order[-1]
            extra = (*grad, user_accum) if final else grad
            end = s == SUBS - 1
            if final and end:
                extra = (*extra, *(m for m in moved if m is not None))
                return tuple(run_chunk(s, n, first, final, chunks, users, factors, states[n], extra))
            state = states[n]
            if s > 0 or not first:
                *grad, state = run_chunk(s, n, first, final, chunks, users, factors, state, extra)
            moved[n] = state if end else move(state, s, n >= chunks // 2)
        users, user_accum = grad
        grad = []
        states = moved
        if s == 0:
            factors = run_factors(args[4:], users.shape[0], chunks, users)


def solution(mesh):
    rows = P(AXES, None)
    placed = (rows,) * 4 + (P(None, AXES),) * 2 + (P(None, AXES, None),) * 2 + (P(None, AXES),) * 2
    return jax.shard_map(
        per_device, mesh=mesh, in_specs=placed, out_specs=(rows,) * 4, check_vma=False
    )
```

time: 139 us -> 130 us (0.935)
  waiting for transfers between devices: 39.6 us -> 66.3 us
  Pallas kernels: 51 us -> 29 us
  local copies, waits for them, and re-layouts: 7.64 us -> 0 us
  starting transfers between devices: 39.6 us -> 33.3 us
    ppermute x20, waiting for transfers between devices: 39.6 us -> 66.3 us  [move(): return lax.ppermute(state, AXES, pairs)]
    pallas_call x24 -> x25, Pallas kernels: 51 us -> 29 us  [the longest x23 25.1 us: run_chunk(): pl.pallas_call(functools.partial(chunk_kernel, s, chunk, first, final, ch...]
    unnamed x20 -> x0, local copies, waits for them, and re-layouts: 7.64 us -> none
    ppermute x20, starting transfers between devices: 39.6 us -> 33.3 us  [move(): return lax.ppermute(state, AXES, pairs)]
  transfers between devices with their start and end apart: 20 -> 20, of which waited for: 10 -> 15; matrix products, arithmetic and copies ran while one was open for 0% -> 0% of each run, Pallas kernels for 33% -> 19%
where the time goes in v2:
time: 130 us
  waiting for transfers between devices  66.3 us (51%)
  starting transfers between devices  33.3 us (26%)
  Pallas kernels  29 us (22%)
    ppermute x20, waiting for transfers between devices, move(): return lax.ppermute(state, AXES, pairs)  66.3 us
    ppermute x20, starting transfers between devices, move(): return lax.ppermute(state, AXES, pairs)  33.3 us
    pallas_call x23, Pallas kernels, run_chunk(): pl.pallas_call(functools.partial(chunk_kernel, s, chunk, first, final, ch...  25.1 us
  transfers between devices with their start and end apart: 20, of which 15 were waited for; matrix products, arithmetic and copies ran while one was open for 0% of the time, Pallas kernels for 19%

profile of v2, /device:TPU:1, one launch (start us, length us, event | category | flops | bytes accessed | tf_op | source)
XLA Modules:
  0.0 129.8 jit_solution(17435471249449881697)
XLA Ops:
  0.6 2.6 %first_chunk.1 = (f32[1024,256]{1,0:T(8,128)S(1)}, f32[1024,256]{1,0:T(8,128)S(1)}, bf16[1024,24]{1,0:T(8,128)(2,1)S(1)}, bf16[4,24,256]{2,1,0:T(8,128)(2,1)S(1)...) custom-call(f32[1024,256]{1,0:T(8,128)} %refs_0_.2, ...), custom_call_target="tpu_custom_call" | custom-call | tf_op jit(solution)/shard_map/first_chunk/pallas_call | solution.py:154
  3.2 3.8 %collective-permute-start.3 = (f32[256,256]{1,0:T(8,128)S(1)}, f32[256,256]{1,0:T(8,128)S(1)}, u32[]{:S(2)}, u32[]{:S(2)}) collective-permute-start(f32[256,256]{1,0:T(8,128)S(1)} %get-tuple-element.80), channel_id=1, source_target_pairs={{0,4},{1,5},{2,6},{3,7},{4,8},{5,9},{6,10},{7,11},{8,12},{9,13},{1... | collective-permute-start | bytes 786440 | tf_op jit(solution)/shard_map/ppermute | solution.py:281
  8.1 2.3 %collective-permute-start.2 = (f32[256,256]{1,0:T(8,128)S(1)}, f32[256,256]{1,0:T(8,128)S(1)}, u32[]{:S(2)}, u32[]{:S(2)}) collective-permute-start(f32[256,256]{1,0:T(8,128)S(1)} %get-tuple-element.79), channel_id=1, source_target_pairs={{0,5},{1,4},{2,7},{3,6},{4,9},{5,8},{6,11},{7,10},{8,13},{9,12},{1... | collective-permute-start | bytes 786440 | tf_op jit(solution)/shard_map/ppermute | solution.py:281
  11.5 3.0 %collective-permute-start.1 = (f32[256,256]{1,0:T(8,128)S(1)}, f32[256,256]{1,0:T(8,128)S(1)}, u32[]{:S(2)}, u32[]{:S(2)}) collective-permute-start(f32[256,256]{1,0:T(8,128)S(1)} %get-tuple-element.78), channel_id=1, source_target_pairs={{0,4},{1,5},{2,6},{3,7},{4,8},{5,9},{6,10},{7,11},{8,12},{9,13},{1... | collective-permute-start | bytes 786440 | tf_op jit(solution)/shard_map/ppermute | solution.py:281
  19.8 2.4 %collective-permute-start.7 = (f32[256,256]{1,0:T(8,128)S(1)}, f32[256,256]{1,0:T(8,128)S(1)}, u32[]{:S(2)}, u32[]{:S(2)}) collective-permute-start(f32[256,256]{1,0:T(8,128)S(1)} %get-tuple-element.89), channel_id=1, source_target_pairs={{0,4},{1,5},{2,6},{3,7},{4,8},{5,9},{6,10},{7,11},{8,12},{9,13},{1... | collective-permute-start | bytes 786440 | tf_op jit(solution)/shard_map/ppermute | solution.py:281
  22.2 3.6 %collective-permute-done.2.refs_3_ = f32[256,256]{1,0:T(8,128)S(1)} collective-permute-done((f32[256,256]{1,0:T(8,128)S(1)}, f32[256,256]{1,0:T(8,128)S(1)}, u32[]{:S(2)}, u32[]{:S(2)}) %collective-permute-start.2) | collective-permute-done | bytes 262176 | tf_op jit(solution)/shard_map/ppermute | solution.py:281
  26.9 3.1 %collective-permute-done.1.refs_3_ = f32[256,256]{1,0:T(8,128)S(1)} collective-permute-done((f32[256,256]{1,0:T(8,128)S(1)}, f32[256,256]{1,0:T(8,128)S(1)}, u32[]{:S(2)}, u32[]{:S(2)}) %collective-permute-start.1) | collective-permute-done | bytes 262176 | tf_op jit(solution)/shard_map/ppermute | solution.py:281
  31.1 5.8 %collective-permute-done.refs_3_ = f32[256,256]{1,0:T(8,128)S(1)} collective-permute-done((f32[256,256]{1,0:T(8,128)S(1)}, f32[256,256]{1,0:T(8,128)S(1)}, u32[]{:S(2)}, u32[]{:S(2)}) %collective-permute-start) | collective-permute-done | bytes 262176 | tf_op jit(solution)/shard_map/ppermute | solution.py:281
  38.1 3.1 %collective-permute-done.7.refs_3_ = f32[256,256]{1,0:T(8,128)S(1)} collective-permute-done((f32[256,256]{1,0:T(8,128)S(1)}, f32[256,256]{1,0:T(8,128)S(1)}, u32[]{:S(2)}, u32[]{:S(2)}) %collective-permute-start.7) | collective-permute-done | bytes 262176 | tf_op jit(solution)/shard_map/ppermute | solution.py:281
  42.5 10.1 %collective-permute-done.6.refs_3_ = f32[256,256]{1,0:T(8,128)S(1)} collective-permute-done((f32[256,256]{1,0:T(8,128)S(1)}, f32[256,256]{1,0:T(8,128)S(1)}, u32[]{:S(2)}, u32[]{:S(2)}) %collective-permute-start.6) | collective-permute-done | bytes 262176 | tf_op jit(solution)/shard_map/ppermute | solution.py:281
  53.7 3.8 %collective-permute-start.10 = (f32[256,256]{1,0:T(8,128)S(1)}, f32[256,256]{1,0:T(8,128)S(1)}, u32[]{:S(2)}, u32[]{:S(2)}) collective-permute-start(f32[256,256]{1,0:T(8,128)S(1)} %get-tuple-element.97), channel_id=1, source_target_pairs={{0,5},{1,4},{2,7},{3,6},{4,9},{5,8},{6,11},{7,10},{8,13},{9,12},{1... | collective-permute-start | bytes 786440 | tf_op jit(solution)/shard_map/ppermute | solution.py:281
  58.6 2.5 %collective-permute-start.9 = (f32[256,256]{1,0:T(8,128)S(1)}, f32[256,256]{1,0:T(8,128)S(1)}, u32[]{:S(2)}, u32[]{:S(2)}) collective-permute-start(f32[256,256]{1,0:T(8,128)S(1)} %get-tuple-element.96), channel_id=1, source_target_pairs={{0,4},{1,5},{2,6},{3,7},{4,8},{5,9},{6,10},{7,11},{8,12},{9,13},{1... | collective-permute-start | bytes 786440 | tf_op jit(solution)/shard_map/ppermute | solution.py:281
  62.2 2.2 %collective-permute-start.8 = (f32[256,256]{1,0:T(8,128)S(1)}, f32[256,256]{1,0:T(8,128)S(1)}, u32[]{:S(2)}, u32[]{:S(2)}) collective-permute-start(f32[256,256]{1,0:T(8,128)S(1)} %get-tuple-element.95), channel_id=1, source_target_pairs={{0,5},{1,4},{2,7},{3,6},{4,9},{5,8},{6,11},{7,10},{8,13},{9,12},{1... | collective-permute-start | bytes 786440 | tf_op jit(solution)/shard_map/ppermute | solution.py:281
  65.5 2.3 %collective-permute-start.15 = (f32[256,256]{1,0:T(8,128)S(1)}, f32[256,256]{1,0:T(8,128)S(1)}, u32[]{:S(2)}, u32[]{:S(2)}) collective-permute-start(f32[256,256]{1,0:T(8,128)S(1)} %get-tuple-element.107), channel_id=1, source_target_pairs={{0,4},{1,5},{2,6},{3,7},{4,8},{5,9},{6,10},{7,11},{8,12},{9,13},{1... | collective-permute-start | bytes 786440 | tf_op jit(solution)/shard_map/ppermute | solution.py:281
  67.8 3.6 %collective-permute-done.10.refs_3_ = f32[256,256]{1,0:T(8,128)S(1)} collective-permute-done((f32[256,256]{1,0:T(8,128)S(1)}, f32[256,256]{1,0:T(8,128)S(1)}, u32[]{:S(2)}, u32[]{:S(2)}) %collective-permute-start.10) | collective-permute-done | bytes 262176 | tf_op jit(solution)/shard_map/ppermute | solution.py:281
  72.6 3.1 %collective-permute-done.9.refs_3_ = f32[256,256]{1,0:T(8,128)S(1)} collective-permute-done((f32[256,256]{1,0:T(8,128)S(1)}, f32[256,256]{1,0:T(8,128)S(1)}, u32[]{:S(2)}, u32[]{:S(2)}) %collective-permute-start.9) | collective-permute-done | bytes 262176 | tf_op jit(solution)/shard_map/ppermute | solution.py:281
  76.8 5.9 %collective-permute-done.8.refs_3_ = f32[256,256]{1,0:T(8,128)S(1)} collective-permute-done((f32[256,256]{1,0:T(8,128)S(1)}, f32[256,256]{1,0:T(8,128)S(1)}, u32[]{:S(2)}, u32[]{:S(2)}) %collective-permute-start.8) | collective-permute-done | bytes 262176 | tf_op jit(solution)/shard_map/ppermute | solution.py:281
  83.8 3.1 %collective-permute-done.15.refs_3_ = f32[256,256]{1,0:T(8,128)S(1)} collective-permute-done((f32[256,256]{1,0:T(8,128)S(1)}, f32[256,256]{1,0:T(8,128)S(1)}, u32[]{:S(2)}, u32[]{:S(2)}) %collective-permute-start.15) | collective-permute-done | bytes 262176 | tf_op jit(solution)/shard_map/ppermute | solution.py:281
  88.1 9.5 %collective-permute-done.14.refs_3_ = f32[256,256]{1,0:T(8,128)S(1)} collective-permute-done((f32[256,256]{1,0:T(8,128)S(1)}, f32[256,256]{1,0:T(8,128)S(1)}, u32[]{:S(2)}, u32[]{:S(2)}) %collective-permute-start.14) | collective-permute-done | bytes 262176 | tf_op jit(solution)/shard_map/ppermute | solution.py:281
  98.7 4.3 %collective-permute-start.18 = (f32[256,256]{1,0:T(8,128)S(1)}, f32[256,256]{1,0:T(8,128)S(1)}, u32[]{:S(2)}, u32[]{:S(2)}) collective-permute-start(f32[256,256]{1,0:T(8,128)S(1)} %get-tuple-element.115), channel_id=1, source_target_pairs={{0,5},{1,4},{2,7},{3,6},{4,9},{5,8},{6,11},{7,10},{8,13},{9,12},{1... | collective-permute-start | bytes 786440 | tf_op jit(solution)/shard_map/ppermute | solution.py:281
  104.0 3.3 %collective-permute-start.17 = (f32[256,256]{1,0:T(8,128)S(1)}, f32[256,256]{1,0:T(8,128)S(1)}, u32[]{:S(2)}, u32[]{:S(2)}) collective-permute-start(f32[256,256]{1,0:T(8,128)S(1)} %get-tuple-element.114), channel_id=1, source_target_pairs={{0,4},{1,5},{2,6},{3,7},{4,8},{5,9},{6,10},{7,11},{8,12},{9,13},{1... | collective-permute-start | bytes 786440 | tf_op jit(solution)/shard_map/ppermute | solution.py:281
  111.2 5.9 %collective-permute-done.18.refs_3_ = f32[256,256]{1,0:T(8,128)S(1)} collective-permute-done((f32[256,256]{1,0:T(8,128)S(1)}, f32[256,256]{1,0:T(8,128)S(1)}, u32[]{:S(2)}, u32[]{:S(2)}) %collective-permute-start.18) | collective-permute-done | bytes 262176 | tf_op jit(solution)/shard_map/ppermute | solution.py:281
  118.2 3.2 %collective-permute-done.17.refs_3_ = f32[256,256]{1,0:T(8,128)S(1)} collective-permute-done((f32[256,256]{1,0:T(8,128)S(1)}, f32[256,256]{1,0:T(8,128)S(1)}, u32[]{:S(2)}, u32[]{:S(2)}) %collective-permute-start.17) | collective-permute-done | bytes 262176 | tf_op jit(solution)/shard_map/ppermute | solution.py:281
  122.5 5.1 %collective-permute-done.16.refs_3_ = f32[256,256]{1,0:T(8,128)S(1)} collective-permute-done((f32[256,256]{1,0:T(8,128)S(1)}, f32[256,256]{1,0:T(8,128)S(1)}, u32[]{:S(2)}, u32[]{:S(2)}) %collective-permute-start.16) | collective-permute-done | bytes 262176 | tf_op jit(solution)/shard_map/ppermute | solution.py:281
  (41 shorter events, 31.0 us)
Async XLA Ops:
  3.2 15.5 %collective-permute-start.3 = (f32[256,256]{1,0:T(8,128)S(1)}, f32[256,256]{1,0:T(8,128)S(1)}, u32[]{:S(2)}, u32[]{:S(2)}) collective-permute-start(f32[256,256]{1,0:T(8,128)S(1)} %get-tuple-element.80), channel_id=1, source_target_pairs={{0,4},{1,5},{2,6},{3,7},{4,8},{5,9},{6,10},{7,11},{8,12},{9,13},{1... | collective-permute-start | bytes 786440 | tf_op jit(solution)/shard_map/ppermute | solution.py:281
  8.1 17.6 %collective-permute-start.2 = (f32[256,256]{1,0:T(8,128)S(1)}, f32[256,256]{1,0:T(8,128)S(1)}, u32[]{:S(2)}, u32[]{:S(2)}) collective-permute-start(f32[256,256]{1,0:T(8,128)S(1)} %get-tuple-element.79), channel_id=1, source_target_pairs={{0,5},{1,4},{2,7},{3,6},{4,9},{5,8},{6,11},{7,10},{8,13},{9,12},{1... | collective-permute-start | bytes 786440 | tf_op jit(solution)/shard_map/ppermute | solution.py:281
  11.5 18.5 %collective-permute-start.1 = (f32[256,256]{1,0:T(8,128)S(1)}, f32[256,256]{1,0:T(8,128)S(1)}, u32[]{:S(2)}, u32[]{:S(2)}) collective-permute-start(f32[256,256]{1,0:T(8,128)S(1)} %get-tuple-element.78), channel_id=1, source_target_pairs={{0,4},{1,5},{2,6},{3,7},{4,8},{5,9},{6,10},{7,11},{8,12},{9,13},{1... | collective-permute-start | bytes 786440 | tf_op jit(solution)/shard_map/ppermute | solution.py:281
  15.5 21.4 %collective-permute-start = (f32[256,256]{1,0:T(8,128)S(1)}, f32[256,256]{1,0:T(8,128)S(1)}, u32[]{:S(2)}, u32[]{:S(2)}) collective-permute-start(f32[256,256]{1,0:T(8,128)S(1)} %get-tuple-element.77), channel_id=1, source_target_pairs={{0,5},{1,4},{2,7},{3,6},{4,9},{5,8},{6,11},{7,10},{8,13},{9,12},{1... | collective-permute-start | bytes 786440 | tf_op jit(solution)/shard_map/ppermute | solution.py:281
  19.8 21.4 %collective-permute-start.7 = (f32[256,256]{1,0:T(8,128)S(1)}, f32[256,256]{1,0:T(8,128)S(1)}, u32[]{:S(2)}, u32[]{:S(2)}) collective-permute-start(f32[256,256]{1,0:T(8,128)S(1)} %get-tuple-element.89), channel_id=1, source_target_pairs={{0,4},{1,5},{2,6},{3,7},{4,8},{5,9},{6,10},{7,11},{8,12},{9,13},{1... | collective-permute-start | bytes 786440 | tf_op jit(solution)/shard_map/ppermute | solution.py:281
  26.8 25.8 %collective-permute-start.6 = (f32[256,256]{1,0:T(8,128)S(1)}, f32[256,256]{1,0:T(8,128)S(1)}, u32[]{:S(2)}, u32[]{:S(2)}) collective-permute-start(f32[256,256]{1,0:T(8,128)S(1)} %get-tuple-element.88), channel_id=1, source_target_pairs={{0,6},{1,7},{2,4},{3,5},{4,10},{5,11},{6,8},{7,9},{8,14},{9,15},{1... | collective-permute-start | bytes 786440 | tf_op jit(solution)/shard_map/ppermute | solution.py:281
  31.0 26.5 %collective-permute-start.5 = (f32[256,256]{1,0:T(8,128)S(1)}, f32[256,256]{1,0:T(8,128)S(1)}, u32[]{:S(2)}, u32[]{:S(2)}) collective-permute-start(f32[256,256]{1,0:T(8,128)S(1)} %get-tuple-element.87), channel_id=1, source_target_pairs={{0,4},{1,5},{2,6},{3,7},{4,8},{5,9},{6,10},{7,11},{8,12},{9,13},{1... | collective-permute-start | bytes 786440 | tf_op jit(solution)/shard_map/ppermute | solution.py:281
  38.0 23.1 %collective-permute-start.4 = (f32[256,256]{1,0:T(8,128)S(1)}, f32[256,256]{1,0:T(8,128)S(1)}, u32[]{:S(2)}, u32[]{:S(2)}) collective-permute-start(f32[256,256]{1,0:T(8,128)S(1)} %get-tuple-element.86), channel_id=1, source_target_pairs={{0,6},{1,7},{2,4},{3,5},{4,10},{5,11},{6,8},{7,9},{8,14},{9,15},{1... | collective-permute-start | bytes 786440 | tf_op jit(solution)/shard_map/ppermute | solution.py:281
  42.3 22.2 %collective-permute-start.11 = (f32[256,256]{1,0:T(8,128)S(1)}, f32[256,256]{1,0:T(8,128)S(1)}, u32[]{:S(2)}, u32[]{:S(2)}) collective-permute-start(f32[256,256]{1,0:T(8,128)S(1)} %get-tuple-element.98), channel_id=1, source_target_pairs={{0,4},{1,5},{2,6},{3,7},{4,8},{5,9},{6,10},{7,11},{8,12},{9,13},{1... | collective-permute-start | bytes 786440 | tf_op jit(solution)/shard_map/ppermute | solution.py:281
  53.7 17.8 %collective-permute-start.10 = (f32[256,256]{1,0:T(8,128)S(1)}, f32[256,256]{1,0:T(8,128)S(1)}, u32[]{:S(2)}, u32[]{:S(2)}) collective-permute-start(f32[256,256]{1,0:T(8,128)S(1)} %get-tuple-element.97), channel_id=1, source_target_pairs={{0,5},{1,4},{2,7},{3,6},{4,9},{5,8},{6,11},{7,10},{8,13},{9,12},{1... | collective-permute-start | bytes 786440 | tf_op jit(solution)/shard_map/ppermute | solution.py:281
  58.6 17.1 %collective-permute-start.9 = (f32[256,256]{1,0:T(8,128)S(1)}, f32[256,256]{1,0:T(8,128)S(1)}, u32[]{:S(2)}, u32[]{:S(2)}) collective-permute-start(f32[256,256]{1,0:T(8,128)S(1)} %get-tuple-element.96), channel_id=1, source_target_pairs={{0,4},{1,5},{2,6},{3,7},{4,8},{5,9},{6,10},{7,11},{8,12},{9,13},{1... | collective-permute-start | bytes 786440 | tf_op jit(solution)/shard_map/ppermute | solution.py:281
  62.2 20.5 %collective-permute-start.8 = (f32[256,256]{1,0:T(8,128)S(1)}, f32[256,256]{1,0:T(8,128)S(1)}, u32[]{:S(2)}, u32[]{:S(2)}) collective-permute-start(f32[256,256]{1,0:T(8,128)S(1)} %get-tuple-element.95), channel_id=1, source_target_pairs={{0,5},{1,4},{2,7},{3,6},{4,9},{5,8},{6,11},{7,10},{8,13},{9,12},{1... | collective-permute-start | bytes 786440 | tf_op jit(solution)/shard_map/ppermute | solution.py:281
  65.5 21.4 %collective-permute-start.15 = (f32[256,256]{1,0:T(8,128)S(1)}, f32[256,256]{1,0:T(8,128)S(1)}, u32[]{:S(2)}, u32[]{:S(2)}) collective-permute-start(f32[256,256]{1,0:T(8,128)S(1)} %get-tuple-element.107), channel_id=1, source_target_pairs={{0,4},{1,5},{2,6},{3,7},{4,8},{5,9},{6,10},{7,11},{8,12},{9,13},{1... | collective-permute-start | bytes 786440 | tf_op jit(solution)/shard_map/ppermute | solution.py:281
  72.5 25.1 %collective-permute-start.14 = (f32[256,256]{1,0:T(8,128)S(1)}, f32[256,256]{1,0:T(8,128)S(1)}, u32[]{:S(2)}, u32[]{:S(2)}) collective-permute-start(f32[256,256]{1,0:T(8,128)S(1)} %get-tuple-element.106), channel_id=1, source_target_pairs={{0,6},{1,7},{2,4},{3,5},{4,10},{5,11},{6,8},{7,9},{8,14},{9,15},{1... | collective-permute-start | bytes 786440 | tf_op jit(solution)/shard_map/ppermute | solution.py:281
  76.8 26.2 %collective-permute-start.13 = (f32[256,256]{1,0:T(8,128)S(1)}, f32[256,256]{1,0:T(8,128)S(1)}, u32[]{:S(2)}, u32[]{:S(2)}) collective-permute-start(f32[256,256]{1,0:T(8,128)S(1)} %get-tuple-element.105), channel_id=1, source_target_pairs={{0,4},{1,5},{2,6},{3,7},{4,8},{5,9},{6,10},{7,11},{8,12},{9,13},{1... | collective-permute-start | bytes 786440 | tf_op jit(solution)/shard_map/ppermute | solution.py:281
  83.8 23.5 %collective-permute-start.12 = (f32[256,256]{1,0:T(8,128)S(1)}, f32[256,256]{1,0:T(8,128)S(1)}, u32[]{:S(2)}, u32[]{:S(2)}) collective-permute-start(f32[256,256]{1,0:T(8,128)S(1)} %get-tuple-element.104), channel_id=1, source_target_pairs={{0,6},{1,7},{2,4},{3,5},{4,10},{5,11},{6,8},{7,9},{8,14},{9,15},{1... | collective-permute-start | bytes 786440 | tf_op jit(solution)/shard_map/ppermute | solution.py:281
  88.0 22.2 %collective-permute-start.19 = (f32[256,256]{1,0:T(8,128)S(1)}, f32[256,256]{1,0:T(8,128)S(1)}, u32[]{:S(2)}, u32[]{:S(2)}) collective-permute-start(f32[256,256]{1,0:T(8,128)S(1)} %get-tuple-element.116), channel_id=1, source_target_pairs={{0,4},{1,5},{2,6},{3,7},{4,8},{5,9},{6,10},{7,11},{8,12},{9,13},{1... | collective-permute-start | bytes 786440 | tf_op jit(solution)/shard_map/ppermute | solution.py:281
  98.7 18.5 %collective-permute-start.18 = (f32[256,256]{1,0:T(8,128)S(1)}, f32[256,256]{1,0:T(8,128)S(1)}, u32[]{:S(2)}, u32[]{:S(2)}) collective-permute-start(f32[256,256]{1,0:T(8,128)S(1)} %get-tuple-element.115), channel_id=1, source_target_pairs={{0,5},{1,4},{2,7},{3,6},{4,9},{5,8},{6,11},{7,10},{8,13},{9,12},{1... | collective-permute-start | bytes 786440 | tf_op jit(solution)/shard_map/ppermute | solution.py:281
  104.0 17.4 %collective-permute-start.17 = (f32[256,256]{1,0:T(8,128)S(1)}, f32[256,256]{1,0:T(8,128)S(1)}, u32[]{:S(2)}, u32[]{:S(2)}) collective-permute-start(f32[256,256]{1,0:T(8,128)S(1)} %get-tuple-element.114), channel_id=1, source_target_pairs={{0,4},{1,5},{2,6},{3,7},{4,8},{5,9},{6,10},{7,11},{8,12},{9,13},{1... | collective-permute-start | bytes 786440 | tf_op jit(solution)/shard_map/ppermute | solution.py:281
  108.4 19.2 %collective-permute-start.16 = (f32[256,256]{1,0:T(8,128)S(1)}, f32[256,256]{1,0:T(8,128)S(1)}, u32[]{:S(2)}, u32[]{:S(2)}) collective-permute-start(f32[256,256]{1,0:T(8,128)S(1)} %get-tuple-element.113), channel_id=1, source_target_pairs={{0,5},{1,4},{2,7},{3,6},{4,9},{5,8},{6,11},{7,10},{8,13},{9,12},{1... | collective-permute-start | bytes 786440 | tf_op jit(solution)/shard_map/ppermute | solution.py:281

commit v3 on v2

--- a/solution.py
+++ b/solution.py
@@ -15,7 +15,8 @@
 DECAY = 0.02
 NEG_WEIGHT = 0.25
 AXES = ("blk", "xor")
-ORDERS = ((0, 2, 1, 3),) * SUBS
+TURNS, ROWS = (0, 2, 1, 3), (0, 1, 2, 3)
+ORDERS = (TURNS, TURNS, ROWS, TURNS, ROWS, TURNS)
 BF = jnp.bfloat16
 F32 = jnp.float32
 VMEM_SPEC = pl.BlockSpec(memory_space=pltpu.VMEM)
@@ -105,8 +106,9 @@
     copies = [pltpu.make_async_copy(src, dst, sems.at[n]) for n, (src, dst) in enumerate(zip(args[4:], small))]
     copies.append(pltpu.make_async_copy(users_hbm, users, sems.at[6]))
     at = 7
-    for chunk in range(chunks):
-        target = raw if chunk == 0 else states[chunk]
+    tile = ORDERS[0][0]
+    for chunk in (tile, *(n for n in range(chunks) if n != tile)):
+        target = raw if chunk == tile else states[chunk]
         rows = pl.ds(chunk * CHUNK, CHUNK)
         for part, source in enumerate((items_hbm, item_accum_hbm)):
             copies.append(
@@ -132,8 +134,8 @@
     def each(at, user, grad):
         grad_out[at, :] = grad
 
-    grad_items = chunk_terms(users, left_out, rights[0], factor, each)
-    store_state(states[0], *adagrad(factor, accum, grad_items))
+    grad_items = chunk_terms(users, left_out, rights[tile], factor, each)
+    store_state(states[tile], *adagrad(factor, accum, grad_items))
     for copy in copies[9:]:
         copy.wait()
 

time: 130 us -> 129 us (level)
  transfers between devices with their start and end apart: 20 -> 20, of which waited for: 15 -> 18; matrix products, arithmetic and copies ran while one was open for 0% -> 0% of each run, Pallas kernels for 19% -> 19%
where the time goes in v3:
time: 129 us
  waiting for transfers between devices  66.2 us (51%)
  starting transfers between devices  32.6 us (25%)
  Pallas kernels  29 us (22%)
    ppermute x20, waiting for transfers between devices, move(): return lax.ppermute(state, AXES, pairs)  66.2 us
    ppermute x20, starting transfers between devices, move(): return lax.ppermute(state, AXES, pairs)  32.6 us
    pallas_call x23, Pallas kernels, run_chunk(): pl.pallas_call(functools.partial(chunk_kernel, s, chunk, first, final, ch...  25.1 us
    pallas_call x1, Pallas kernels, run_first(): pl.pallas_call(functools.partial(first_kernel, chunks), out_shape=out, in...  2.59 us
  transfers between devices with their start and end apart: 20, of which 18 were waited for; matrix products, arithmetic and copies ran while one was open for 0% of the time, Pallas kernels for 19%

profile of v3, /device:TPU:1, one launch (start us, length us, event | category | flops | bytes accessed | tf_op | source)
XLA Modules:
  0.0 129.0 jit_solution(1022698859292972375)
XLA Ops:
  0.6 2.6 %first_chunk.1 = (f32[1024,256]{1,0:T(8,128)S(1)}, f32[1024,256]{1,0:T(8,128)S(1)}, bf16[1024,24]{1,0:T(8,128)(2,1)S(1)}, bf16[4,24,256]{2,1,0:T(8,128)(2,1)S(1)...) custom-call(f32[1024,256]{1,0:T(8,128)} %refs_0_.2, ...), custom_call_target="tpu_custom_call" | custom-call | tf_op jit(solution)/shard_map/first_chunk/pallas_call | solution.py:156
  3.2 3.8 %collective-permute-start.3 = (f32[256,256]{1,0:T(8,128)S(1)}, f32[256,256]{1,0:T(8,128)S(1)}, u32[]{:S(2)}, u32[]{:S(2)}) collective-permute-start(f32[256,256]{1,0:T(8,128)S(1)} %get-tuple-element.80), channel_id=1, source_target_pairs={{0,4},{1,5},{2,6},{3,7},{4,8},{5,9},{6,10},{7,11},{8,12},{9,13},{1... | collective-permute-start | bytes 786440 | tf_op jit(solution)/shard_map/ppermute | solution.py:283
  8.1 2.3 %collective-permute-start.2 = (f32[256,256]{1,0:T(8,128)S(1)}, f32[256,256]{1,0:T(8,128)S(1)}, u32[]{:S(2)}, u32[]{:S(2)}) collective-permute-start(f32[256,256]{1,0:T(8,128)S(1)} %get-tuple-element.79), channel_id=1, source_target_pairs={{0,5},{1,4},{2,7},{3,6},{4,9},{5,8},{6,11},{7,10},{8,13},{9,12},{1... | collective-permute-start | bytes 786440 | tf_op jit(solution)/shard_map/ppermute | solution.py:283
  11.5 3.0 %collective-permute-start.1 = (f32[256,256]{1,0:T(8,128)S(1)}, f32[256,256]{1,0:T(8,128)S(1)}, u32[]{:S(2)}, u32[]{:S(2)}) collective-permute-start(f32[256,256]{1,0:T(8,128)S(1)} %get-tuple-element.78), channel_id=1, source_target_pairs={{0,4},{1,5},{2,6},{3,7},{4,8},{5,9},{6,10},{7,11},{8,12},{9,13},{1... | collective-permute-start | bytes 786440 | tf_op jit(solution)/shard_map/ppermute | solution.py:283
  19.8 2.4 %collective-permute-start.7 = (f32[256,256]{1,0:T(8,128)S(1)}, f32[256,256]{1,0:T(8,128)S(1)}, u32[]{:S(2)}, u32[]{:S(2)}) collective-permute-start(f32[256,256]{1,0:T(8,128)S(1)} %get-tuple-element.89), channel_id=1, source_target_pairs={{0,4},{1,5},{2,6},{3,7},{4,8},{5,9},{6,10},{7,11},{8,12},{9,13},{1... | collective-permute-start | bytes 786440 | tf_op jit(solution)/shard_map/ppermute | solution.py:283
  22.2 3.6 %collective-permute-done.2.refs_3_ = f32[256,256]{1,0:T(8,128)S(1)} collective-permute-done((f32[256,256]{1,0:T(8,128)S(1)}, f32[256,256]{1,0:T(8,128)S(1)}, u32[]{:S(2)}, u32[]{:S(2)}) %collective-permute-start.2) | collective-permute-done | bytes 262176 | tf_op jit(solution)/shard_map/ppermute | solution.py:283
  26.8 3.2 %collective-permute-done.1.refs_3_ = f32[256,256]{1,0:T(8,128)S(1)} collective-permute-done((f32[256,256]{1,0:T(8,128)S(1)}, f32[256,256]{1,0:T(8,128)S(1)}, u32[]{:S(2)}, u32[]{:S(2)}) %collective-permute-start.1) | collective-permute-done | bytes 262176 | tf_op jit(solution)/shard_map/ppermute | solution.py:283
  31.2 5.8 %collective-permute-done.refs_3_ = f32[256,256]{1,0:T(8,128)S(1)} collective-permute-done((f32[256,256]{1,0:T(8,128)S(1)}, f32[256,256]{1,0:T(8,128)S(1)}, u32[]{:S(2)}, u32[]{:S(2)}) %collective-permute-start) | collective-permute-done | bytes 262176 | tf_op jit(solution)/shard_map/ppermute | solution.py:283
  38.1 3.1 %collective-permute-done.7.refs_3_ = f32[256,256]{1,0:T(8,128)S(1)} collective-permute-done((f32[256,256]{1,0:T(8,128)S(1)}, f32[256,256]{1,0:T(8,128)S(1)}, u32[]{:S(2)}, u32[]{:S(2)}) %collective-permute-start.7) | collective-permute-done | bytes 262176 | tf_op jit(solution)/shard_map/ppermute | solution.py:283
  42.5 4.3 %collective-permute-done.6.refs_3_ = f32[256,256]{1,0:T(8,128)S(1)} collective-permute-done((f32[256,256]{1,0:T(8,128)S(1)}, f32[256,256]{1,0:T(8,128)S(1)}, u32[]{:S(2)}, u32[]{:S(2)}) %collective-permute-start.6) | collective-permute-done | bytes 262176 | tf_op jit(solution)/shard_map/ppermute | solution.py:283
  47.9 4.6 %collective-permute-done.5.refs_3_ = f32[256,256]{1,0:T(8,128)S(1)} collective-permute-done((f32[256,256]{1,0:T(8,128)S(1)}, f32[256,256]{1,0:T(8,128)S(1)}, u32[]{:S(2)}, u32[]{:S(2)}) %collective-permute-start.5) | collective-permute-done | bytes 262176 | tf_op jit(solution)/shard_map/ppermute | solution.py:283
  53.6 4.1 %collective-permute-start.10 = (f32[256,256]{1,0:T(8,128)S(1)}, f32[256,256]{1,0:T(8,128)S(1)}, u32[]{:S(2)}, u32[]{:S(2)}) collective-permute-start(f32[256,256]{1,0:T(8,128)S(1)} %get-tuple-element.97), channel_id=1, source_target_pairs={{0,5},{1,4},{2,7},{3,6},{4,9},{5,8},{6,11},{7,10},{8,13},{9,12},{1... | collective-permute-start | bytes 786440 | tf_op jit(solution)/shard_map/ppermute | solution.py:283
  57.7 2.3 %collective-permute-start.9 = (f32[256,256]{1,0:T(8,128)S(1)}, f32[256,256]{1,0:T(8,128)S(1)}, u32[]{:S(2)}, u32[]{:S(2)}) collective-permute-start(f32[256,256]{1,0:T(8,128)S(1)} %get-tuple-element.96), channel_id=1, source_target_pairs={{0,4},{1,5},{2,6},{3,7},{4,8},{5,9},{6,10},{7,11},{8,12},{9,13},{1... | collective-permute-start | bytes 786440 | tf_op jit(solution)/shard_map/ppermute | solution.py:283
  66.7 4.6 %collective-permute-done.10.refs_3_ = f32[256,256]{1,0:T(8,128)S(1)} collective-permute-done((f32[256,256]{1,0:T(8,128)S(1)}, f32[256,256]{1,0:T(8,128)S(1)}, u32[]{:S(2)}, u32[]{:S(2)}) %collective-permute-start.10) | collective-permute-done | bytes 262176 | tf_op jit(solution)/shard_map/ppermute | solution.py:283
  72.4 3.2 %collective-permute-done.9.refs_3_ = f32[256,256]{1,0:T(8,128)S(1)} collective-permute-done((f32[256,256]{1,0:T(8,128)S(1)}, f32[256,256]{1,0:T(8,128)S(1)}, u32[]{:S(2)}, u32[]{:S(2)}) %collective-permute-start.9) | collective-permute-done | bytes 262176 | tf_op jit(solution)/shard_map/ppermute | solution.py:283
  78.1 4.5 %collective-permute-done.8.refs_3_ = f32[256,256]{1,0:T(8,128)S(1)} collective-permute-done((f32[256,256]{1,0:T(8,128)S(1)}, f32[256,256]{1,0:T(8,128)S(1)}, u32[]{:S(2)}, u32[]{:S(2)}) %collective-permute-start.8) | collective-permute-done | bytes 262176 | tf_op jit(solution)/shard_map/ppermute | solution.py:283
  83.7 3.1 %collective-permute-done.15.refs_3_ = f32[256,256]{1,0:T(8,128)S(1)} collective-permute-done((f32[256,256]{1,0:T(8,128)S(1)}, f32[256,256]{1,0:T(8,128)S(1)}, u32[]{:S(2)}, u32[]{:S(2)}) %collective-permute-start.15) | collective-permute-done | bytes 262176 | tf_op jit(solution)/shard_map/ppermute | solution.py:283
  87.9 4.5 %collective-permute-done.14.refs_3_ = f32[256,256]{1,0:T(8,128)S(1)} collective-permute-done((f32[256,256]{1,0:T(8,128)S(1)}, f32[256,256]{1,0:T(8,128)S(1)}, u32[]{:S(2)}, u32[]{:S(2)}) %collective-permute-start.14) | collective-permute-done | bytes 262176 | tf_op jit(solution)/shard_map/ppermute | solution.py:283
  93.5 4.9 %collective-permute-done.13.refs_3_ = f32[256,256]{1,0:T(8,128)S(1)} collective-permute-done((f32[256,256]{1,0:T(8,128)S(1)}, f32[256,256]{1,0:T(8,128)S(1)}, u32[]{:S(2)}, u32[]{:S(2)}) %collective-permute-start.13) | collective-permute-done | bytes 262176 | tf_op jit(solution)/shard_map/ppermute | solution.py:283
  99.4 3.5 %collective-permute-start.18 = (f32[256,256]{1,0:T(8,128)S(1)}, f32[256,256]{1,0:T(8,128)S(1)}, u32[]{:S(2)}, u32[]{:S(2)}) collective-permute-start(f32[256,256]{1,0:T(8,128)S(1)} %get-tuple-element.115), channel_id=1, source_target_pairs={{0,5},{1,4},{2,7},{3,6},{4,9},{5,8},{6,11},{7,10},{8,13},{9,12},{1... | collective-permute-start | bytes 786440 | tf_op jit(solution)/shard_map/ppermute | solution.py:283
  102.9 3.0 %collective-permute-start.17 = (f32[256,256]{1,0:T(8,128)S(1)}, f32[256,256]{1,0:T(8,128)S(1)}, u32[]{:S(2)}, u32[]{:S(2)}) collective-permute-start(f32[256,256]{1,0:T(8,128)S(1)} %get-tuple-element.114), channel_id=1, source_target_pairs={{0,4},{1,5},{2,6},{3,7},{4,8},{5,9},{6,10},{7,11},{8,12},{9,13},{1... | collective-permute-start | bytes 786440 | tf_op jit(solution)/shard_map/ppermute | solution.py:283
  110.5 5.9 %collective-permute-done.18.refs_3_ = f32[256,256]{1,0:T(8,128)S(1)} collective-permute-done((f32[256,256]{1,0:T(8,128)S(1)}, f32[256,256]{1,0:T(8,128)S(1)}, u32[]{:S(2)}, u32[]{:S(2)}) %collective-permute-start.18) | collective-permute-done | bytes 262176 | tf_op jit(solution)/shard_map/ppermute | solution.py:283
  117.4 3.2 %collective-permute-done.17.refs_3_ = f32[256,256]{1,0:T(8,128)S(1)} collective-permute-done((f32[256,256]{1,0:T(8,128)S(1)}, f32[256,256]{1,0:T(8,128)S(1)}, u32[]{:S(2)}, u32[]{:S(2)}) %collective-permute-start.17) | collective-permute-done | bytes 262176 | tf_op jit(solution)/shard_map/ppermute | solution.py:283
  121.7 5.1 %collective-permute-done.16.refs_3_ = f32[256,256]{1,0:T(8,128)S(1)} collective-permute-done((f32[256,256]{1,0:T(8,128)S(1)}, f32[256,256]{1,0:T(8,128)S(1)}, u32[]{:S(2)}, u32[]{:S(2)}) %collective-permute-start.16) | collective-permute-done | bytes 262176 | tf_op jit(solution)/shard_map/ppermute | solution.py:283
  (41 shorter events, 37.3 us)
Async XLA Ops:
  3.2 15.5 %collective-permute-start.3 = (f32[256,256]{1,0:T(8,128)S(1)}, f32[256,256]{1,0:T(8,128)S(1)}, u32[]{:S(2)}, u32[]{:S(2)}) collective-permute-start(f32[256,256]{1,0:T(8,128)S(1)} %get-tuple-element.80), channel_id=1, source_target_pairs={{0,4},{1,5},{2,6},{3,7},{4,8},{5,9},{6,10},{7,11},{8,12},{9,13},{1... | collective-permute-start | bytes 786440 | tf_op jit(solution)/shard_map/ppermute | solution.py:283
  8.1 17.6 %collective-permute-start.2 = (f32[256,256]{1,0:T(8,128)S(1)}, f32[256,256]{1,0:T(8,128)S(1)}, u32[]{:S(2)}, u32[]{:S(2)}) collective-permute-start(f32[256,256]{1,0:T(8,128)S(1)} %get-tuple-element.79), channel_id=1, source_target_pairs={{0,5},{1,4},{2,7},{3,6},{4,9},{5,8},{6,11},{7,10},{8,13},{9,12},{1... | collective-permute-start | bytes 786440 | tf_op jit(solution)/shard_map/ppermute | solution.py:283
  11.5 18.5 %collective-permute-start.1 = (f32[256,256]{1,0:T(8,128)S(1)}, f32[256,256]{1,0:T(8,128)S(1)}, u32[]{:S(2)}, u32[]{:S(2)}) collective-permute-start(f32[256,256]{1,0:T(8,128)S(1)} %get-tuple-element.78), channel_id=1, source_target_pairs={{0,4},{1,5},{2,6},{3,7},{4,8},{5,9},{6,10},{7,11},{8,12},{9,13},{1... | collective-permute-start | bytes 786440 | tf_op jit(solution)/shard_map/ppermute | solution.py:283
  15.5 21.4 %collective-permute-start = (f32[256,256]{1,0:T(8,128)S(1)}, f32[256,256]{1,0:T(8,128)S(1)}, u32[]{:S(2)}, u32[]{:S(2)}) collective-permute-start(f32[256,256]{1,0:T(8,128)S(1)} %get-tuple-element.77), channel_id=1, source_target_pairs={{0,5},{1,4},{2,7},{3,6},{4,9},{5,8},{6,11},{7,10},{8,13},{9,12},{1... | collective-permute-start | bytes 786440 | tf_op jit(solution)/shard_map/ppermute | solution.py:283
  19.8 21.4 %collective-permute-start.7 = (f32[256,256]{1,0:T(8,128)S(1)}, f32[256,256]{1,0:T(8,128)S(1)}, u32[]{:S(2)}, u32[]{:S(2)}) collective-permute-start(f32[256,256]{1,0:T(8,128)S(1)} %get-tuple-element.89), channel_id=1, source_target_pairs={{0,4},{1,5},{2,6},{3,7},{4,8},{5,9},{6,10},{7,11},{8,12},{9,13},{1... | collective-permute-start | bytes 786440 | tf_op jit(solution)/shard_map/ppermute | solution.py:283
  31.0 15.8 %collective-permute-start.6 = (f32[256,256]{1,0:T(8,128)S(1)}, f32[256,256]{1,0:T(8,128)S(1)}, u32[]{:S(2)}, u32[]{:S(2)}) collective-permute-start(f32[256,256]{1,0:T(8,128)S(1)} %get-tuple-element.88), channel_id=1, source_target_pairs={{0,4},{1,5},{2,6},{3,7},{4,8},{5,9},{6,10},{7,11},{8,12},{9,13},{1... | collective-permute-start | bytes 786440 | tf_op jit(solution)/shard_map/ppermute | solution.py:283
  31.1 21.4 %collective-permute-start.5 = (f32[256,256]{1,0:T(8,128)S(1)}, f32[256,256]{1,0:T(8,128)S(1)}, u32[]{:S(2)}, u32[]{:S(2)}) collective-permute-start(f32[256,256]{1,0:T(8,128)S(1)} %get-tuple-element.87), channel_id=1, source_target_pairs={{0,6},{1,7},{2,4},{3,5},{4,10},{5,11},{6,8},{7,9},{8,14},{9,15},{1... | collective-permute-start | bytes 786440 | tf_op jit(solution)/shard_map/ppermute | solution.py:283
  38.0 22.0 %collective-permute-start.4 = (f32[256,256]{1,0:T(8,128)S(1)}, f32[256,256]{1,0:T(8,128)S(1)}, u32[]{:S(2)}, u32[]{:S(2)}) collective-permute-start(f32[256,256]{1,0:T(8,128)S(1)} %get-tuple-element.86), channel_id=1, source_target_pairs={{0,6},{1,7},{2,4},{3,5},{4,10},{5,11},{6,8},{7,9},{8,14},{9,15},{1... | collective-permute-start | bytes 786440 | tf_op jit(solution)/shard_map/ppermute | solution.py:283
  42.3 22.1 %collective-permute-start.11 = (f32[256,256]{1,0:T(8,128)S(1)}, f32[256,256]{1,0:T(8,128)S(1)}, u32[]{:S(2)}, u32[]{:S(2)}) collective-permute-start(f32[256,256]{1,0:T(8,128)S(1)} %get-tuple-element.98), channel_id=1, source_target_pairs={{0,4},{1,5},{2,6},{3,7},{4,8},{5,9},{6,10},{7,11},{8,12},{9,13},{1... | collective-permute-start | bytes 786440 | tf_op jit(solution)/shard_map/ppermute | solution.py:283
  53.6 17.8 %collective-permute-start.10 = (f32[256,256]{1,0:T(8,128)S(1)}, f32[256,256]{1,0:T(8,128)S(1)}, u32[]{:S(2)}, u32[]{:S(2)}) collective-permute-start(f32[256,256]{1,0:T(8,128)S(1)} %get-tuple-element.97), channel_id=1, source_target_pairs={{0,5},{1,4},{2,7},{3,6},{4,9},{5,8},{6,11},{7,10},{8,13},{9,12},{1... | collective-permute-start | bytes 786440 | tf_op jit(solution)/shard_map/ppermute | solution.py:283
  57.7 17.9 %collective-permute-start.9 = (f32[256,256]{1,0:T(8,128)S(1)}, f32[256,256]{1,0:T(8,128)S(1)}, u32[]{:S(2)}, u32[]{:S(2)}) collective-permute-start(f32[256,256]{1,0:T(8,128)S(1)} %get-tuple-element.96), channel_id=1, source_target_pairs={{0,4},{1,5},{2,6},{3,7},{4,8},{5,9},{6,10},{7,11},{8,12},{9,13},{1... | collective-permute-start | bytes 786440 | tf_op jit(solution)/shard_map/ppermute | solution.py:283
  61.1 21.5 %collective-permute-start.8 = (f32[256,256]{1,0:T(8,128)S(1)}, f32[256,256]{1,0:T(8,128)S(1)}, u32[]{:S(2)}, u32[]{:S(2)}) collective-permute-start(f32[256,256]{1,0:T(8,128)S(1)} %get-tuple-element.95), channel_id=1, source_target_pairs={{0,5},{1,4},{2,7},{3,6},{4,9},{5,8},{6,11},{7,10},{8,13},{9,12},{1... | collective-permute-start | bytes 786440 | tf_op jit(solution)/shard_map/ppermute | solution.py:283
  65.4 21.4 %collective-permute-start.15 = (f32[256,256]{1,0:T(8,128)S(1)}, f32[256,256]{1,0:T(8,128)S(1)}, u32[]{:S(2)}, u32[]{:S(2)}) collective-permute-start(f32[256,256]{1,0:T(8,128)S(1)} %get-tuple-element.107), channel_id=1, source_target_pairs={{0,4},{1,5},{2,6},{3,7},{4,8},{5,9},{6,10},{7,11},{8,12},{9,13},{1... | collective-permute-start | bytes 786440 | tf_op jit(solution)/shard_map/ppermute | solution.py:283
  76.6 15.8 %collective-permute-start.14 = (f32[256,256]{1,0:T(8,128)S(1)}, f32[256,256]{1,0:T(8,128)S(1)}, u32[]{:S(2)}, u32[]{:S(2)}) collective-permute-start(f32[256,256]{1,0:T(8,128)S(1)} %get-tuple-element.106), channel_id=1, source_target_pairs={{0,4},{1,5},{2,6},{3,7},{4,8},{5,9},{6,10},{7,11},{8,12},{9,13},{1... | collective-permute-start | bytes 786440 | tf_op jit(solution)/shard_map/ppermute | solution.py:283
  76.7 21.7 %collective-permute-start.13 = (f32[256,256]{1,0:T(8,128)S(1)}, f32[256,256]{1,0:T(8,128)S(1)}, u32[]{:S(2)}, u32[]{:S(2)}) collective-permute-start(f32[256,256]{1,0:T(8,128)S(1)} %get-tuple-element.105), channel_id=1, source_target_pairs={{0,6},{1,7},{2,4},{3,5},{4,10},{5,11},{6,8},{7,9},{8,14},{9,15},{1... | collective-permute-start | bytes 786440 | tf_op jit(solution)/shard_map/ppermute | solution.py:283
  83.6 22.3 %collective-permute-start.12 = (f32[256,256]{1,0:T(8,128)S(1)}, f32[256,256]{1,0:T(8,128)S(1)}, u32[]{:S(2)}, u32[]{:S(2)}) collective-permute-start(f32[256,256]{1,0:T(8,128)S(1)} %get-tuple-element.104), channel_id=1, source_target_pairs={{0,6},{1,7},{2,4},{3,5},{4,10},{5,11},{6,8},{7,9},{8,14},{9,15},{1... | collective-permute-start | bytes 786440 | tf_op jit(solution)/shard_map/ppermute | solution.py:283
  87.9 21.5 %collective-permute-start.19 = (f32[256,256]{1,0:T(8,128)S(1)}, f32[256,256]{1,0:T(8,128)S(1)}, u32[]{:S(2)}, u32[]{:S(2)}) collective-permute-start(f32[256,256]{1,0:T(8,128)S(1)} %get-tuple-element.116), channel_id=1, source_target_pairs={{0,4},{1,5},{2,6},{3,7},{4,8},{5,9},{6,10},{7,11},{8,12},{9,13},{1... | collective-permute-start | bytes 786440 | tf_op jit(solution)/shard_map/ppermute | solution.py:283
  99.4 17.0 %collective-permute-start.18 = (f32[256,256]{1,0:T(8,128)S(1)}, f32[256,256]{1,0:T(8,128)S(1)}, u32[]{:S(2)}, u32[]{:S(2)}) collective-permute-start(f32[256,256]{1,0:T(8,128)S(1)} %get-tuple-element.115), channel_id=1, source_target_pairs={{0,5},{1,4},{2,7},{3,6},{4,9},{5,8},{6,11},{7,10},{8,13},{9,12},{1... | collective-permute-start | bytes 786440 | tf_op jit(solution)/shard_map/ppermute | solution.py:283
  102.9 17.7 %collective-permute-start.17 = (f32[256,256]{1,0:T(8,128)S(1)}, f32[256,256]{1,0:T(8,128)S(1)}, u32[]{:S(2)}, u32[]{:S(2)}) collective-permute-start(f32[256,256]{1,0:T(8,128)S(1)} %get-tuple-element.114), channel_id=1, source_target_pairs={{0,4},{1,5},{2,6},{3,7},{4,8},{5,9},{6,10},{7,11},{8,12},{9,13},{1... | collective-permute-start | bytes 786440 | tf_op jit(solution)/shard_map/ppermute | solution.py:283
  107.0 19.8 %collective-permute-start.16 = (f32[256,256]{1,0:T(8,128)S(1)}, f32[256,256]{1,0:T(8,128)S(1)}, u32[]{:S(2)}, u32[]{:S(2)}) collective-permute-start(f32[256,256]{1,0:T(8,128)S(1)} %get-tuple-element.113), channel_id=1, source_target_pairs={{0,5},{1,4},{2,7},{3,6},{4,9},{5,8},{6,11},{7,10},{8,13},{9,12},{1... | collective-permute-start | bytes 786440 | tf_op jit(solution)/shard_map/ppermute | solution.py:283

commit v4 on v3

--- a/solution.py
+++ b/solution.py
@@ -39,15 +39,21 @@
     return groups[0] if count == 1 else jnp.concatenate(groups, axis=1)
 
 
+def padded(terms):
+    return -(-terms // 16) * 16
+
+
 def pair_factors(s, su, si, nu, ni, row_live, col_live, user_tiles, chunks):
     rows = row_live[s].astype(F32)
     cols = col_live[s].astype(F32)
     ones = jnp.ones((nu.shape[1], TILE), F32)
     at = slice(s, s + 1)
+    spare = padded(su.shape[1] + nu.shape[1]) - su.shape[1] - nu.shape[1]
     left = jnp.concatenate(
         [
             spread(down(su[at, :]), rows, 0, user_tiles),
             spread(down(nu[at, :]), ones, 0, user_tiles),
+            jnp.zeros((spare, user_tiles * TILE), F32),
         ],
         axis=0,
     )
@@ -62,6 +68,7 @@
                 [
                     jnp.concatenate([seen, seen], axis=1),
                     jnp.concatenate([NEG_WEIGHT * sampled, jnp.zeros_like(sampled)], axis=1),
+                    jnp.zeros((spare, 2 * CHUNK), F32),
                 ],
                 axis=0,
             ).astype(BF)
@@ -144,7 +151,7 @@
     users, user_accum, items, item_accum, *small = args
     width = users.shape[1]
     chunks = items.shape[0] // CHUNK
-    terms = small[0].shape[1] + small[4].shape[1]
+    terms = padded(small[0].shape[1] + small[4].shape[1])
     sds = jax.ShapeDtypeStruct
     out = [
         sds(users.shape, F32),
@@ -181,7 +188,7 @@
 
 
 def run_factors(small, user_rows, chunks, after):
-    terms = small[0].shape[1] + small[4].shape[1]
+    terms = padded(small[0].shape[1] + small[4].shape[1])
     pinned = [pltpu.with_memory_space_constraint(x, pltpu.HBM) for x in small]
     return pl.pallas_call(
         functools.partial(factors_kernel, user_rows // TILE, chunks),

time: 129 us -> 129 us (level)
  no operation moved by 1% of the time
where the time goes in v4:
time: 129 us
  waiting for transfers between devices  66.3 us (51%)
  starting transfers between devices  32.6 us (25%)
  Pallas kernels  29 us (22%)
    ppermute x20, waiting for transfers between devices, move(): return lax.ppermute(state, AXES, pairs)  66.3 us
    ppermute x20, starting transfers between devices, move(): return lax.ppermute(state, AXES, pairs)  32.6 us
    pallas_call x23, Pallas kernels, run_chunk(): pl.pallas_call(functools.partial(chunk_kernel, s, chunk, first, final, ch...  25 us
    pallas_call x1, Pallas kernels, run_first(): pl.pallas_call(functools.partial(first_kernel, chunks), out_shape=out, in...  2.59 us
  transfers between devices with their start and end apart: 20, of which 18 were waited for; matrix products, arithmetic and copies ran while one was open for 0% of the time, Pallas kernels for 19%

profile of v4, /device:TPU:1, one launch (start us, length us, event | category | flops | bytes accessed | tf_op | source)
XLA Modules:
  0.0 129.0 jit_solution(10719006414642111895)
XLA Ops:
  0.6 2.6 %first_chunk.1 = (f32[1024,256]{1,0:T(8,128)S(1)}, f32[1024,256]{1,0:T(8,128)S(1)}, bf16[1024,32]{1,0:T(8,128)(2,1)S(1)}, bf16[4,32,256]{2,1,0:T(8,128)(2,1)S(1)...) custom-call(f32[1024,256]{1,0:T(8,128)} %refs_0_.2, ...), custom_call_target="tpu_custom_call" | custom-call | tf_op jit(solution)/shard_map/first_chunk/pallas_call | solution.py:163
  3.2 3.8 %collective-permute-start.3 = (f32[256,256]{1,0:T(8,128)S(1)}, f32[256,256]{1,0:T(8,128)S(1)}, u32[]{:S(2)}, u32[]{:S(2)}) collective-permute-start(f32[256,256]{1,0:T(8,128)S(1)} %get-tuple-element.80), channel_id=1, source_target_pairs={{0,4},{1,5},{2,6},{3,7},{4,8},{5,9},{6,10},{7,11},{8,12},{9,13},{1... | collective-permute-start | bytes 786440 | tf_op jit(solution)/shard_map/ppermute | solution.py:290
  8.1 2.3 %collective-permute-start.2 = (f32[256,256]{1,0:T(8,128)S(1)}, f32[256,256]{1,0:T(8,128)S(1)}, u32[]{:S(2)}, u32[]{:S(2)}) collective-permute-start(f32[256,256]{1,0:T(8,128)S(1)} %get-tuple-element.79), channel_id=1, source_target_pairs={{0,5},{1,4},{2,7},{3,6},{4,9},{5,8},{6,11},{7,10},{8,13},{9,12},{1... | collective-permute-start | bytes 786440 | tf_op jit(solution)/shard_map/ppermute | solution.py:290
  11.5 3.0 %collective-permute-start.1 = (f32[256,256]{1,0:T(8,128)S(1)}, f32[256,256]{1,0:T(8,128)S(1)}, u32[]{:S(2)}, u32[]{:S(2)}) collective-permute-start(f32[256,256]{1,0:T(8,128)S(1)} %get-tuple-element.78), channel_id=1, source_target_pairs={{0,4},{1,5},{2,6},{3,7},{4,8},{5,9},{6,10},{7,11},{8,12},{9,13},{1... | collective-permute-start | bytes 786440 | tf_op jit(solution)/shard_map/ppermute | solution.py:290
  19.8 2.4 %collective-permute-start.7 = (f32[256,256]{1,0:T(8,128)S(1)}, f32[256,256]{1,0:T(8,128)S(1)}, u32[]{:S(2)}, u32[]{:S(2)}) collective-permute-start(f32[256,256]{1,0:T(8,128)S(1)} %get-tuple-element.89), channel_id=1, source_target_pairs={{0,4},{1,5},{2,6},{3,7},{4,8},{5,9},{6,10},{7,11},{8,12},{9,13},{1... | collective-permute-start | bytes 786440 | tf_op jit(solution)/shard_map/ppermute | solution.py:290
  22.2 3.6 %collective-permute-done.2.refs_3_ = f32[256,256]{1,0:T(8,128)S(1)} collective-permute-done((f32[256,256]{1,0:T(8,128)S(1)}, f32[256,256]{1,0:T(8,128)S(1)}, u32[]{:S(2)}, u32[]{:S(2)}) %collective-permute-start.2) | collective-permute-done | bytes 262176 | tf_op jit(solution)/shard_map/ppermute | solution.py:290
  26.8 3.2 %collective-permute-done.1.refs_3_ = f32[256,256]{1,0:T(8,128)S(1)} collective-permute-done((f32[256,256]{1,0:T(8,128)S(1)}, f32[256,256]{1,0:T(8,128)S(1)}, u32[]{:S(2)}, u32[]{:S(2)}) %collective-permute-start.1) | collective-permute-done | bytes 262176 | tf_op jit(solution)/shard_map/ppermute | solution.py:290
  31.2 5.8 %collective-permute-done.refs_3_ = f32[256,256]{1,0:T(8,128)S(1)} collective-permute-done((f32[256,256]{1,0:T(8,128)S(1)}, f32[256,256]{1,0:T(8,128)S(1)}, u32[]{:S(2)}, u32[]{:S(2)}) %collective-permute-start) | collective-permute-done | bytes 262176 | tf_op jit(solution)/shard_map/ppermute | solution.py:290
  38.1 3.1 %collective-permute-done.7.refs_3_ = f32[256,256]{1,0:T(8,128)S(1)} collective-permute-done((f32[256,256]{1,0:T(8,128)S(1)}, f32[256,256]{1,0:T(8,128)S(1)}, u32[]{:S(2)}, u32[]{:S(2)}) %collective-permute-start.7) | collective-permute-done | bytes 262176 | tf_op jit(solution)/shard_map/ppermute | solution.py:290
  42.5 4.3 %collective-permute-done.6.refs_3_ = f32[256,256]{1,0:T(8,128)S(1)} collective-permute-done((f32[256,256]{1,0:T(8,128)S(1)}, f32[256,256]{1,0:T(8,128)S(1)}, u32[]{:S(2)}, u32[]{:S(2)}) %collective-permute-start.6) | collective-permute-done | bytes 262176 | tf_op jit(solution)/shard_map/ppermute | solution.py:290
  47.9 4.6 %collective-permute-done.5.refs_3_ = f32[256,256]{1,0:T(8,128)S(1)} collective-permute-done((f32[256,256]{1,0:T(8,128)S(1)}, f32[256,256]{1,0:T(8,128)S(1)}, u32[]{:S(2)}, u32[]{:S(2)}) %collective-permute-start.5) | collective-permute-done | bytes 262176 | tf_op jit(solution)/shard_map/ppermute | solution.py:290
  53.6 4.1 %collective-permute-start.10 = (f32[256,256]{1,0:T(8,128)S(1)}, f32[256,256]{1,0:T(8,128)S(1)}, u32[]{:S(2)}, u32[]{:S(2)}) collective-permute-start(f32[256,256]{1,0:T(8,128)S(1)} %get-tuple-element.97), channel_id=1, source_target_pairs={{0,5},{1,4},{2,7},{3,6},{4,9},{5,8},{6,11},{7,10},{8,13},{9,12},{1... | collective-permute-start | bytes 786440 | tf_op jit(solution)/shard_map/ppermute | solution.py:290
  57.7 2.3 %collective-permute-start.9 = (f32[256,256]{1,0:T(8,128)S(1)}, f32[256,256]{1,0:T(8,128)S(1)}, u32[]{:S(2)}, u32[]{:S(2)}) collective-permute-start(f32[256,256]{1,0:T(8,128)S(1)} %get-tuple-element.96), channel_id=1, source_target_pairs={{0,4},{1,5},{2,6},{3,7},{4,8},{5,9},{6,10},{7,11},{8,12},{9,13},{1... | collective-permute-start | bytes 786440 | tf_op jit(solution)/shard_map/ppermute | solution.py:290
  66.7 4.7 %collective-permute-done.10.refs_3_ = f32[256,256]{1,0:T(8,128)S(1)} collective-permute-done((f32[256,256]{1,0:T(8,128)S(1)}, f32[256,256]{1,0:T(8,128)S(1)}, u32[]{:S(2)}, u32[]{:S(2)}) %collective-permute-start.10) | collective-permute-done | bytes 262176 | tf_op jit(solution)/shard_map/ppermute | solution.py:290
  72.4 3.2 %collective-permute-done.9.refs_3_ = f32[256,256]{1,0:T(8,128)S(1)} collective-permute-done((f32[256,256]{1,0:T(8,128)S(1)}, f32[256,256]{1,0:T(8,128)S(1)}, u32[]{:S(2)}, u32[]{:S(2)}) %collective-permute-start.9) | collective-permute-done | bytes 262176 | tf_op jit(solution)/shard_map/ppermute | solution.py:290
  78.1 4.5 %collective-permute-done.8.refs_3_ = f32[256,256]{1,0:T(8,128)S(1)} collective-permute-done((f32[256,256]{1,0:T(8,128)S(1)}, f32[256,256]{1,0:T(8,128)S(1)}, u32[]{:S(2)}, u32[]{:S(2)}) %collective-permute-start.8) | collective-permute-done | bytes 262176 | tf_op jit(solution)/shard_map/ppermute | solution.py:290
  83.7 3.1 %collective-permute-done.15.refs_3_ = f32[256,256]{1,0:T(8,128)S(1)} collective-permute-done((f32[256,256]{1,0:T(8,128)S(1)}, f32[256,256]{1,0:T(8,128)S(1)}, u32[]{:S(2)}, u32[]{:S(2)}) %collective-permute-start.15) | collective-permute-done | bytes 262176 | tf_op jit(solution)/shard_map/ppermute | solution.py:290
  87.9 4.5 %collective-permute-done.14.refs_3_ = f32[256,256]{1,0:T(8,128)S(1)} collective-permute-done((f32[256,256]{1,0:T(8,128)S(1)}, f32[256,256]{1,0:T(8,128)S(1)}, u32[]{:S(2)}, u32[]{:S(2)}) %collective-permute-start.14) | collective-permute-done | bytes 262176 | tf_op jit(solution)/shard_map/ppermute | solution.py:290
  93.5 4.9 %collective-permute-done.13.refs_3_ = f32[256,256]{1,0:T(8,128)S(1)} collective-permute-done((f32[256,256]{1,0:T(8,128)S(1)}, f32[256,256]{1,0:T(8,128)S(1)}, u32[]{:S(2)}, u32[]{:S(2)}) %collective-permute-start.13) | collective-permute-done | bytes 262176 | tf_op jit(solution)/shard_map/ppermute | solution.py:290
  99.4 3.5 %collective-permute-start.18 = (f32[256,256]{1,0:T(8,128)S(1)}, f32[256,256]{1,0:T(8,128)S(1)}, u32[]{:S(2)}, u32[]{:S(2)}) collective-permute-start(f32[256,256]{1,0:T(8,128)S(1)} %get-tuple-element.115), channel_id=1, source_target_pairs={{0,5},{1,4},{2,7},{3,6},{4,9},{5,8},{6,11},{7,10},{8,13},{9,12},{1... | collective-permute-start | bytes 786440 | tf_op jit(solution)/shard_map/ppermute | solution.py:290
  102.9 3.0 %collective-permute-start.17 = (f32[256,256]{1,0:T(8,128)S(1)}, f32[256,256]{1,0:T(8,128)S(1)}, u32[]{:S(2)}, u32[]{:S(2)}) collective-permute-start(f32[256,256]{1,0:T(8,128)S(1)} %get-tuple-element.114), channel_id=1, source_target_pairs={{0,4},{1,5},{2,6},{3,7},{4,8},{5,9},{6,10},{7,11},{8,12},{9,13},{1... | collective-permute-start | bytes 786440 | tf_op jit(solution)/shard_map/ppermute | solution.py:290
  110.5 5.9 %collective-permute-done.18.refs_3_ = f32[256,256]{1,0:T(8,128)S(1)} collective-permute-done((f32[256,256]{1,0:T(8,128)S(1)}, f32[256,256]{1,0:T(8,128)S(1)}, u32[]{:S(2)}, u32[]{:S(2)}) %collective-permute-start.18) | collective-permute-done | bytes 262176 | tf_op jit(solution)/shard_map/ppermute | solution.py:290
  117.4 3.2 %collective-permute-done.17.refs_3_ = f32[256,256]{1,0:T(8,128)S(1)} collective-permute-done((f32[256,256]{1,0:T(8,128)S(1)}, f32[256,256]{1,0:T(8,128)S(1)}, u32[]{:S(2)}, u32[]{:S(2)}) %collective-permute-start.17) | collective-permute-done | bytes 262176 | tf_op jit(solution)/shard_map/ppermute | solution.py:290
  121.7 5.1 %collective-permute-done.16.refs_3_ = f32[256,256]{1,0:T(8,128)S(1)} collective-permute-done((f32[256,256]{1,0:T(8,128)S(1)}, f32[256,256]{1,0:T(8,128)S(1)}, u32[]{:S(2)}, u32[]{:S(2)}) %collective-permute-start.16) | collective-permute-done | bytes 262176 | tf_op jit(solution)/shard_map/ppermute | solution.py:290
  (41 shorter events, 37.3 us)
Async XLA Ops:
  3.2 15.5 %collective-permute-start.3 = (f32[256,256]{1,0:T(8,128)S(1)}, f32[256,256]{1,0:T(8,128)S(1)}, u32[]{:S(2)}, u32[]{:S(2)}) collective-permute-start(f32[256,256]{1,0:T(8,128)S(1)} %get-tuple-element.80), channel_id=1, source_target_pairs={{0,4},{1,5},{2,6},{3,7},{4,8},{5,9},{6,10},{7,11},{8,12},{9,13},{1... | collective-permute-start | bytes 786440 | tf_op jit(solution)/shard_map/ppermute | solution.py:290
  8.1 17.6 %collective-permute-start.2 = (f32[256,256]{1,0:T(8,128)S(1)}, f32[256,256]{1,0:T(8,128)S(1)}, u32[]{:S(2)}, u32[]{:S(2)}) collective-permute-start(f32[256,256]{1,0:T(8,128)S(1)} %get-tuple-element.79), channel_id=1, source_target_pairs={{0,5},{1,4},{2,7},{3,6},{4,9},{5,8},{6,11},{7,10},{8,13},{9,12},{1... | collective-permute-start | bytes 786440 | tf_op jit(solution)/shard_map/ppermute | solution.py:290
  11.5 18.5 %collective-permute-start.1 = (f32[256,256]{1,0:T(8,128)S(1)}, f32[256,256]{1,0:T(8,128)S(1)}, u32[]{:S(2)}, u32[]{:S(2)}) collective-permute-start(f32[256,256]{1,0:T(8,128)S(1)} %get-tuple-element.78), channel_id=1, source_target_pairs={{0,4},{1,5},{2,6},{3,7},{4,8},{5,9},{6,10},{7,11},{8,12},{9,13},{1... | collective-permute-start | bytes 786440 | tf_op jit(solution)/shard_map/ppermute | solution.py:290
  15.5 21.4 %collective-permute-start = (f32[256,256]{1,0:T(8,128)S(1)}, f32[256,256]{1,0:T(8,128)S(1)}, u32[]{:S(2)}, u32[]{:S(2)}) collective-permute-start(f32[256,256]{1,0:T(8,128)S(1)} %get-tuple-element.77), channel_id=1, source_target_pairs={{0,5},{1,4},{2,7},{3,6},{4,9},{5,8},{6,11},{7,10},{8,13},{9,12},{1... | collective-permute-start | bytes 786440 | tf_op jit(solution)/shard_map/ppermute | solution.py:290
  19.8 21.4 %collective-permute-start.7 = (f32[256,256]{1,0:T(8,128)S(1)}, f32[256,256]{1,0:T(8,128)S(1)}, u32[]{:S(2)}, u32[]{:S(2)}) collective-permute-start(f32[256,256]{1,0:T(8,128)S(1)} %get-tuple-element.89), channel_id=1, source_target_pairs={{0,4},{1,5},{2,6},{3,7},{4,8},{5,9},{6,10},{7,11},{8,12},{9,13},{1... | collective-permute-start | bytes 786440 | tf_op jit(solution)/shard_map/ppermute | solution.py:290
  31.0 15.8 %collective-permute-start.6 = (f32[256,256]{1,0:T(8,128)S(1)}, f32[256,256]{1,0:T(8,128)S(1)}, u32[]{:S(2)}, u32[]{:S(2)}) collective-permute-start(f32[256,256]{1,0:T(8,128)S(1)} %get-tuple-element.88), channel_id=1, source_target_pairs={{0,4},{1,5},{2,6},{3,7},{4,8},{5,9},{6,10},{7,11},{8,12},{9,13},{1... | collective-permute-start | bytes 786440 | tf_op jit(solution)/shard_map/ppermute | solution.py:290
  31.1 21.4 %collective-permute-start.5 = (f32[256,256]{1,0:T(8,128)S(1)}, f32[256,256]{1,0:T(8,128)S(1)}, u32[]{:S(2)}, u32[]{:S(2)}) collective-permute-start(f32[256,256]{1,0:T(8,128)S(1)} %get-tuple-element.87), channel_id=1, source_target_pairs={{0,6},{1,7},{2,4},{3,5},{4,10},{5,11},{6,8},{7,9},{8,14},{9,15},{1... | collective-permute-start | bytes 786440 | tf_op jit(solution)/shard_map/ppermute | solution.py:290
  38.0 22.0 %collective-permute-start.4 = (f32[256,256]{1,0:T(8,128)S(1)}, f32[256,256]{1,0:T(8,128)S(1)}, u32[]{:S(2)}, u32[]{:S(2)}) collective-permute-start(f32[256,256]{1,0:T(8,128)S(1)} %get-tuple-element.86), channel_id=1, source_target_pairs={{0,6},{1,7},{2,4},{3,5},{4,10},{5,11},{6,8},{7,9},{8,14},{9,15},{1... | collective-permute-start | bytes 786440 | tf_op jit(solution)/shard_map/ppermute | solution.py:290
  42.3 22.1 %collective-permute-start.11 = (f32[256,256]{1,0:T(8,128)S(1)}, f32[256,256]{1,0:T(8,128)S(1)}, u32[]{:S(2)}, u32[]{:S(2)}) collective-permute-start(f32[256,256]{1,0:T(8,128)S(1)} %get-tuple-element.98), channel_id=1, source_target_pairs={{0,4},{1,5},{2,6},{3,7},{4,8},{5,9},{6,10},{7,11},{8,12},{9,13},{1... | collective-permute-start | bytes 786440 | tf_op jit(solution)/shard_map/ppermute | solution.py:290
  53.6 17.8 %collective-permute-start.10 = (f32[256,256]{1,0:T(8,128)S(1)}, f32[256,256]{1,0:T(8,128)S(1)}, u32[]{:S(2)}, u32[]{:S(2)}) collective-permute-start(f32[256,256]{1,0:T(8,128)S(1)} %get-tuple-element.97), channel_id=1, source_target_pairs={{0,5},{1,4},{2,7},{3,6},{4,9},{5,8},{6,11},{7,10},{8,13},{9,12},{1... | collective-permute-start | bytes 786440 | tf_op jit(solution)/shard_map/ppermute | solution.py:290
  57.7 17.9 %collective-permute-start.9 = (f32[256,256]{1,0:T(8,128)S(1)}, f32[256,256]{1,0:T(8,128)S(1)}, u32[]{:S(2)}, u32[]{:S(2)}) collective-permute-start(f32[256,256]{1,0:T(8,128)S(1)} %get-tuple-element.96), channel_id=1, source_target_pairs={{0,4},{1,5},{2,6},{3,7},{4,8},{5,9},{6,10},{7,11},{8,12},{9,13},{1... | collective-permute-start | bytes 786440 | tf_op jit(solution)/shard_map/ppermute | solution.py:290
  61.1 21.5 %collective-permute-start.8 = (f32[256,256]{1,0:T(8,128)S(1)}, f32[256,256]{1,0:T(8,128)S(1)}, u32[]{:S(2)}, u32[]{:S(2)}) collective-permute-start(f32[256,256]{1,0:T(8,128)S(1)} %get-tuple-element.95), channel_id=1, source_target_pairs={{0,5},{1,4},{2,7},{3,6},{4,9},{5,8},{6,11},{7,10},{8,13},{9,12},{1... | collective-permute-start | bytes 786440 | tf_op jit(solution)/shard_map/ppermute | solution.py:290
  65.4 21.4 %collective-permute-start.15 = (f32[256,256]{1,0:T(8,128)S(1)}, f32[256,256]{1,0:T(8,128)S(1)}, u32[]{:S(2)}, u32[]{:S(2)}) collective-permute-start(f32[256,256]{1,0:T(8,128)S(1)} %get-tuple-element.107), channel_id=1, source_target_pairs={{0,4},{1,5},{2,6},{3,7},{4,8},{5,9},{6,10},{7,11},{8,12},{9,13},{1... | collective-permute-start | bytes 786440 | tf_op jit(solution)/shard_map/ppermute | solution.py:290
  76.6 15.8 %collective-permute-start.14 = (f32[256,256]{1,0:T(8,128)S(1)}, f32[256,256]{1,0:T(8,128)S(1)}, u32[]{:S(2)}, u32[]{:S(2)}) collective-permute-start(f32[256,256]{1,0:T(8,128)S(1)} %get-tuple-element.106), channel_id=1, source_target_pairs={{0,4},{1,5},{2,6},{3,7},{4,8},{5,9},{6,10},{7,11},{8,12},{9,13},{1... | collective-permute-start | bytes 786440 | tf_op jit(solution)/shard_map/ppermute | solution.py:290
  76.7 21.7 %collective-permute-start.13 = (f32[256,256]{1,0:T(8,128)S(1)}, f32[256,256]{1,0:T(8,128)S(1)}, u32[]{:S(2)}, u32[]{:S(2)}) collective-permute-start(f32[256,256]{1,0:T(8,128)S(1)} %get-tuple-element.105), channel_id=1, source_target_pairs={{0,6},{1,7},{2,4},{3,5},{4,10},{5,11},{6,8},{7,9},{8,14},{9,15},{1... | collective-permute-start | bytes 786440 | tf_op jit(solution)/shard_map/ppermute | solution.py:290
  83.6 22.3 %collective-permute-start.12 = (f32[256,256]{1,0:T(8,128)S(1)}, f32[256,256]{1,0:T(8,128)S(1)}, u32[]{:S(2)}, u32[]{:S(2)}) collective-permute-start(f32[256,256]{1,0:T(8,128)S(1)} %get-tuple-element.104), channel_id=1, source_target_pairs={{0,6},{1,7},{2,4},{3,5},{4,10},{5,11},{6,8},{7,9},{8,14},{9,15},{1... | collective-permute-start | bytes 786440 | tf_op jit(solution)/shard_map/ppermute | solution.py:290
  87.9 21.5 %collective-permute-start.19 = (f32[256,256]{1,0:T(8,128)S(1)}, f32[256,256]{1,0:T(8,128)S(1)}, u32[]{:S(2)}, u32[]{:S(2)}) collective-permute-start(f32[256,256]{1,0:T(8,128)S(1)} %get-tuple-element.116), channel_id=1, source_target_pairs={{0,4},{1,5},{2,6},{3,7},{4,8},{5,9},{6,10},{7,11},{8,12},{9,13},{1... | collective-permute-start | bytes 786440 | tf_op jit(solution)/shard_map/ppermute | solution.py:290
  99.4 17.0 %collective-permute-start.18 = (f32[256,256]{1,0:T(8,128)S(1)}, f32[256,256]{1,0:T(8,128)S(1)}, u32[]{:S(2)}, u32[]{:S(2)}) collective-permute-start(f32[256,256]{1,0:T(8,128)S(1)} %get-tuple-element.115), channel_id=1, source_target_pairs={{0,5},{1,4},{2,7},{3,6},{4,9},{5,8},{6,11},{7,10},{8,13},{9,12},{1... | collective-permute-start | bytes 786440 | tf_op jit(solution)/shard_map/ppermute | solution.py:290
  102.9 17.7 %collective-permute-start.17 = (f32[256,256]{1,0:T(8,128)S(1)}, f32[256,256]{1,0:T(8,128)S(1)}, u32[]{:S(2)}, u32[]{:S(2)}) collective-permute-start(f32[256,256]{1,0:T(8,128)S(1)} %get-tuple-element.114), channel_id=1, source_target_pairs={{0,4},{1,5},{2,6},{3,7},{4,8},{5,9},{6,10},{7,11},{8,12},{9,13},{1... | collective-permute-start | bytes 786440 | tf_op jit(solution)/shard_map/ppermute | solution.py:290
  107.0 19.8 %collective-permute-start.16 = (f32[256,256]{1,0:T(8,128)S(1)}, f32[256,256]{1,0:T(8,128)S(1)}, u32[]{:S(2)}, u32[]{:S(2)}) collective-permute-start(f32[256,256]{1,0:T(8,128)S(1)} %get-tuple-element.113), channel_id=1, source_target_pairs={{0,5},{1,4},{2,7},{3,6},{4,9},{5,8},{6,11},{7,10},{8,13},{9,12},{1... | collective-permute-start | bytes 786440 | tf_op jit(solution)/shard_map/ppermute | solution.py:290

commit v5 on v4

--- a/solution.py
+++ b/solution.py
@@ -110,7 +110,11 @@
     users_hbm, user_accum_hbm, items_hbm, item_accum_hbm = args[:4]
     users, user_accum, left_out, right_out, grad_out, *states = outs
     small, (raw, sems) = scratch[:6], scratch[6:]
-    copies = [pltpu.make_async_copy(src, dst, sems.at[n]) for n, (src, dst) in enumerate(zip(args[4:], small))]
+    copies = []
+    for n, (src, dst) in enumerate(zip(args[4:], small)):
+        if len(src.shape) == 3:
+            src, dst = src.at[pl.ds(0, 1)], dst.at[pl.ds(0, 1)]
+        copies.append(pltpu.make_async_copy(src, dst, sems.at[n]))
     copies.append(pltpu.make_async_copy(users_hbm, users, sems.at[6]))
     at = 7
     tile = ORDERS[0][0]
@@ -223,9 +227,11 @@
             copies.append(pltpu.make_async_copy(src, dst, sems.at[len(copies)]))
             copies[-1].start()
 
-        for n, other in zip([n for n in range(chunks) if n != chunk], others):
-            for part in range(2):
-                send(other.at[pl.ds(part * CHUNK, CHUNK)], outs[2 + part].at[pl.ds(n * CHUNK, CHUNK)])
+        def send_others():
+            for n, other in zip([n for n in range(chunks) if n != chunk], others):
+                for part in range(2):
+                    send(other.at[pl.ds(part * CHUNK, CHUNK)], outs[2 + part].at[pl.ds(n * CHUNK, CHUNK)])
+
     elif final:
         users_out, user_accum_out, state_out = refs
     else:
@@ -242,6 +248,8 @@
                 rows = pl.ds(at.start, STEP)
                 send(users_out.at[rows], outs[0].at[rows])
                 send(user_accum_out.at[rows], outs[1].at[rows])
+                if at.start == 0:
+                    send_others()
         else:
             grad_out[at, :] = grad
 

time: 129 us -> 129 us (level)
  no operation moved by 1% of the time
where the time goes in v5:
time: 129 us
  waiting for transfers between devices  66.3 us (51%)
  starting transfers between devices  32.6 us (25%)
  Pallas kernels  29.1 us (23%)
    ppermute x20, waiting for transfers between devices, move(): return lax.ppermute(state, AXES, pairs)  66.3 us
    ppermute x20, starting transfers between devices, move(): return lax.ppermute(state, AXES, pairs)  32.6 us
    pallas_call x23, Pallas kernels, run_chunk(): pl.pallas_call(functools.partial(chunk_kernel, s, chunk, first, final, ch...  25.2 us
  transfers between devices with their start and end apart: 20, of which 18 were waited for; matrix products, arithmetic and copies ran while one was open for 0% of the time, Pallas kernels for 19%

profile of v5, /device:TPU:1, one launch (start us, length us, event | category | flops | bytes accessed | tf_op | source)
XLA Modules:
  0.0 129.1 jit_solution(2413537823516626978)
XLA Ops:
  0.6 2.6 %first_chunk.1 = (f32[1024,256]{1,0:T(8,128)S(1)}, f32[1024,256]{1,0:T(8,128)S(1)}, bf16[1024,32]{1,0:T(8,128)(2,1)S(1)}, bf16[4,32,256]{2,1,0:T(8,128)(2,1)S(1)...) custom-call(f32[1024,256]{1,0:T(8,128)} %refs_0_.2, ...), custom_call_target="tpu_custom_call" | custom-call | tf_op jit(solution)/shard_map/first_chunk/pallas_call | solution.py:167
  3.2 3.8 %collective-permute-start.3 = (f32[256,256]{1,0:T(8,128)S(1)}, f32[256,256]{1,0:T(8,128)S(1)}, u32[]{:S(2)}, u32[]{:S(2)}) collective-permute-start(f32[256,256]{1,0:T(8,128)S(1)} %get-tuple-element.80), channel_id=1, source_target_pairs={{0,4},{1,5},{2,6},{3,7},{4,8},{5,9},{6,10},{7,11},{8,12},{9,13},{1... | collective-permute-start | bytes 786440 | tf_op jit(solution)/shard_map/ppermute | solution.py:298
  8.1 2.3 %collective-permute-start.2 = (f32[256,256]{1,0:T(8,128)S(1)}, f32[256,256]{1,0:T(8,128)S(1)}, u32[]{:S(2)}, u32[]{:S(2)}) collective-permute-start(f32[256,256]{1,0:T(8,128)S(1)} %get-tuple-element.79), channel_id=1, source_target_pairs={{0,5},{1,4},{2,7},{3,6},{4,9},{5,8},{6,11},{7,10},{8,13},{9,12},{1... | collective-permute-start | bytes 786440 | tf_op jit(solution)/shard_map/ppermute | solution.py:298
  11.4 3.0 %collective-permute-start.1 = (f32[256,256]{1,0:T(8,128)S(1)}, f32[256,256]{1,0:T(8,128)S(1)}, u32[]{:S(2)}, u32[]{:S(2)}) collective-permute-start(f32[256,256]{1,0:T(8,128)S(1)} %get-tuple-element.78), channel_id=1, source_target_pairs={{0,4},{1,5},{2,6},{3,7},{4,8},{5,9},{6,10},{7,11},{8,12},{9,13},{1... | collective-permute-start | bytes 786440 | tf_op jit(solution)/shard_map/ppermute | solution.py:298
  19.8 2.4 %collective-permute-start.7 = (f32[256,256]{1,0:T(8,128)S(1)}, f32[256,256]{1,0:T(8,128)S(1)}, u32[]{:S(2)}, u32[]{:S(2)}) collective-permute-start(f32[256,256]{1,0:T(8,128)S(1)} %get-tuple-element.89), channel_id=1, source_target_pairs={{0,4},{1,5},{2,6},{3,7},{4,8},{5,9},{6,10},{7,11},{8,12},{9,13},{1... | collective-permute-start | bytes 786440 | tf_op jit(solution)/shard_map/ppermute | solution.py:298
  22.1 3.6 %collective-permute-done.2.refs_3_ = f32[256,256]{1,0:T(8,128)S(1)} collective-permute-done((f32[256,256]{1,0:T(8,128)S(1)}, f32[256,256]{1,0:T(8,128)S(1)}, u32[]{:S(2)}, u32[]{:S(2)}) %collective-permute-start.2) | collective-permute-done | bytes 262176 | tf_op jit(solution)/shard_map/ppermute | solution.py:298
  26.8 3.2 %collective-permute-done.1.refs_3_ = f32[256,256]{1,0:T(8,128)S(1)} collective-permute-done((f32[256,256]{1,0:T(8,128)S(1)}, f32[256,256]{1,0:T(8,128)S(1)}, u32[]{:S(2)}, u32[]{:S(2)}) %collective-permute-start.1) | collective-permute-done | bytes 262176 | tf_op jit(solution)/shard_map/ppermute | solution.py:298
  31.2 5.8 %collective-permute-done.refs_3_ = f32[256,256]{1,0:T(8,128)S(1)} collective-permute-done((f32[256,256]{1,0:T(8,128)S(1)}, f32[256,256]{1,0:T(8,128)S(1)}, u32[]{:S(2)}, u32[]{:S(2)}) %collective-permute-start) | collective-permute-done | bytes 262176 | tf_op jit(solution)/shard_map/ppermute | solution.py:298
  38.1 3.1 %collective-permute-done.7.refs_3_ = f32[256,256]{1,0:T(8,128)S(1)} collective-permute-done((f32[256,256]{1,0:T(8,128)S(1)}, f32[256,256]{1,0:T(8,128)S(1)}, u32[]{:S(2)}, u32[]{:S(2)}) %collective-permute-start.7) | collective-permute-done | bytes 262176 | tf_op jit(solution)/shard_map/ppermute | solution.py:298
  42.5 4.3 %collective-permute-done.6.refs_3_ = f32[256,256]{1,0:T(8,128)S(1)} collective-permute-done((f32[256,256]{1,0:T(8,128)S(1)}, f32[256,256]{1,0:T(8,128)S(1)}, u32[]{:S(2)}, u32[]{:S(2)}) %collective-permute-start.6) | collective-permute-done | bytes 262176 | tf_op jit(solution)/shard_map/ppermute | solution.py:298
  47.9 4.6 %collective-permute-done.5.refs_3_ = f32[256,256]{1,0:T(8,128)S(1)} collective-permute-done((f32[256,256]{1,0:T(8,128)S(1)}, f32[256,256]{1,0:T(8,128)S(1)}, u32[]{:S(2)}, u32[]{:S(2)}) %collective-permute-start.5) | collective-permute-done | bytes 262176 | tf_op jit(solution)/shard_map/ppermute | solution.py:298
  53.5 4.1 %collective-permute-start.10 = (f32[256,256]{1,0:T(8,128)S(1)}, f32[256,256]{1,0:T(8,128)S(1)}, u32[]{:S(2)}, u32[]{:S(2)}) collective-permute-start(f32[256,256]{1,0:T(8,128)S(1)} %get-tuple-element.97), channel_id=1, source_target_pairs={{0,5},{1,4},{2,7},{3,6},{4,9},{5,8},{6,11},{7,10},{8,13},{9,12},{1... | collective-permute-start | bytes 786440 | tf_op jit(solution)/shard_map/ppermute | solution.py:298
  57.7 2.3 %collective-permute-start.9 = (f32[256,256]{1,0:T(8,128)S(1)}, f32[256,256]{1,0:T(8,128)S(1)}, u32[]{:S(2)}, u32[]{:S(2)}) collective-permute-start(f32[256,256]{1,0:T(8,128)S(1)} %get-tuple-element.96), channel_id=1, source_target_pairs={{0,4},{1,5},{2,6},{3,7},{4,8},{5,9},{6,10},{7,11},{8,12},{9,13},{1... | collective-permute-start | bytes 786440 | tf_op jit(solution)/shard_map/ppermute | solution.py:298
  66.7 4.7 %collective-permute-done.10.refs_3_ = f32[256,256]{1,0:T(8,128)S(1)} collective-permute-done((f32[256,256]{1,0:T(8,128)S(1)}, f32[256,256]{1,0:T(8,128)S(1)}, u32[]{:S(2)}, u32[]{:S(2)}) %collective-permute-start.10) | collective-permute-done | bytes 262176 | tf_op jit(solution)/shard_map/ppermute | solution.py:298
  72.4 3.2 %collective-permute-done.9.refs_3_ = f32[256,256]{1,0:T(8,128)S(1)} collective-permute-done((f32[256,256]{1,0:T(8,128)S(1)}, f32[256,256]{1,0:T(8,128)S(1)}, u32[]{:S(2)}, u32[]{:S(2)}) %collective-permute-start.9) | collective-permute-done | bytes 262176 | tf_op jit(solution)/shard_map/ppermute | solution.py:298
  78.1 4.5 %collective-permute-done.8.refs_3_ = f32[256,256]{1,0:T(8,128)S(1)} collective-permute-done((f32[256,256]{1,0:T(8,128)S(1)}, f32[256,256]{1,0:T(8,128)S(1)}, u32[]{:S(2)}, u32[]{:S(2)}) %collective-permute-start.8) | collective-permute-done | bytes 262176 | tf_op jit(solution)/shard_map/ppermute | solution.py:298
  83.7 3.1 %collective-permute-done.15.refs_3_ = f32[256,256]{1,0:T(8,128)S(1)} collective-permute-done((f32[256,256]{1,0:T(8,128)S(1)}, f32[256,256]{1,0:T(8,128)S(1)}, u32[]{:S(2)}, u32[]{:S(2)}) %collective-permute-start.15) | collective-permute-done | bytes 262176 | tf_op jit(solution)/shard_map/ppermute | solution.py:298
  87.9 4.5 %collective-permute-done.14.refs_3_ = f32[256,256]{1,0:T(8,128)S(1)} collective-permute-done((f32[256,256]{1,0:T(8,128)S(1)}, f32[256,256]{1,0:T(8,128)S(1)}, u32[]{:S(2)}, u32[]{:S(2)}) %collective-permute-start.14) | collective-permute-done | bytes 262176 | tf_op jit(solution)/shard_map/ppermute | solution.py:298
  93.5 4.9 %collective-permute-done.13.refs_3_ = f32[256,256]{1,0:T(8,128)S(1)} collective-permute-done((f32[256,256]{1,0:T(8,128)S(1)}, f32[256,256]{1,0:T(8,128)S(1)}, u32[]{:S(2)}, u32[]{:S(2)}) %collective-permute-start.13) | collective-permute-done | bytes 262176 | tf_op jit(solution)/shard_map/ppermute | solution.py:298
  99.4 3.5 %collective-permute-start.18 = (f32[256,256]{1,0:T(8,128)S(1)}, f32[256,256]{1,0:T(8,128)S(1)}, u32[]{:S(2)}, u32[]{:S(2)}) collective-permute-start(f32[256,256]{1,0:T(8,128)S(1)} %get-tuple-element.115), channel_id=1, source_target_pairs={{0,5},{1,4},{2,7},{3,6},{4,9},{5,8},{6,11},{7,10},{8,13},{9,12},{1... | collective-permute-start | bytes 786440 | tf_op jit(solution)/shard_map/ppermute | solution.py:298
  102.9 3.0 %collective-permute-start.17 = (f32[256,256]{1,0:T(8,128)S(1)}, f32[256,256]{1,0:T(8,128)S(1)}, u32[]{:S(2)}, u32[]{:S(2)}) collective-permute-start(f32[256,256]{1,0:T(8,128)S(1)} %get-tuple-element.114), channel_id=1, source_target_pairs={{0,4},{1,5},{2,6},{3,7},{4,8},{5,9},{6,10},{7,11},{8,12},{9,13},{1... | collective-permute-start | bytes 786440 | tf_op jit(solution)/shard_map/ppermute | solution.py:298
  110.4 5.9 %collective-permute-done.18.refs_3_ = f32[256,256]{1,0:T(8,128)S(1)} collective-permute-done((f32[256,256]{1,0:T(8,128)S(1)}, f32[256,256]{1,0:T(8,128)S(1)}, u32[]{:S(2)}, u32[]{:S(2)}) %collective-permute-start.18) | collective-permute-done | bytes 262176 | tf_op jit(solution)/shard_map/ppermute | solution.py:298
  117.4 3.2 %collective-permute-done.17.refs_3_ = f32[256,256]{1,0:T(8,128)S(1)} collective-permute-done((f32[256,256]{1,0:T(8,128)S(1)}, f32[256,256]{1,0:T(8,128)S(1)}, u32[]{:S(2)}, u32[]{:S(2)}) %collective-permute-start.17) | collective-permute-done | bytes 262176 | tf_op jit(solution)/shard_map/ppermute | solution.py:298
  121.7 5.1 %collective-permute-done.16.refs_3_ = f32[256,256]{1,0:T(8,128)S(1)} collective-permute-done((f32[256,256]{1,0:T(8,128)S(1)}, f32[256,256]{1,0:T(8,128)S(1)}, u32[]{:S(2)}, u32[]{:S(2)}) %collective-permute-start.16) | collective-permute-done | bytes 262176 | tf_op jit(solution)/shard_map/ppermute | solution.py:298
  (41 shorter events, 37.4 us)
Async XLA Ops:
  3.2 15.5 %collective-permute-start.3 = (f32[256,256]{1,0:T(8,128)S(1)}, f32[256,256]{1,0:T(8,128)S(1)}, u32[]{:S(2)}, u32[]{:S(2)}) collective-permute-start(f32[256,256]{1,0:T(8,128)S(1)} %get-tuple-element.80), channel_id=1, source_target_pairs={{0,4},{1,5},{2,6},{3,7},{4,8},{5,9},{6,10},{7,11},{8,12},{9,13},{1... | collective-permute-start | bytes 786440 | tf_op jit(solution)/shard_map/ppermute | solution.py:298
  8.1 17.6 %collective-permute-start.2 = (f32[256,256]{1,0:T(8,128)S(1)}, f32[256,256]{1,0:T(8,128)S(1)}, u32[]{:S(2)}, u32[]{:S(2)}) collective-permute-start(f32[256,256]{1,0:T(8,128)S(1)} %get-tuple-element.79), channel_id=1, source_target_pairs={{0,5},{1,4},{2,7},{3,6},{4,9},{5,8},{6,11},{7,10},{8,13},{9,12},{1... | collective-permute-start | bytes 786440 | tf_op jit(solution)/shard_map/ppermute | solution.py:298
  11.4 18.5 %collective-permute-start.1 = (f32[256,256]{1,0:T(8,128)S(1)}, f32[256,256]{1,0:T(8,128)S(1)}, u32[]{:S(2)}, u32[]{:S(2)}) collective-permute-start(f32[256,256]{1,0:T(8,128)S(1)} %get-tuple-element.78), channel_id=1, source_target_pairs={{0,4},{1,5},{2,6},{3,7},{4,8},{5,9},{6,10},{7,11},{8,12},{9,13},{1... | collective-permute-start | bytes 786440 | tf_op jit(solution)/shard_map/ppermute | solution.py:298
  15.5 21.4 %collective-permute-start = (f32[256,256]{1,0:T(8,128)S(1)}, f32[256,256]{1,0:T(8,128)S(1)}, u32[]{:S(2)}, u32[]{:S(2)}) collective-permute-start(f32[256,256]{1,0:T(8,128)S(1)} %get-tuple-element.77), channel_id=1, source_target_pairs={{0,5},{1,4},{2,7},{3,6},{4,9},{5,8},{6,11},{7,10},{8,13},{9,12},{1... | collective-permute-start | bytes 786440 | tf_op jit(solution)/shard_map/ppermute | solution.py:298
  19.8 21.4 %collective-permute-start.7 = (f32[256,256]{1,0:T(8,128)S(1)}, f32[256,256]{1,0:T(8,128)S(1)}, u32[]{:S(2)}, u32[]{:S(2)}) collective-permute-start(f32[256,256]{1,0:T(8,128)S(1)} %get-tuple-element.89), channel_id=1, source_target_pairs={{0,4},{1,5},{2,6},{3,7},{4,8},{5,9},{6,10},{7,11},{8,12},{9,13},{1... | collective-permute-start | bytes 786440 | tf_op jit(solution)/shard_map/ppermute | solution.py:298
  31.0 15.8 %collective-permute-start.6 = (f32[256,256]{1,0:T(8,128)S(1)}, f32[256,256]{1,0:T(8,128)S(1)}, u32[]{:S(2)}, u32[]{:S(2)}) collective-permute-start(f32[256,256]{1,0:T(8,128)S(1)} %get-tuple-element.88), channel_id=1, source_target_pairs={{0,4},{1,5},{2,6},{3,7},{4,8},{5,9},{6,10},{7,11},{8,12},{9,13},{1... | collective-permute-start | bytes 786440 | tf_op jit(solution)/shard_map/ppermute | solution.py:298
  31.1 21.4 %collective-permute-start.5 = (f32[256,256]{1,0:T(8,128)S(1)}, f32[256,256]{1,0:T(8,128)S(1)}, u32[]{:S(2)}, u32[]{:S(2)}) collective-permute-start(f32[256,256]{1,0:T(8,128)S(1)} %get-tuple-element.87), channel_id=1, source_target_pairs={{0,6},{1,7},{2,4},{3,5},{4,10},{5,11},{6,8},{7,9},{8,14},{9,15},{1... | collective-permute-start | bytes 786440 | tf_op jit(solution)/shard_map/ppermute | solution.py:298
  38.0 22.0 %collective-permute-start.4 = (f32[256,256]{1,0:T(8,128)S(1)}, f32[256,256]{1,0:T(8,128)S(1)}, u32[]{:S(2)}, u32[]{:S(2)}) collective-permute-start(f32[256,256]{1,0:T(8,128)S(1)} %get-tuple-element.86), channel_id=1, source_target_pairs={{0,6},{1,7},{2,4},{3,5},{4,10},{5,11},{6,8},{7,9},{8,14},{9,15},{1... | collective-permute-start | bytes 786440 | tf_op jit(solution)/shard_map/ppermute | solution.py:298
  42.2 22.1 %collective-permute-start.11 = (f32[256,256]{1,0:T(8,128)S(1)}, f32[256,256]{1,0:T(8,128)S(1)}, u32[]{:S(2)}, u32[]{:S(2)}) collective-permute-start(f32[256,256]{1,0:T(8,128)S(1)} %get-tuple-element.98), channel_id=1, source_target_pairs={{0,4},{1,5},{2,6},{3,7},{4,8},{5,9},{6,10},{7,11},{8,12},{9,13},{1... | collective-permute-start | bytes 786440 | tf_op jit(solution)/shard_map/ppermute | solution.py:298
  53.5 17.8 %collective-permute-start.10 = (f32[256,256]{1,0:T(8,128)S(1)}, f32[256,256]{1,0:T(8,128)S(1)}, u32[]{:S(2)}, u32[]{:S(2)}) collective-permute-start(f32[256,256]{1,0:T(8,128)S(1)} %get-tuple-element.97), channel_id=1, source_target_pairs={{0,5},{1,4},{2,7},{3,6},{4,9},{5,8},{6,11},{7,10},{8,13},{9,12},{1... | collective-permute-start | bytes 786440 | tf_op jit(solution)/shard_map/ppermute | solution.py:298
  57.7 17.9 %collective-permute-start.9 = (f32[256,256]{1,0:T(8,128)S(1)}, f32[256,256]{1,0:T(8,128)S(1)}, u32[]{:S(2)}, u32[]{:S(2)}) collective-permute-start(f32[256,256]{1,0:T(8,128)S(1)} %get-tuple-element.96), channel_id=1, source_target_pairs={{0,4},{1,5},{2,6},{3,7},{4,8},{5,9},{6,10},{7,11},{8,12},{9,13},{1... | collective-permute-start | bytes 786440 | tf_op jit(solution)/shard_map/ppermute | solution.py:298
  61.0 21.5 %collective-permute-start.8 = (f32[256,256]{1,0:T(8,128)S(1)}, f32[256,256]{1,0:T(8,128)S(1)}, u32[]{:S(2)}, u32[]{:S(2)}) collective-permute-start(f32[256,256]{1,0:T(8,128)S(1)} %get-tuple-element.95), channel_id=1, source_target_pairs={{0,5},{1,4},{2,7},{3,6},{4,9},{5,8},{6,11},{7,10},{8,13},{9,12},{1... | collective-permute-start | bytes 786440 | tf_op jit(solution)/shard_map/ppermute | solution.py:298
  65.4 21.4 %collective-permute-start.15 = (f32[256,256]{1,0:T(8,128)S(1)}, f32[256,256]{1,0:T(8,128)S(1)}, u32[]{:S(2)}, u32[]{:S(2)}) collective-permute-start(f32[256,256]{1,0:T(8,128)S(1)} %get-tuple-element.107), channel_id=1, source_target_pairs={{0,4},{1,5},{2,6},{3,7},{4,8},{5,9},{6,10},{7,11},{8,12},{9,13},{1... | collective-permute-start | bytes 786440 | tf_op jit(solution)/shard_map/ppermute | solution.py:298
  76.6 15.8 %collective-permute-start.14 = (f32[256,256]{1,0:T(8,128)S(1)}, f32[256,256]{1,0:T(8,128)S(1)}, u32[]{:S(2)}, u32[]{:S(2)}) collective-permute-start(f32[256,256]{1,0:T(8,128)S(1)} %get-tuple-element.106), channel_id=1, source_target_pairs={{0,4},{1,5},{2,6},{3,7},{4,8},{5,9},{6,10},{7,11},{8,12},{9,13},{1... | collective-permute-start | bytes 786440 | tf_op jit(solution)/shard_map/ppermute | solution.py:298
  76.7 21.7 %collective-permute-start.13 = (f32[256,256]{1,0:T(8,128)S(1)}, f32[256,256]{1,0:T(8,128)S(1)}, u32[]{:S(2)}, u32[]{:S(2)}) collective-permute-start(f32[256,256]{1,0:T(8,128)S(1)} %get-tuple-element.105), channel_id=1, source_target_pairs={{0,6},{1,7},{2,4},{3,5},{4,10},{5,11},{6,8},{7,9},{8,14},{9,15},{1... | collective-permute-start | bytes 786440 | tf_op jit(solution)/shard_map/ppermute | solution.py:298
  83.6 22.3 %collective-permute-start.12 = (f32[256,256]{1,0:T(8,128)S(1)}, f32[256,256]{1,0:T(8,128)S(1)}, u32[]{:S(2)}, u32[]{:S(2)}) collective-permute-start(f32[256,256]{1,0:T(8,128)S(1)} %get-tuple-element.104), channel_id=1, source_target_pairs={{0,6},{1,7},{2,4},{3,5},{4,10},{5,11},{6,8},{7,9},{8,14},{9,15},{1... | collective-permute-start | bytes 786440 | tf_op jit(solution)/shard_map/ppermute | solution.py:298
  87.8 21.5 %collective-permute-start.19 = (f32[256,256]{1,0:T(8,128)S(1)}, f32[256,256]{1,0:T(8,128)S(1)}, u32[]{:S(2)}, u32[]{:S(2)}) collective-permute-start(f32[256,256]{1,0:T(8,128)S(1)} %get-tuple-element.116), channel_id=1, source_target_pairs={{0,4},{1,5},{2,6},{3,7},{4,8},{5,9},{6,10},{7,11},{8,12},{9,13},{1... | collective-permute-start | bytes 786440 | tf_op jit(solution)/shard_map/ppermute | solution.py:298
  99.4 17.0 %collective-permute-start.18 = (f32[256,256]{1,0:T(8,128)S(1)}, f32[256,256]{1,0:T(8,128)S(1)}, u32[]{:S(2)}, u32[]{:S(2)}) collective-permute-start(f32[256,256]{1,0:T(8,128)S(1)} %get-tuple-element.115), channel_id=1, source_target_pairs={{0,5},{1,4},{2,7},{3,6},{4,9},{5,8},{6,11},{7,10},{8,13},{9,12},{1... | collective-permute-start | bytes 786440 | tf_op jit(solution)/shard_map/ppermute | solution.py:298
  102.9 17.7 %collective-permute-start.17 = (f32[256,256]{1,0:T(8,128)S(1)}, f32[256,256]{1,0:T(8,128)S(1)}, u32[]{:S(2)}, u32[]{:S(2)}) collective-permute-start(f32[256,256]{1,0:T(8,128)S(1)} %get-tuple-element.114), channel_id=1, source_target_pairs={{0,4},{1,5},{2,6},{3,7},{4,8},{5,9},{6,10},{7,11},{8,12},{9,13},{1... | collective-permute-start | bytes 786440 | tf_op jit(solution)/shard_map/ppermute | solution.py:298
  107.0 19.8 %collective-permute-start.16 = (f32[256,256]{1,0:T(8,128)S(1)}, f32[256,256]{1,0:T(8,128)S(1)}, u32[]{:S(2)}, u32[]{:S(2)}) collective-permute-start(f32[256,256]{1,0:T(8,128)S(1)} %get-tuple-element.113), channel_id=1, source_target_pairs={{0,5},{1,4},{2,7},{3,6},{4,9},{5,8},{6,11},{7,10},{8,13},{9,12},{1... | collective-permute-start | bytes 786440 | tf_op jit(solution)/shard_map/ppermute | solution.py:298

commit v6 on v4

--- a/solution.py
+++ b/solution.py
@@ -110,7 +110,11 @@
     users_hbm, user_accum_hbm, items_hbm, item_accum_hbm = args[:4]
     users, user_accum, left_out, right_out, grad_out, *states = outs
     small, (raw, sems) = scratch[:6], scratch[6:]
-    copies = [pltpu.make_async_copy(src, dst, sems.at[n]) for n, (src, dst) in enumerate(zip(args[4:], small))]
+    copies = []
+    for n, (src, dst) in enumerate(zip(args[4:], small)):
+        if len(src.shape) == 3:
+            src, dst = src.at[pl.ds(0, 1)], dst.at[pl.ds(0, 1)]
+        copies.append(pltpu.make_async_copy(src, dst, sems.at[n]))
     copies.append(pltpu.make_async_copy(users_hbm, users, sems.at[6]))
     at = 7
     tile = ORDERS[0][0]

time: 129 us -> 129 us (level)
  no operation moved by 1% of the time
where the time goes in v6:
time: 129 us
  waiting for transfers between devices  66.3 us (51%)
  starting transfers between devices  32.6 us (25%)
  Pallas kernels  29 us (22%)
    ppermute x20, waiting for transfers between devices, move(): return lax.ppermute(state, AXES, pairs)  66.3 us
    ppermute x20, starting transfers between devices, move(): return lax.ppermute(state, AXES, pairs)  32.6 us
    pallas_call x23, Pallas kernels, run_chunk(): pl.pallas_call(functools.partial(chunk_kernel, s, chunk, first, final, ch...  25 us
  transfers between devices with their start and end apart: 20, of which 18 were waited for; matrix products, arithmetic and copies ran while one was open for 0% of the time, Pallas kernels for 19%

profile of v6, /device:TPU:1, one launch (start us, length us, event | category | flops | bytes accessed | tf_op | source)
XLA Modules:
  0.0 129.0 jit_solution(8909632212628944291)
XLA Ops:
  0.6 2.6 %first_chunk.1 = (f32[1024,256]{1,0:T(8,128)S(1)}, f32[1024,256]{1,0:T(8,128)S(1)}, bf16[1024,32]{1,0:T(8,128)(2,1)S(1)}, bf16[4,32,256]{2,1,0:T(8,128)(2,1)S(1)...) custom-call(f32[1024,256]{1,0:T(8,128)} %refs_0_.2, ...), custom_call_target="tpu_custom_call" | custom-call | tf_op jit(solution)/shard_map/first_chunk/pallas_call | solution.py:167
  3.2 3.8 %collective-permute-start.3 = (f32[256,256]{1,0:T(8,128)S(1)}, f32[256,256]{1,0:T(8,128)S(1)}, u32[]{:S(2)}, u32[]{:S(2)}) collective-permute-start(f32[256,256]{1,0:T(8,128)S(1)} %get-tuple-element.80), channel_id=1, source_target_pairs={{0,4},{1,5},{2,6},{3,7},{4,8},{5,9},{6,10},{7,11},{8,12},{9,13},{1... | collective-permute-start | bytes 786440 | tf_op jit(solution)/shard_map/ppermute | solution.py:294
  8.1 2.3 %collective-permute-start.2 = (f32[256,256]{1,0:T(8,128)S(1)}, f32[256,256]{1,0:T(8,128)S(1)}, u32[]{:S(2)}, u32[]{:S(2)}) collective-permute-start(f32[256,256]{1,0:T(8,128)S(1)} %get-tuple-element.79), channel_id=1, source_target_pairs={{0,5},{1,4},{2,7},{3,6},{4,9},{5,8},{6,11},{7,10},{8,13},{9,12},{1... | collective-permute-start | bytes 786440 | tf_op jit(solution)/shard_map/ppermute | solution.py:294
  11.4 3.0 %collective-permute-start.1 = (f32[256,256]{1,0:T(8,128)S(1)}, f32[256,256]{1,0:T(8,128)S(1)}, u32[]{:S(2)}, u32[]{:S(2)}) collective-permute-start(f32[256,256]{1,0:T(8,128)S(1)} %get-tuple-element.78), channel_id=1, source_target_pairs={{0,4},{1,5},{2,6},{3,7},{4,8},{5,9},{6,10},{7,11},{8,12},{9,13},{1... | collective-permute-start | bytes 786440 | tf_op jit(solution)/shard_map/ppermute | solution.py:294
  19.8 2.4 %collective-permute-start.7 = (f32[256,256]{1,0:T(8,128)S(1)}, f32[256,256]{1,0:T(8,128)S(1)}, u32[]{:S(2)}, u32[]{:S(2)}) collective-permute-start(f32[256,256]{1,0:T(8,128)S(1)} %get-tuple-element.89), channel_id=1, source_target_pairs={{0,4},{1,5},{2,6},{3,7},{4,8},{5,9},{6,10},{7,11},{8,12},{9,13},{1... | collective-permute-start | bytes 786440 | tf_op jit(solution)/shard_map/ppermute | solution.py:294
  22.1 3.6 %collective-permute-done.2.refs_3_ = f32[256,256]{1,0:T(8,128)S(1)} collective-permute-done((f32[256,256]{1,0:T(8,128)S(1)}, f32[256,256]{1,0:T(8,128)S(1)}, u32[]{:S(2)}, u32[]{:S(2)}) %collective-permute-start.2) | collective-permute-done | bytes 262176 | tf_op jit(solution)/shard_map/ppermute | solution.py:294
  26.8 3.2 %collective-permute-done.1.refs_3_ = f32[256,256]{1,0:T(8,128)S(1)} collective-permute-done((f32[256,256]{1,0:T(8,128)S(1)}, f32[256,256]{1,0:T(8,128)S(1)}, u32[]{:S(2)}, u32[]{:S(2)}) %collective-permute-start.1) | collective-permute-done | bytes 262176 | tf_op jit(solution)/shard_map/ppermute | solution.py:294
  31.2 5.8 %collective-permute-done.refs_3_ = f32[256,256]{1,0:T(8,128)S(1)} collective-permute-done((f32[256,256]{1,0:T(8,128)S(1)}, f32[256,256]{1,0:T(8,128)S(1)}, u32[]{:S(2)}, u32[]{:S(2)}) %collective-permute-start) | collective-permute-done | bytes 262176 | tf_op jit(solution)/shard_map/ppermute | solution.py:294
  38.1 3.1 %collective-permute-done.7.refs_3_ = f32[256,256]{1,0:T(8,128)S(1)} collective-permute-done((f32[256,256]{1,0:T(8,128)S(1)}, f32[256,256]{1,0:T(8,128)S(1)}, u32[]{:S(2)}, u32[]{:S(2)}) %collective-permute-start.7) | collective-permute-done | bytes 262176 | tf_op jit(solution)/shard_map/ppermute | solution.py:294
  42.5 4.3 %collective-permute-done.6.refs_3_ = f32[256,256]{1,0:T(8,128)S(1)} collective-permute-done((f32[256,256]{1,0:T(8,128)S(1)}, f32[256,256]{1,0:T(8,128)S(1)}, u32[]{:S(2)}, u32[]{:S(2)}) %collective-permute-start.6) | collective-permute-done | bytes 262176 | tf_op jit(solution)/shard_map/ppermute | solution.py:294
  47.9 4.6 %collective-permute-done.5.refs_3_ = f32[256,256]{1,0:T(8,128)S(1)} collective-permute-done((f32[256,256]{1,0:T(8,128)S(1)}, f32[256,256]{1,0:T(8,128)S(1)}, u32[]{:S(2)}, u32[]{:S(2)}) %collective-permute-start.5) | collective-permute-done | bytes 262176 | tf_op jit(solution)/shard_map/ppermute | solution.py:294
  53.5 4.1 %collective-permute-start.10 = (f32[256,256]{1,0:T(8,128)S(1)}, f32[256,256]{1,0:T(8,128)S(1)}, u32[]{:S(2)}, u32[]{:S(2)}) collective-permute-start(f32[256,256]{1,0:T(8,128)S(1)} %get-tuple-element.97), channel_id=1, source_target_pairs={{0,5},{1,4},{2,7},{3,6},{4,9},{5,8},{6,11},{7,10},{8,13},{9,12},{1... | collective-permute-start | bytes 786440 | tf_op jit(solution)/shard_map/ppermute | solution.py:294
  57.7 2.3 %collective-permute-start.9 = (f32[256,256]{1,0:T(8,128)S(1)}, f32[256,256]{1,0:T(8,128)S(1)}, u32[]{:S(2)}, u32[]{:S(2)}) collective-permute-start(f32[256,256]{1,0:T(8,128)S(1)} %get-tuple-element.96), channel_id=1, source_target_pairs={{0,4},{1,5},{2,6},{3,7},{4,8},{5,9},{6,10},{7,11},{8,12},{9,13},{1... | collective-permute-start | bytes 786440 | tf_op jit(solution)/shard_map/ppermute | solution.py:294
  66.7 4.7 %collective-permute-done.10.refs_3_ = f32[256,256]{1,0:T(8,128)S(1)} collective-permute-done((f32[256,256]{1,0:T(8,128)S(1)}, f32[256,256]{1,0:T(8,128)S(1)}, u32[]{:S(2)}, u32[]{:S(2)}) %collective-permute-start.10) | collective-permute-done | bytes 262176 | tf_op jit(solution)/shard_map/ppermute | solution.py:294
  72.4 3.2 %collective-permute-done.9.refs_3_ = f32[256,256]{1,0:T(8,128)S(1)} collective-permute-done((f32[256,256]{1,0:T(8,128)S(1)}, f32[256,256]{1,0:T(8,128)S(1)}, u32[]{:S(2)}, u32[]{:S(2)}) %collective-permute-start.9) | collective-permute-done | bytes 262176 | tf_op jit(solution)/shard_map/ppermute | solution.py:294
  78.1 4.5 %collective-permute-done.8.refs_3_ = f32[256,256]{1,0:T(8,128)S(1)} collective-permute-done((f32[256,256]{1,0:T(8,128)S(1)}, f32[256,256]{1,0:T(8,128)S(1)}, u32[]{:S(2)}, u32[]{:S(2)}) %collective-permute-start.8) | collective-permute-done | bytes 262176 | tf_op jit(solution)/shard_map/ppermute | solution.py:294
  83.7 3.1 %collective-permute-done.15.refs_3_ = f32[256,256]{1,0:T(8,128)S(1)} collective-permute-done((f32[256,256]{1,0:T(8,128)S(1)}, f32[256,256]{1,0:T(8,128)S(1)}, u32[]{:S(2)}, u32[]{:S(2)}) %collective-permute-start.15) | collective-permute-done | bytes 262176 | tf_op jit(solution)/shard_map/ppermute | solution.py:294
  87.9 4.5 %collective-permute-done.14.refs_3_ = f32[256,256]{1,0:T(8,128)S(1)} collective-permute-done((f32[256,256]{1,0:T(8,128)S(1)}, f32[256,256]{1,0:T(8,128)S(1)}, u32[]{:S(2)}, u32[]{:S(2)}) %collective-permute-start.14) | collective-permute-done | bytes 262176 | tf_op jit(solution)/shard_map/ppermute | solution.py:294
  93.5 4.9 %collective-permute-done.13.refs_3_ = f32[256,256]{1,0:T(8,128)S(1)} collective-permute-done((f32[256,256]{1,0:T(8,128)S(1)}, f32[256,256]{1,0:T(8,128)S(1)}, u32[]{:S(2)}, u32[]{:S(2)}) %collective-permute-start.13) | collective-permute-done | bytes 262176 | tf_op jit(solution)/shard_map/ppermute | solution.py:294
  99.4 3.5 %collective-permute-start.18 = (f32[256,256]{1,0:T(8,128)S(1)}, f32[256,256]{1,0:T(8,128)S(1)}, u32[]{:S(2)}, u32[]{:S(2)}) collective-permute-start(f32[256,256]{1,0:T(8,128)S(1)} %get-tuple-element.115), channel_id=1, source_target_pairs={{0,5},{1,4},{2,7},{3,6},{4,9},{5,8},{6,11},{7,10},{8,13},{9,12},{1... | collective-permute-start | bytes 786440 | tf_op jit(solution)/shard_map/ppermute | solution.py:294
  102.9 3.0 %collective-permute-start.17 = (f32[256,256]{1,0:T(8,128)S(1)}, f32[256,256]{1,0:T(8,128)S(1)}, u32[]{:S(2)}, u32[]{:S(2)}) collective-permute-start(f32[256,256]{1,0:T(8,128)S(1)} %get-tuple-element.114), channel_id=1, source_target_pairs={{0,4},{1,5},{2,6},{3,7},{4,8},{5,9},{6,10},{7,11},{8,12},{9,13},{1... | collective-permute-start | bytes 786440 | tf_op jit(solution)/shard_map/ppermute | solution.py:294
  110.4 5.9 %collective-permute-done.18.refs_3_ = f32[256,256]{1,0:T(8,128)S(1)} collective-permute-done((f32[256,256]{1,0:T(8,128)S(1)}, f32[256,256]{1,0:T(8,128)S(1)}, u32[]{:S(2)}, u32[]{:S(2)}) %collective-permute-start.18) | collective-permute-done | bytes 262176 | tf_op jit(solution)/shard_map/ppermute | solution.py:294
  117.4 3.2 %collective-permute-done.17.refs_3_ = f32[256,256]{1,0:T(8,128)S(1)} collective-permute-done((f32[256,256]{1,0:T(8,128)S(1)}, f32[256,256]{1,0:T(8,128)S(1)}, u32[]{:S(2)}, u32[]{:S(2)}) %collective-permute-start.17) | collective-permute-done | bytes 262176 | tf_op jit(solution)/shard_map/ppermute | solution.py:294
  121.7 5.1 %collective-permute-done.16.refs_3_ = f32[256,256]{1,0:T(8,128)S(1)} collective-permute-done((f32[256,256]{1,0:T(8,128)S(1)}, f32[256,256]{1,0:T(8,128)S(1)}, u32[]{:S(2)}, u32[]{:S(2)}) %collective-permute-start.16) | collective-permute-done | bytes 262176 | tf_op jit(solution)/shard_map/ppermute | solution.py:294
  (41 shorter events, 37.3 us)
Async XLA Ops:
  3.2 15.5 %collective-permute-start.3 = (f32[256,256]{1,0:T(8,128)S(1)}, f32[256,256]{1,0:T(8,128)S(1)}, u32[]{:S(2)}, u32[]{:S(2)}) collective-permute-start(f32[256,256]{1,0:T(8,128)S(1)} %get-tuple-element.80), channel_id=1, source_target_pairs={{0,4},{1,5},{2,6},{3,7},{4,8},{5,9},{6,10},{7,11},{8,12},{9,13},{1... | collective-permute-start | bytes 786440 | tf_op jit(solution)/shard_map/ppermute | solution.py:294
  8.1 17.6 %collective-permute-start.2 = (f32[256,256]{1,0:T(8,128)S(1)}, f32[256,256]{1,0:T(8,128)S(1)}, u32[]{:S(2)}, u32[]{:S(2)}) collective-permute-start(f32[256,256]{1,0:T(8,128)S(1)} %get-tuple-element.79), channel_id=1, source_target_pairs={{0,5},{1,4},{2,7},{3,6},{4,9},{5,8},{6,11},{7,10},{8,13},{9,12},{1... | collective-permute-start | bytes 786440 | tf_op jit(solution)/shard_map/ppermute | solution.py:294
  11.4 18.5 %collective-permute-start.1 = (f32[256,256]{1,0:T(8,128)S(1)}, f32[256,256]{1,0:T(8,128)S(1)}, u32[]{:S(2)}, u32[]{:S(2)}) collective-permute-start(f32[256,256]{1,0:T(8,128)S(1)} %get-tuple-element.78), channel_id=1, source_target_pairs={{0,4},{1,5},{2,6},{3,7},{4,8},{5,9},{6,10},{7,11},{8,12},{9,13},{1... | collective-permute-start | bytes 786440 | tf_op jit(solution)/shard_map/ppermute | solution.py:294
  15.5 21.4 %collective-permute-start = (f32[256,256]{1,0:T(8,128)S(1)}, f32[256,256]{1,0:T(8,128)S(1)}, u32[]{:S(2)}, u32[]{:S(2)}) collective-permute-start(f32[256,256]{1,0:T(8,128)S(1)} %get-tuple-element.77), channel_id=1, source_target_pairs={{0,5},{1,4},{2,7},{3,6},{4,9},{5,8},{6,11},{7,10},{8,13},{9,12},{1... | collective-permute-start | bytes 786440 | tf_op jit(solution)/shard_map/ppermute | solution.py:294
  19.8 21.4 %collective-permute-start.7 = (f32[256,256]{1,0:T(8,128)S(1)}, f32[256,256]{1,0:T(8,128)S(1)}, u32[]{:S(2)}, u32[]{:S(2)}) collective-permute-start(f32[256,256]{1,0:T(8,128)S(1)} %get-tuple-element.89), channel_id=1, source_target_pairs={{0,4},{1,5},{2,6},{3,7},{4,8},{5,9},{6,10},{7,11},{8,12},{9,13},{1... | collective-permute-start | bytes 786440 | tf_op jit(solution)/shard_map/ppermute | solution.py:294
  31.0 15.8 %collective-permute-start.6 = (f32[256,256]{1,0:T(8,128)S(1)}, f32[256,256]{1,0:T(8,128)S(1)}, u32[]{:S(2)}, u32[]{:S(2)}) collective-permute-start(f32[256,256]{1,0:T(8,128)S(1)} %get-tuple-element.88), channel_id=1, source_target_pairs={{0,4},{1,5},{2,6},{3,7},{4,8},{5,9},{6,10},{7,11},{8,12},{9,13},{1... | collective-permute-start | bytes 786440 | tf_op jit(solution)/shard_map/ppermute | solution.py:294
  31.1 21.4 %collective-permute-start.5 = (f32[256,256]{1,0:T(8,128)S(1)}, f32[256,256]{1,0:T(8,128)S(1)}, u32[]{:S(2)}, u32[]{:S(2)}) collective-permute-start(f32[256,256]{1,0:T(8,128)S(1)} %get-tuple-element.87), channel_id=1, source_target_pairs={{0,6},{1,7},{2,4},{3,5},{4,10},{5,11},{6,8},{7,9},{8,14},{9,15},{1... | collective-permute-start | bytes 786440 | tf_op jit(solution)/shard_map/ppermute | solution.py:294
  38.0 22.0 %collective-permute-start.4 = (f32[256,256]{1,0:T(8,128)S(1)}, f32[256,256]{1,0:T(8,128)S(1)}, u32[]{:S(2)}, u32[]{:S(2)}) collective-permute-start(f32[256,256]{1,0:T(8,128)S(1)} %get-tuple-element.86), channel_id=1, source_target_pairs={{0,6},{1,7},{2,4},{3,5},{4,10},{5,11},{6,8},{7,9},{8,14},{9,15},{1... | collective-permute-start | bytes 786440 | tf_op jit(solution)/shard_map/ppermute | solution.py:294
  42.2 22.1 %collective-permute-start.11 = (f32[256,256]{1,0:T(8,128)S(1)}, f32[256,256]{1,0:T(8,128)S(1)}, u32[]{:S(2)}, u32[]{:S(2)}) collective-permute-start(f32[256,256]{1,0:T(8,128)S(1)} %get-tuple-element.98), channel_id=1, source_target_pairs={{0,4},{1,5},{2,6},{3,7},{4,8},{5,9},{6,10},{7,11},{8,12},{9,13},{1... | collective-permute-start | bytes 786440 | tf_op jit(solution)/shard_map/ppermute | solution.py:294
  53.5 17.8 %collective-permute-start.10 = (f32[256,256]{1,0:T(8,128)S(1)}, f32[256,256]{1,0:T(8,128)S(1)}, u32[]{:S(2)}, u32[]{:S(2)}) collective-permute-start(f32[256,256]{1,0:T(8,128)S(1)} %get-tuple-element.97), channel_id=1, source_target_pairs={{0,5},{1,4},{2,7},{3,6},{4,9},{5,8},{6,11},{7,10},{8,13},{9,12},{1... | collective-permute-start | bytes 786440 | tf_op jit(solution)/shard_map/ppermute | solution.py:294
  57.7 17.9 %collective-permute-start.9 = (f32[256,256]{1,0:T(8,128)S(1)}, f32[256,256]{1,0:T(8,128)S(1)}, u32[]{:S(2)}, u32[]{:S(2)}) collective-permute-start(f32[256,256]{1,0:T(8,128)S(1)} %get-tuple-element.96), channel_id=1, source_target_pairs={{0,4},{1,5},{2,6},{3,7},{4,8},{5,9},{6,10},{7,11},{8,12},{9,13},{1... | collective-permute-start | bytes 786440 | tf_op jit(solution)/shard_map/ppermute | solution.py:294
  61.0 21.5 %collective-permute-start.8 = (f32[256,256]{1,0:T(8,128)S(1)}, f32[256,256]{1,0:T(8,128)S(1)}, u32[]{:S(2)}, u32[]{:S(2)}) collective-permute-start(f32[256,256]{1,0:T(8,128)S(1)} %get-tuple-element.95), channel_id=1, source_target_pairs={{0,5},{1,4},{2,7},{3,6},{4,9},{5,8},{6,11},{7,10},{8,13},{9,12},{1... | collective-permute-start | bytes 786440 | tf_op jit(solution)/shard_map/ppermute | solution.py:294
  65.4 21.4 %collective-permute-start.15 = (f32[256,256]{1,0:T(8,128)S(1)}, f32[256,256]{1,0:T(8,128)S(1)}, u32[]{:S(2)}, u32[]{:S(2)}) collective-permute-start(f32[256,256]{1,0:T(8,128)S(1)} %get-tuple-element.107), channel_id=1, source_target_pairs={{0,4},{1,5},{2,6},{3,7},{4,8},{5,9},{6,10},{7,11},{8,12},{9,13},{1... | collective-permute-start | bytes 786440 | tf_op jit(solution)/shard_map/ppermute | solution.py:294
  76.6 15.8 %collective-permute-start.14 = (f32[256,256]{1,0:T(8,128)S(1)}, f32[256,256]{1,0:T(8,128)S(1)}, u32[]{:S(2)}, u32[]{:S(2)}) collective-permute-start(f32[256,256]{1,0:T(8,128)S(1)} %get-tuple-element.106), channel_id=1, source_target_pairs={{0,4},{1,5},{2,6},{3,7},{4,8},{5,9},{6,10},{7,11},{8,12},{9,13},{1... | collective-permute-start | bytes 786440 | tf_op jit(solution)/shard_map/ppermute | solution.py:294
  76.7 21.7 %collective-permute-start.13 = (f32[256,256]{1,0:T(8,128)S(1)}, f32[256,256]{1,0:T(8,128)S(1)}, u32[]{:S(2)}, u32[]{:S(2)}) collective-permute-start(f32[256,256]{1,0:T(8,128)S(1)} %get-tuple-element.105), channel_id=1, source_target_pairs={{0,6},{1,7},{2,4},{3,5},{4,10},{5,11},{6,8},{7,9},{8,14},{9,15},{1... | collective-permute-start | bytes 786440 | tf_op jit(solution)/shard_map/ppermute | solution.py:294
  83.6 22.3 %collective-permute-start.12 = (f32[256,256]{1,0:T(8,128)S(1)}, f32[256,256]{1,0:T(8,128)S(1)}, u32[]{:S(2)}, u32[]{:S(2)}) collective-permute-start(f32[256,256]{1,0:T(8,128)S(1)} %get-tuple-element.104), channel_id=1, source_target_pairs={{0,6},{1,7},{2,4},{3,5},{4,10},{5,11},{6,8},{7,9},{8,14},{9,15},{1... | collective-permute-start | bytes 786440 | tf_op jit(solution)/shard_map/ppermute | solution.py:294
  87.8 21.5 %collective-permute-start.19 = (f32[256,256]{1,0:T(8,128)S(1)}, f32[256,256]{1,0:T(8,128)S(1)}, u32[]{:S(2)}, u32[]{:S(2)}) collective-permute-start(f32[256,256]{1,0:T(8,128)S(1)} %get-tuple-element.116), channel_id=1, source_target_pairs={{0,4},{1,5},{2,6},{3,7},{4,8},{5,9},{6,10},{7,11},{8,12},{9,13},{1... | collective-permute-start | bytes 786440 | tf_op jit(solution)/shard_map/ppermute | solution.py:294
  99.4 17.0 %collective-permute-start.18 = (f32[256,256]{1,0:T(8,128)S(1)}, f32[256,256]{1,0:T(8,128)S(1)}, u32[]{:S(2)}, u32[]{:S(2)}) collective-permute-start(f32[256,256]{1,0:T(8,128)S(1)} %get-tuple-element.115), channel_id=1, source_target_pairs={{0,5},{1,4},{2,7},{3,6},{4,9},{5,8},{6,11},{7,10},{8,13},{9,12},{1... | collective-permute-start | bytes 786440 | tf_op jit(solution)/shard_map/ppermute | solution.py:294
  102.9 17.7 %collective-permute-start.17 = (f32[256,256]{1,0:T(8,128)S(1)}, f32[256,256]{1,0:T(8,128)S(1)}, u32[]{:S(2)}, u32[]{:S(2)}) collective-permute-start(f32[256,256]{1,0:T(8,128)S(1)} %get-tuple-element.114), channel_id=1, source_target_pairs={{0,4},{1,5},{2,6},{3,7},{4,8},{5,9},{6,10},{7,11},{8,12},{9,13},{1... | collective-permute-start | bytes 786440 | tf_op jit(solution)/shard_map/ppermute | solution.py:294
  107.0 19.8 %collective-permute-start.16 = (f32[256,256]{1,0:T(8,128)S(1)}, f32[256,256]{1,0:T(8,128)S(1)}, u32[]{:S(2)}, u32[]{:S(2)}) collective-permute-start(f32[256,256]{1,0:T(8,128)S(1)} %get-tuple-element.113), channel_id=1, source_target_pairs={{0,5},{1,4},{2,7},{3,6},{4,9},{5,8},{6,11},{7,10},{8,13},{9,12},{1... | collective-permute-start | bytes 786440 | tf_op jit(solution)/shard_map/ppermute | solution.py:294
